TPU v7x, 256 devices: a whole 4x4x8 slice. The times are simulated.
256 devices in a mesh: window: 32 (over z, x_lo, core), token: 8 (over x_hi, y).
Axes of the slice: x: 4 (x_hi: 2, x_lo: 2; x = x_hi * 2 + x_lo), y: 4, z: 8, core: 2. Of those that a mesh axis runs over, the one named last changes fastest.
Arguments:
- latents: bfloat16 [32, 9, 128, 5120], P('window', None, 'token'), may hold values from -36 to 36
- queries: bfloat16 [32, 9, 128, 5120], P('window', None, 'token'), may hold values from -128 to 128
- attn_keys: bfloat16 [32, 9, 128, 5120], P('window', None, 'token'), may hold values from -4.5 to 4.5
- cached: bfloat16 [4, 32, 9, 128, 5120], P(None, 'window', None, 'token'), may hold values from -3 to 3
- plan: int32 [4], replicated, may hold values from 0 to 1
- refresh: int32 [32], replicated, may hold values from 0 to 3
- value_gain: float32 [5120], replicated, may hold values from 0.1 to 1.9
- attn_gate: float32 [5120], replicated, may hold values from 0.5 to 3
- intersections: int32 [32], replicated, may hold values from 1 to 4, as said below
Outputs:
- looped: bfloat16 [32, 9, 128, 5120], P('window', None, 'token')
Inputs may be any that keep to these rules, and one draw needn't show every extreme that they name: `intersections`: some window has exactly 4.
All inputs are finite; a program needn't handle non-finite values.
Results may differ from a plain program's by a relative error of at most 0.0065.
Values may be sent and summed in bfloat16 or wider, within the bound.
No kernel may reach another device: no remote copies, remote signals or barrier semaphores. Data moves between devices by JAX's collectives and lax.ppermute only.
A program may use at most 128 MiB of HBM per device.

v0:
```python
import math

import jax
import jax.numpy as jnp
from jax import lax
from jax.experimental import pallas as pl
from jax.experimental.pallas import tpu as pltpu
from jax.sharding import PartitionSpec as P

HEAD_DIM = 128
MAXOV = 4
XS, YS = 2, 4
MOVES = (0, 1, 3, 2)
ANY = pl.BlockSpec(memory_space=pl.ANY)
SMEM = pl.BlockSpec(memory_space=pltpu.SMEM)
VMEM_BYTES = 56 * 2**20
PARTS = (6, 4)


def send(value, move):
    pairs = [(x * YS + y, x * YS + (y + move) % YS) for x in range(XS) for y in range(YS)]
    return lax.ppermute(value, "token", pairs)


def send_back(value, move):
    return send(value, YS - move)


def across(value):
    half = XS // 2
    pairs = [(x * YS + y, (x + half) % XS * YS + y) for x in range(XS) for y in range(YS)]
    return lax.ppermute(value, "token", pairs)


def owner(move):
    return lax.rem(lax.axis_index("token") + move, YS)


def lanes(start, size):
    return pl.ds(pl.multiple_of(start, HEAD_DIM), size)


def whole(refs, sems):
    copies = [pltpu.make_async_copy(a, b, sems.at[i]) for i, (a, b) in enumerate(refs)]
    for copy in copies:
        copy.start()
    return copies


def pack(value, wide, after=()):
    rows = value.shape[0]
    count = len(MOVES)

    def body(value_ref, *refs):
        refs = refs[len(after) :]
        outs, (held, in_sems, out_sems) = refs[:count], refs[count:]
        arriving = whole(
            [
                (value_ref.at[:, lanes(owner(move) * wide, wide)], held.at[i])
                for i, move in enumerate(MOVES)
            ],
            in_sems,
        )
        leaving = [
            pltpu.make_async_copy(held.at[i], outs[i], out_sems.at[i]) for i in range(count)
        ]
        for i in range(count):
            arriving[i].wait()
            leaving[i].start()
        for copy in leaving:
            copy.wait()

    return pl.pallas_call(
        body,
        name="pack",
        out_shape=[jax.ShapeDtypeStruct((rows, wide), value.dtype)] * count,
        in_specs=[ANY] * (1 + len(after)),
        out_specs=[ANY] * count,
        scratch_shapes=[
            pltpu.VMEM((count, rows, wide), value.dtype),
            pltpu.SemaphoreType.DMA((count,)),
            pltpu.SemaphoreType.DMA((count,)),
        ],
        compiler_params=pltpu.CompilerParams(vmem_limit_bytes=4 * 2**20),
        cost_estimate=pl.CostEstimate(flops=0, bytes_accessed=4 * value.size, transcendentals=0),
    )(value, *after)


def stack(pieces, skip, take, after=()):
    rows = pieces[0].shape[0]
    count = len(pieces)

    def body(*refs):
        sources = refs[:count]
        out, held, in_sems, out_sem = refs[count + len(after) :]
        arriving = whole(
            [
                (source.at[:, pl.ds(skip, take)], held.at[pl.ds(i * rows, rows)])
                for i, source in enumerate(sources)
            ],
            in_sems,
        )
        for copy in arriving:
            copy.wait()
        leaving = pltpu.make_async_copy(held, out, out_sem)
        leaving.start()
        leaving.wait()

    return pl.pallas_call(
        body,
        name="stack",
        out_shape=jax.ShapeDtypeStruct((count * rows, take), pieces[0].dtype),
        in_specs=[ANY] * (count + len(after)),
        out_specs=ANY,
        scratch_shapes=[
            pltpu.VMEM((count * rows, take), pieces[0].dtype),
            pltpu.SemaphoreType.DMA((count,)),
            pltpu.SemaphoreType.DMA,
        ],
        compiler_params=pltpu.CompilerParams(vmem_limit_bytes=4 * 2**20),
        cost_estimate=pl.CostEstimate(
            flops=0, bytes_accessed=4 * count * rows * take, transcendentals=0
        ),
    )(*pieces, *after)


def hide(latents, cached, plan, refresh, gain, wide, parts, after):
    blocks = cached.shape[0]
    frames, spots, width = latents.shape
    count = len(MOVES)
    step = 3
    rows = step * spots

    def body(plan_ref, refresh_ref, latents_ref, cached_ref, gain_ref, *refs):
        values_ref, *laters, later_ref = refs[1:]
        chosen = refresh_ref[lax.axis_index("window")]
        for i in range(step):
            span = pl.ds(i * spots, spots)
            hidden = latents_ref[i].astype(jnp.float32)
            after = jnp.zeros_like(hidden)
            for b in range(blocks):
                mix = plan_ref[b].astype(jnp.float32)
                block = cached_ref[b, i].astype(jnp.float32)
                hidden = hidden + jnp.where(b < chosen, mix, 0.0) * block
                after = after + jnp.where(b > chosen, mix, 0.0) * block
            later_ref[span, :] = hidden + after
            mean_square = jnp.mean(hidden * hidden, axis=-1, keepdims=True)
            values = hidden * lax.rsqrt(mean_square + 1e-06) * gain_ref[...]
            values_ref[span, :] = values.astype(values_ref.dtype)
        for i, move in enumerate(MOVES):
            start = owner(move) * wide
            skip = 0
            for take, later in zip(parts, laters):
                later[:, pl.ds(i * take, take)] = later_ref[:, lanes(start + skip, take)]
                skip += take

    return pl.pallas_call(
        body,
        name="hide",
        grid=(frames // step,),
        out_shape=[jax.ShapeDtypeStruct((frames * spots, width), jnp.bfloat16)]
        + [jax.ShapeDtypeStruct((frames * spots, count * take), jnp.float32) for take in parts],
        in_specs=[
            SMEM,
            SMEM,
            pl.BlockSpec((step, spots, width), lambda f: (f, 0, 0)),
            pl.BlockSpec((blocks, step, spots, width), lambda f: (0, f, 0, 0)),
            pl.BlockSpec((1, width), lambda f: (0, 0)),
            ANY,
        ],
        out_specs=[pl.BlockSpec((rows, width), lambda f: (f, 0))]
        + [pl.BlockSpec((rows, count * take), lambda f: (f, 0)) for take in parts],
        scratch_shapes=[pltpu.VMEM((rows, width), jnp.float32)],
        compiler_params=pltpu.CompilerParams(vmem_limit_bytes=VMEM_BYTES),
        cost_estimate=pl.CostEstimate(
            flops=20 * latents.size, bytes_accessed=16 * latents.size, transcendentals=0
        ),
    )(plan, refresh, latents, cached, gain, after)


def attend(asked, keys, values, skip, take):
    rows = asked[0].shape[0]
    count, places = len(asked), len(keys)
    pieces = [(piece, 0, skip) for piece in asked] + keys + values
    arrays = list({id(piece[0]): piece[0] for piece in pieces}.values())
    index = {id(array): i for i, array in enumerate(arrays)}
    where = [(index[id(array)], row, col) for array, row, col in pieces]
    block = count * rows // 2
    scale = math.log2(math.e) / math.sqrt(HEAD_DIM)

    def body(*refs):
        sources, outs = refs[: len(arrays)], refs[len(arrays) : len(arrays) + count]
        q_ref, k_ref, v_ref, result, in_sems, out_sems = refs[len(arrays) + count :]
        holds = (
            [q_ref.at[pl.ds(i * rows, rows)] for i in range(count)]
            + [k_ref.at[pl.ds(i * rows, rows)] for i in range(places)]
            + [v_ref.at[pl.ds(i * rows, rows)] for i in range(places)]
        )
        arriving = whole(
            [
                (sources[i].at[pl.ds(row, rows), pl.ds(col, take)], held)
                for (i, row, col), held in zip(where, holds)
            ],
            in_sems,
        )
        for copy in arriving:
            copy.wait()

        @pl.loop(0, take // HEAD_DIM)
        def _(head):
            cols = lanes(head * HEAD_DIM, HEAD_DIM)
            for i in range(count * rows // block):
                span = pl.ds(i * block, block)
                scores = lax.dot_general(
                    q_ref[span, cols],
                    k_ref[:, cols],
                    (((1,), (1,)), ((), ())),
                    preferred_element_type=jnp.float32,
                )
                peak = jnp.max(scores, axis=1, keepdims=True)
                weights = jnp.exp2((scores - peak) * scale).astype(jnp.bfloat16)
                value = v_ref[:, cols]
                both = jnp.concatenate([value, jnp.ones_like(value)], axis=1)
                total = jnp.dot(weights, both, preferred_element_type=jnp.float32)
                result[span, cols] = (total[:, :HEAD_DIM] / total[:, HEAD_DIM:]).astype(
                    result.dtype
                )

        leaving = whole(
            [(result.at[pl.ds(i * rows, rows)], out) for i, out in enumerate(outs)], out_sems
        )
        for copy in leaving:
            copy.wait()

    work = count * rows * places * rows * take
    return pl.pallas_call(
        body,
        name="attend",
        out_shape=[jax.ShapeDtypeStruct((rows, take), jnp.bfloat16)] * count,
        in_specs=[ANY] * len(arrays),
        out_specs=[ANY] * count,
        scratch_shapes=[
            pltpu.VMEM((count * rows, take), jnp.bfloat16),
            pltpu.VMEM((places * rows, take), jnp.bfloat16),
            pltpu.VMEM((places * rows, take), jnp.bfloat16),
            pltpu.VMEM((count * rows, take), jnp.bfloat16),
            pltpu.SemaphoreType.DMA((len(pieces),)),
            pltpu.SemaphoreType.DMA((count,)),
        ],
        compiler_params=pltpu.CompilerParams(vmem_limit_bytes=24 * 2**20),
        cost_estimate=pl.CostEstimate(
            flops=8 * work,
            bytes_accessed=12 * places * rows * take,
            transcendentals=work // HEAD_DIM,
        ),
    )(*arrays)


def join(later, gate, attended, frames, wide, skip):
    count = len(MOVES)
    rows, take = attended[0].shape
    spots = rows // frames
    ends = MAXOV * spots
    sizes = (ends, rows - 2 * ends, ends)

    def body(later_ref, gate_ref, *refs):
        pieces, outs = refs[:count], refs[count : count + 3]
        laters, held, result, in_sems, out_sems = refs[count + 3 :]
        arriving = []
        for i in range(count):
            span = pl.ds(i * take, take)
            arriving.append(
                pltpu.make_async_copy(later_ref.at[:, span], laters.at[:, span], in_sems.at[i, 0])
            )
            arriving.append(
                pltpu.make_async_copy(pieces[i], held.at[:, span], in_sems.at[i, 1])
            )
        for copy in arriving:
            copy.start()
        for i, move in enumerate(MOVES):
            span = pl.ds(i * take, take)
            gates = gate_ref[:, lanes(owner(move) * wide + skip, take)]
            arriving[2 * i].wait()
            arriving[2 * i + 1].wait()
            pre = laters[:, span] + gates * held[:, span].astype(jnp.float32)
            result[:, span] = pre.astype(result.dtype)
        leaving, start = [], 0
        for i, size in enumerate(sizes):
            leaving.append(
                pltpu.make_async_copy(result.at[pl.ds(start, size)], outs[i], out_sems.at[i])
            )
            start += size
        for copy in leaving:
            copy.start()
        for copy in leaving:
            copy.wait()

    return pl.pallas_call(
        body,
        name="join",
        out_shape=[jax.ShapeDtypeStruct((size, count * take), jnp.bfloat16) for size in sizes],
        in_specs=[ANY, pl.BlockSpec(memory_space=pltpu.VMEM)] + [ANY] * count,
        out_specs=[ANY] * 3,
        scratch_shapes=[
            pltpu.VMEM((rows, count * take), jnp.float32),
            pltpu.VMEM((rows, count * take), jnp.bfloat16),
            pltpu.VMEM((rows, count * take), jnp.bfloat16),
            pltpu.SemaphoreType.DMA((count, 2)),
            pltpu.SemaphoreType.DMA((3,)),
        ],
        compiler_params=pltpu.CompilerParams(vmem_limit_bytes=8 * 2**20),
        cost_estimate=pl.CostEstimate(
            flops=2 * later.size, bytes_accessed=8 * later.size, transcendentals=0
        ),
    )(later, gate, *attended)


def blend(intersections, first, middle, last, from_prev, from_next, frames, wide, skip, before):
    count = len(MOVES)
    take = first.shape[1] // count
    ends = first.shape[0]
    spots = ends // MAXOV
    rows = frames * spots

    def body(overlaps_ref, *refs):
        sources = refs[:5]
        out_ref, result, mine, prev, after, in_sems, out_sems = refs[-7:]
        window, windows = lax.axis_index("window"), lax.axis_size("window")
        ov_next = overlaps_ref[window]
        ov_prev = overlaps_ref[lax.rem(window + windows - 1, windows)]
        first_in, last_in = mine.at[pl.ds(0, ends)], mine.at[pl.ds(ends, ends)]
        middle_in = result.at[pl.ds(ends, rows - 2 * ends)]
        arriving = whole(
            zip(sources, (first_in, middle_in, last_in, prev, after)), in_sems
        )
        for copy in arriving:
            copy.wait()
        for f in range(MAXOV):
            ramp = jnp.where(
                f < ov_prev, jnp.float32(f + 1) / (ov_prev + 1).astype(jnp.float32), 1.0
            )
            other = jnp.clip(MAXOV - ov_prev + f, 0, MAXOV - 1) * spots
            mixed = (1.0 - ramp) * prev[pl.ds(pl.multiple_of(other, 16), spots), :].astype(
                jnp.float32
            ) + ramp * mine[pl.ds(f * spots, spots), :].astype(jnp.float32)
            result[pl.ds(f * spots, spots), :] = mixed.astype(result.dtype)
        for f in range(frames - MAXOV, frames):
            tail = f - frames + ov_next
            ramp = jnp.where(
                tail >= 0,
                (tail + 1).astype(jnp.float32) / (ov_next + 1).astype(jnp.float32),
                0.0,
            )
            other = jnp.clip(tail, 0, MAXOV - 1) * spots
            own = pl.ds(ends + (f - frames + MAXOV) * spots, spots)
            mixed = (1.0 - ramp) * mine[own, :].astype(jnp.float32) + ramp * after[
                pl.ds(pl.multiple_of(other, 16), spots), :
            ].astype(jnp.float32)
            result[pl.ds(f * spots, spots), :] = mixed.astype(result.dtype)
        leaving = whole(
            [
                (
                    result.at[:, pl.ds(i * take, take)],
                    out_ref.at[:, lanes(owner(move) * wide + skip, take)],
                )
                for i, move in enumerate(MOVES)
            ],
            out_sems,
        )
        for copy in leaving:
            copy.wait()

    extra = () if before is None else (before,)
    return pl.pallas_call(
        body,
        name="blend",
        out_shape=jax.ShapeDtypeStruct((rows, count * wide), jnp.bfloat16),
        in_specs=[SMEM] + [ANY] * (5 + len(extra)),
        out_specs=ANY,
        input_output_aliases={6: 0} if extra else {},
        scratch_shapes=[
            pltpu.VMEM((rows, count * take), jnp.bfloat16),
            pltpu.VMEM((2 * ends, count * take), jnp.bfloat16),
            pltpu.VMEM((ends, count * take), jnp.bfloat16),
            pltpu.VMEM((ends, count * take), jnp.bfloat16),
            pltpu.SemaphoreType.DMA((5,)),
            pltpu.SemaphoreType.DMA((count,)),
        ],
        compiler_params=pltpu.CompilerParams(vmem_limit_bytes=6 * 2**20),
        cost_estimate=pl.CostEstimate(
            flops=4 * rows * count * take,
            bytes_accessed=8 * rows * count * take,
            transcendentals=0,
        ),
    )(intersections, first, middle, last, from_prev, from_next, *extra)


def shift(value, steps):
    count = lax.axis_size("window")
    pairs = [(source, (source + steps) % count) for source in range(count)]
    return lax.ppermute(value, "window", pairs)


def spread(pieces, how):
    return [how(piece, move) if move else piece for piece, move in zip(pieces, MOVES)]


def on_device(
    latents, queries, attn_keys, cached, plan, refresh, value_gain, attn_gate, intersections
):
    _, frames, spots, width = latents.shape
    rows = frames * spots
    wide = width // len(MOVES)
    parts = [heads * HEAD_DIM for heads in PARTS]
    skips = [sum(parts[:i]) for i in range(len(parts))]
    queries = queries.reshape(rows, width)
    gate = attn_gate.reshape(1, width)
    packed = pack(attn_keys.reshape(rows, width), wide)
    keys = spread(packed, send)
    values, *laters = hide(
        latents[0],
        cached[:, 0],
        plan,
        refresh,
        value_gain.reshape(1, width),
        wide,
        parts,
        packed[0],
    )
    far_keys = [across(key) for key in keys[:3]]
    values = spread(pack(values, wide, (*keys[1:3], far_keys[0])), send)
    far_value = across(values[0])
    asked = spread(pack(queries, wide, (*values[1:3], far_keys[1])), send)
    moved = [keys[3], *values[1:]]
    afters = ((far_keys[1], far_value), (far_keys[2],))
    rests = [
        across(stack(moved, skip, take, after))
        for skip, take, after in zip(skips, parts, afters)
    ]
    out = None
    for later, rest, skip, take in zip(laters, rests, skips, parts):
        key_places = [(key, 0, skip) for key in keys + far_keys] + [(rest, 0, 0)]
        value_places = [(value, 0, skip) for value in [*values, far_value]] + [
            (rest, i * rows, 0) for i in (1, 2, 3)
        ]
        attended = spread(attend(asked, key_places, value_places, skip, take), send_back)
        first, middle, last = join(later, gate, attended, frames, wide, skip)
        from_prev = shift(last, 1)
        from_next = shift(first, -1)
        out = blend(
            intersections, first, middle, last, from_prev, from_next, frames, wide, skip, out
        )
    return out.reshape(1, frames, spots, width)


def solution(mesh):
    in_specs = (
        P("window", None, "token", None),
        P("window", None, "token", None),
        P("window", None, "token", None),
        P(None, "window", None, "token", None),
        P(),
        P(),
        P(),
        P(),
        P(),
    )
    out_specs = P("window", None, "token", None)
    return jax.shard_map(
        on_device, mesh=mesh, in_specs=in_specs, out_specs=out_specs, check_vma=False
    )
```

profile of v0, /device:TPU:1, one launch (start us, length us, event | category | flops | bytes accessed | tf_op | source)
XLA Modules:
  0.0 123.1 jit_solution(13196453327273705851)
XLA Ops:
  0.0 1.4 %copy-done.3 = bf16[1,9,16,5120]{3,2,1,0:T(8,128)(2,1)S(1)} copy-done((bf16[1,9,16,5120]{3,2,1,0:T(8,128)(2,1)S(1)}, bf16[1,9,16,5120]{3,2,1,0:T(8,128)(2,1)}, u32[]{:S(2)}) %copy-start.3) | copy-done | bytes 1474584
  1.4 0.8 pack.3
  2.2 2.2 %collective-permute-start = (bf16[144,1280]{1,0:T(8,128)(2,1)S(1)}, bf16[144,1280]{1,0:T(8,128)(2,1)S(1)}, u32[]{:S(2)}, u32[]{:S(2)}) collective-permute-start(bf16[144,1280]{1,0:T(8,128)(2,1)S(1)} %get-tuple-element.37), channel_id=1, source_target_pairs={{0,1},{1,2},{2,3},{3,0},{4,5},{5,6},{6,7},{7,4},{8,9},{9,10},{10,1... | collective-permute-start | bytes 1105928 | tf_op jit(solution)/shard_map/ppermute | solution.py:22
  4.4 1.5 %collective-permute-start.1 = (bf16[144,1280]{1,0:T(8,128)(2,1)S(1)}, bf16[144,1280]{1,0:T(8,128)(2,1)S(1)}, u32[]{:S(2)}, u32[]{:S(2)}) collective-permute-start(bf16[144,1280]{1,0:T(8,128)(2,1)S(1)} %get-tuple-element.38), channel_id=1, source_target_pairs={{0,3},{1,0},{2,1},{3,2},{4,7},{5,4},{6,5},{7,6},{8,11},{9,8},{10,9... | collective-permute-start | bytes 1105928 | tf_op jit(solution)/shard_map/ppermute | solution.py:22
  5.9 2.7 %collective-permute-start.2 = (bf16[144,1280]{1,0:T(8,128)(2,1)S(1)}, bf16[144,1280]{1,0:T(8,128)(2,1)S(1)}, u32[]{:S(2)}, u32[]{:S(2)}) collective-permute-start(bf16[144,1280]{1,0:T(8,128)(2,1)S(1)} %get-tuple-element.34.refs_0_.refs_4_), channel_id=1, source_target_pairs={{0,4},{1,5},{2,6},{3,7},{4,0},{5,1},{6,2},{7,3},{8,12},{9,13},{10,... | collective-permute-start | bytes 1105928 | tf_op jit(solution)/shard_map/ppermute | solution.py:32
  8.7 1.6 %collective-permute-start.9 = (bf16[144,1280]{1,0:T(8,128)(2,1)S(1)}, bf16[144,1280]{1,0:T(8,128)(2,1)S(1)}, u32[]{:S(2)}, u32[]{:S(2)}) collective-permute-start(bf16[144,1280]{1,0:T(8,128)(2,1)S(1)} %get-tuple-element.45), channel_id=1, source_target_pairs={{0,2},{1,3},{2,0},{3,1},{4,6},{5,7},{6,4},{7,5},{8,10},{9,11},{10,... | collective-permute-start | bytes 1105928 | tf_op jit(solution)/shard_map/ppermute | solution.py:22
  10.3 7.3 %hide.1 = (bf16[144,5120]{1,0:T(8,128)(2,1)}, f32[144,3072]{1,0:T(8,128)}, f32[144,2048]{1,0:T(8,128)}) custom-call(s32[4]{0:T(128)} %plan_ref.1, s32[32]{0:T(128)} %refresh_ref.1, bf16[9,16,5120]{2,1,0:T(8,128)(2,1)} %bitcast.12, bf16[4,9,16,5120]{3,2,1,0:T(8,128)(2,1)} %bitcast.11, f32[1,5120]{1,0:T(1,128)} %bitcast.13, bf16[144,1280]{1,0:T(8,128)(2,1)} %copy-done.5), custom_call_target="tpu_custom_call" | custom-call | flops 14745600 | bytes 11796480 | tf_op jit(solution)/shard_map/hide/pallas_call | solution.py:157
  17.5 0.0 collective-permute-done.refs_0_.refs_5_
  17.5 0.0 collective-permute-done.1.refs_1_.refs_6_
  17.5 0.0 collective-permute-done.2.refs_2_.refs_8_
  17.5 0.0 copy-start.2
  17.5 1.4 %copy-done.2 = bf16[144,5120]{1,0:T(8,128)(2,1)S(1)} copy-done((bf16[144,5120]{1,0:T(8,128)(2,1)S(1)}, bf16[144,5120]{1,0:T(8,128)(2,1)}, u32[]{:S(2)}) %copy-start.2) | copy-done | bytes 1474584
  18.9 0.8 pack.4
  19.7 0.5 collective-permute-start.3
  20.2 2.3 %collective-permute-start.4 = (bf16[144,1280]{1,0:T(8,128)(2,1)S(1)}, bf16[144,1280]{1,0:T(8,128)(2,1)S(1)}, u32[]{:S(2)}, u32[]{:S(2)}) collective-permute-start(bf16[144,1280]{1,0:T(8,128)(2,1)S(1)} %get-tuple-element.40), channel_id=1, source_target_pairs={{0,3},{1,0},{2,1},{3,2},{4,7},{5,4},{6,5},{7,6},{8,11},{9,8},{10,9... | collective-permute-start | bytes 1105928 | tf_op jit(solution)/shard_map/ppermute | solution.py:22
  22.5 0.2 collective-permute-start.11
  22.7 1.6 %collective-permute-start.5 = (bf16[144,1280]{1,0:T(8,128)(2,1)S(1)}, bf16[144,1280]{1,0:T(8,128)(2,1)S(1)}, u32[]{:S(2)}, u32[]{:S(2)}) collective-permute-start(bf16[144,1280]{1,0:T(8,128)(2,1)S(1)} %collective-permute-done.refs_0_.refs_5_), channel_id=1, source_target_pairs={{0,4},{1,5},{2,6},{3,7},{4,0},{5,1},{6,2},{7,3},{8,12},{9,13},{10,... | collective-permute-start | bytes 1105928 | tf_op jit(solution)/shard_map/ppermute | solution.py:32
  24.3 0.0 collective-permute-done.9.refs_0_.refs_7_
  24.4 1.3 %collective-permute-start.13 = (bf16[144,1280]{1,0:T(8,128)(2,1)S(1)}, bf16[144,1280]{1,0:T(8,128)(2,1)S(1)}, u32[]{:S(2)}, u32[]{:S(2)}) collective-permute-start(bf16[144,1280]{1,0:T(8,128)(2,1)S(1)} %get-tuple-element.47.refs_12_), channel_id=1, source_target_pairs={{0,4},{1,5},{2,6},{3,7},{4,0},{5,1},{6,2},{7,3},{8,12},{9,13},{10,... | collective-permute-start | bytes 1105928 | tf_op jit(solution)/shard_map/ppermute | solution.py:32
  25.7 6.5 %collective-permute-done.3.refs_0_.refs_1_.refs_13_ = bf16[144,1280]{1,0:T(8,128)(2,1)S(1)} collective-permute-done((bf16[144,1280]{1,0:T(8,128)(2,1)S(1)}, bf16[144,1280]{1,0:T(8,128)(2,1)S(1)}, u32[]{:S(2)}, u32[]{:S(2)}) %collective-permute-start.3) | collective-permute-done | bytes 368672 | tf_op jit(solution)/shard_map/ppermute | solution.py:22
  32.2 0.0 collective-permute-done.4.refs_1_.refs_2_.refs_14_
  32.2 0.0 collective-permute-done.5.refs_2_.refs_9_.refs_4_
  32.2 0.2 collective-permute-done.11.refs_3_.refs_15_
  32.5 2.1 %collective-permute-done.13.refs_16_.refs_5_ = bf16[144,1280]{1,0:T(8,128)(2,1)S(1)} collective-permute-done((bf16[144,1280]{1,0:T(8,128)(2,1)S(1)}, bf16[144,1280]{1,0:T(8,128)(2,1)S(1)}, u32[]{:S(2)}, u32[]{:S(2)}) %collective-permute-start.13) | collective-permute-done | bytes 368672 | tf_op jit(solution)/shard_map/ppermute | solution.py:32
  34.5 0.3 stack.3
  34.8 2.0 %collective-permute-start.19 = (bf16[576,768]{1,0:T(8,128)(2,1)S(1)}, bf16[576,768]{1,0:T(8,128)(2,1)S(1)}, u32[]{:S(2)}, u32[]{:S(2)}) collective-permute-start(bf16[576,768]{1,0:T(8,128)(2,1)S(1)} %stack.3), channel_id=1, source_target_pairs={{0,4},{1,5},{2,6},{3,7},{4,0},{5,1},{6,2},{7,3},{8,12},{9,13},{10,... | collective-permute-start | bytes 2654216 | tf_op jit(solution)/shard_map/ppermute | solution.py:32
  36.8 1.0 collective-permute-start.10
  37.9 0.8 pack.5
  38.7 0.5 collective-permute-start.6
  39.2 2.4 %collective-permute-start.7 = (bf16[144,1280]{1,0:T(8,128)(2,1)S(1)}, bf16[144,1280]{1,0:T(8,128)(2,1)S(1)}, u32[]{:S(2)}, u32[]{:S(2)}) collective-permute-start(bf16[144,1280]{1,0:T(8,128)(2,1)S(1)} %get-tuple-element.43), channel_id=1, source_target_pairs={{0,3},{1,0},{2,1},{3,2},{4,7},{5,4},{6,5},{7,6},{8,11},{9,8},{10,9... | collective-permute-start | bytes 1105928 | tf_op jit(solution)/shard_map/ppermute | solution.py:22
  41.6 2.6 %collective-permute-start.8 = (bf16[144,1280]{1,0:T(8,128)(2,1)S(1)}, bf16[144,1280]{1,0:T(8,128)(2,1)S(1)}, u32[]{:S(2)}, u32[]{:S(2)}) collective-permute-start(bf16[144,1280]{1,0:T(8,128)(2,1)S(1)} %get-tuple-element.44), channel_id=1, source_target_pairs={{0,2},{1,3},{2,0},{3,1},{4,6},{5,7},{6,4},{7,5},{8,10},{9,11},{10,... | collective-permute-start | bytes 1105928 | tf_op jit(solution)/shard_map/ppermute | solution.py:22
  44.2 16.3 %collective-permute-done.10.refs_4_.refs_10_ = bf16[144,1280]{1,0:T(8,128)(2,1)S(1)} collective-permute-done((bf16[144,1280]{1,0:T(8,128)(2,1)S(1)}, bf16[144,1280]{1,0:T(8,128)(2,1)S(1)}, u32[]{:S(2)}, u32[]{:S(2)}) %collective-permute-start.10) | collective-permute-done | bytes 368672 | tf_op jit(solution)/shard_map/ppermute | solution.py:32
  60.5 0.2 stack.2
  60.7 2.2 %collective-permute-start.12 = (bf16[576,512]{1,0:T(8,128)(2,1)S(1)}, bf16[576,512]{1,0:T(8,128)(2,1)S(1)}, u32[]{:S(2)}, u32[]{:S(2)}) collective-permute-start(bf16[576,512]{1,0:T(8,128)(2,1)S(1)} %stack.2), channel_id=1, source_target_pairs={{0,4},{1,5},{2,6},{3,7},{4,0},{5,1},{6,2},{7,3},{8,12},{9,13},{10,... | collective-permute-start | bytes 1769480 | tf_op jit(solution)/shard_map/ppermute | solution.py:32
  63.0 0.0 collective-permute-done.6.refs_1_
  63.0 0.0 collective-permute-done.7.refs_2_
  63.0 0.0 collective-permute-done.8.refs_3_
  63.0 0.0 collective-permute-done.19.refs_11_
  63.0 10.5 %attend.3 = (bf16[144,768]{1,0:T(8,128)(2,1)S(1)}, bf16[144,768]{1,0:T(8,128)(2,1)S(1)}, bf16[144,768]{1,0:T(8,128)(2,1)S(1)}, bf16[144,768]{1,0:T(8,128)(2,1)S(1)}) custom-call(bf16[144,1280]{1,0:T(8,128)(2,1)S(1)} %get-tuple-element.41.refs_0_, bf16[144,1280]{1,0:T(8,128)(2,1)S(1)} %collective-permute-done.6.refs_1_, ...), custom_call_target="tpu_custom_call" | custom-call | flops 4076863488 | bytes 10616832 | tf_op jit(solution)/shard_map/attend/pallas_call | solution.py:236
  73.5 2.6 %collective-permute-start.20 = (bf16[144,768]{1,0:T(8,128)(2,1)S(1)}, bf16[144,768]{1,0:T(8,128)(2,1)S(1)}, u32[]{:S(2)}, u32[]{:S(2)}) collective-permute-start(bf16[144,768]{1,0:T(8,128)(2,1)S(1)} %get-tuple-element.57), channel_id=1, source_target_pairs={{0,3},{1,0},{2,1},{3,2},{4,7},{5,4},{6,5},{7,6},{8,11},{9,8},{10,9... | collective-permute-start | bytes 663560 | tf_op jit(solution)/shard_map/ppermute | solution.py:22
  76.1 0.0 collective-permute-start.21
  76.1 2.5 %collective-permute-start.22 = (bf16[144,768]{1,0:T(8,128)(2,1)S(1)}, bf16[144,768]{1,0:T(8,128)(2,1)S(1)}, u32[]{:S(2)}, u32[]{:S(2)}) collective-permute-start(bf16[144,768]{1,0:T(8,128)(2,1)S(1)} %get-tuple-element.59), channel_id=1, source_target_pairs={{0,2},{1,3},{2,0},{3,1},{4,6},{5,7},{6,4},{7,5},{8,10},{9,11},{10,... | collective-permute-start | bytes 663560 | tf_op jit(solution)/shard_map/ppermute | solution.py:22
  78.7 0.0 collective-permute-done.12.refs_11_
  78.7 7.1 %attend.2 = (bf16[144,512]{1,0:T(8,128)(2,1)S(1)}, bf16[144,512]{1,0:T(8,128)(2,1)S(1)}, bf16[144,512]{1,0:T(8,128)(2,1)S(1)}, bf16[144,512]{1,0:T(8,128)(2,1)S(1)}) custom-call(bf16[144,1280]{1,0:T(8,128)(2,1)S(1)} %get-tuple-element.41.refs_0_, bf16[144,1280]{1,0:T(8,128)(2,1)S(1)} %collective-permute-done.6.refs_1_, ...), custom_call_target="tpu_custom_call" | custom-call | flops 2717908992 | bytes 7077888 | tf_op jit(solution)/shard_map/attend/pallas_call | solution.py:236
  85.8 0.8 collective-permute-start.14
  86.5 0.8 collective-permute-start.15
  87.3 0.0 collective-permute-done.20.refs_1_
  87.3 1.0 collective-permute-start.16
  88.3 0.0 collective-permute-done.21.refs_2_
  88.3 0.0 collective-permute-done.22.refs_3_
  88.3 1.1 join.3
  89.4 0.0 copy-start.8
  89.5 14.6 %collective-permute-start.23 = (bf16[64,3072]{1,0:T(8,128)(2,1)S(1)}, bf16[64,3072]{1,0:T(8,128)(2,1)S(1)}, u32[]{:S(2)}, u32[]{:S(2)}) collective-permute-start(bf16[64,3072]{1,0:T(8,128)(2,1)S(1)} %get-tuple-element.62.refs_2_), channel_id=1, source_target_pairs={{0,8},{8,16},{16,24},{24,32},{32,40},{40,48},{48,56},{56,64},{64,7... | collective-permute-start | bytes 1179656 | tf_op jit(solution)/shard_map/ppermute | solution.py:401
  104.0 0.0 collective-permute-start.24
  104.0 0.0 collective-permute-done.14.refs_1_
  104.0 0.0 collective-permute-done.15.refs_2_
  104.0 0.0 collective-permute-done.16.refs_3_
  104.1 0.5 join.2
  104.6 5.2 %collective-permute-start.17 = (bf16[64,2048]{1,0:T(8,128)(2,1)S(1)}, bf16[64,2048]{1,0:T(8,128)(2,1)S(1)}, u32[]{:S(2)}, u32[]{:S(2)}) collective-permute-start(bf16[64,2048]{1,0:T(8,128)(2,1)S(1)} %get-tuple-element.54.refs_2_), channel_id=1, source_target_pairs={{0,8},{8,16},{16,24},{24,32},{32,40},{40,48},{48,56},{56,64},{64,7... | collective-permute-start | bytes 786440 | tf_op jit(solution)/shard_map/ppermute | solution.py:401
  109.8 0.0 collective-permute-start.18
  109.8 8.4 %collective-permute-done.24.refs_4_ = bf16[64,3072]{1,0:T(8,128)(2,1)S(1)} collective-permute-done((bf16[64,3072]{1,0:T(8,128)(2,1)S(1)}, bf16[64,3072]{1,0:T(8,128)(2,1)S(1)}, u32[]{:S(2)}, u32[]{:S(2)}) %collective-permute-start.24) | collective-permute-done | bytes 393248 | tf_op jit(solution)/shard_map/ppermute | solution.py:401
  118.3 2.8 %blend.2.refs_5_ = bf16[144,5120]{1,0:T(8,128)(2,1)} custom-call(s32[32]{0:T(128)S(1)} %copy-done.8, bf16[64,3072]{1,0:T(8,128)(2,1)S(1)} %get-tuple-element.60.refs_0_, bf16[16,3072]{1,0:T(8,128)(2,1)S(1)} %get-tuple-element.61.refs_1_, bf16[64,3072]{1,0:T(8,128)(2,1)S(1)} %get-tuple-element.62.refs_2_, ...), custom_call_target="tpu_custom_call" | custom-call | flops 1769472 | bytes 3538944 | tf_op jit(solution)/shard_map/blend/pallas_call | solution.py:374
  121.1 0.0 collective-permute-done.17.refs_3_
  121.1 1.8 %blend.3 = bf16[144,5120]{1,0:T(8,128)(2,1)} custom-call(s32[32]{0:T(128)S(1)} %copy-done.8, bf16[64,2048]{1,0:T(8,128)(2,1)S(1)} %get-tuple-element.52.refs_0_, bf16[16,2048]{1,0:T(8,128)(2,1)S(1)} %get-tuple-element.53.refs_1_, bf16[64,2048]{1,0:T(8,128)(2,1)S(1)} %get-tuple-element.54.refs_2_, ...), custom_call_target="tpu_custom_call", output_to_operand_aliasing={{}: (6, {})} | custom-call | flops 1179648 | bytes 2359296 | tf_op jit(solution)/shard_map/blend/pallas_call | solution.py:374
  (16 shorter events, 0.0 us)
Async XLA Ops:
  0.0 1.4 %copy-start.3 = (bf16[1,9,16,5120]{3,2,1,0:T(8,128)(2,1)S(1)}, bf16[1,9,16,5120]{3,2,1,0:T(8,128)(2,1)}, u32[]{:S(2)}) copy-start(bf16[1,9,16,5120]{3,2,1,0:T(8,128)(2,1)} %param.11) | copy-start | bytes 4423684
  2.2 8.0 %copy-start.5 = (bf16[144,1280]{1,0:T(8,128)(2,1)}, bf16[144,1280]{1,0:T(8,128)(2,1)S(1)}, u32[]{:S(2)}) copy-start(bf16[144,1280]{1,0:T(8,128)(2,1)S(1)} %get-tuple-element.34.refs_0_.refs_4_) | copy-start | bytes 1105924
  2.2 15.3 %collective-permute-start = (bf16[144,1280]{1,0:T(8,128)(2,1)S(1)}, bf16[144,1280]{1,0:T(8,128)(2,1)S(1)}, u32[]{:S(2)}, u32[]{:S(2)}) collective-permute-start(bf16[144,1280]{1,0:T(8,128)(2,1)S(1)} %get-tuple-element.37), channel_id=1, source_target_pairs={{0,1},{1,2},{2,3},{3,0},{4,5},{5,6},{6,7},{7,4},{8,9},{9,10},{10,1... | collective-permute-start | bytes 1105928 | tf_op jit(solution)/shard_map/ppermute | solution.py:22
  4.4 13.1 %collective-permute-start.1 = (bf16[144,1280]{1,0:T(8,128)(2,1)S(1)}, bf16[144,1280]{1,0:T(8,128)(2,1)S(1)}, u32[]{:S(2)}, u32[]{:S(2)}) collective-permute-start(bf16[144,1280]{1,0:T(8,128)(2,1)S(1)} %get-tuple-element.38), channel_id=1, source_target_pairs={{0,3},{1,0},{2,1},{3,2},{4,7},{5,4},{6,5},{7,6},{8,11},{9,8},{10,9... | collective-permute-start | bytes 1105928 | tf_op jit(solution)/shard_map/ppermute | solution.py:22
  5.9 11.6 %collective-permute-start.2 = (bf16[144,1280]{1,0:T(8,128)(2,1)S(1)}, bf16[144,1280]{1,0:T(8,128)(2,1)S(1)}, u32[]{:S(2)}, u32[]{:S(2)}) collective-permute-start(bf16[144,1280]{1,0:T(8,128)(2,1)S(1)} %get-tuple-element.34.refs_0_.refs_4_), channel_id=1, source_target_pairs={{0,4},{1,5},{2,6},{3,7},{4,0},{5,1},{6,2},{7,3},{8,12},{9,13},{10,... | collective-permute-start | bytes 1105928 | tf_op jit(solution)/shard_map/ppermute | solution.py:32
  8.7 15.7 %collective-permute-start.9 = (bf16[144,1280]{1,0:T(8,128)(2,1)S(1)}, bf16[144,1280]{1,0:T(8,128)(2,1)S(1)}, u32[]{:S(2)}, u32[]{:S(2)}) collective-permute-start(bf16[144,1280]{1,0:T(8,128)(2,1)S(1)} %get-tuple-element.45), channel_id=1, source_target_pairs={{0,2},{1,3},{2,0},{3,1},{4,6},{5,7},{6,4},{7,5},{8,10},{9,11},{10,... | collective-permute-start | bytes 1105928 | tf_op jit(solution)/shard_map/ppermute | solution.py:22
  17.5 1.4 %copy-start.2 = (bf16[144,5120]{1,0:T(8,128)(2,1)S(1)}, bf16[144,5120]{1,0:T(8,128)(2,1)}, u32[]{:S(2)}) copy-start(bf16[144,5120]{1,0:T(8,128)(2,1)} %get-tuple-element.36.value_ref) | copy-start | bytes 4423684
  19.7 12.5 %collective-permute-start.3 = (bf16[144,1280]{1,0:T(8,128)(2,1)S(1)}, bf16[144,1280]{1,0:T(8,128)(2,1)S(1)}, u32[]{:S(2)}, u32[]{:S(2)}) collective-permute-start(bf16[144,1280]{1,0:T(8,128)(2,1)S(1)} %get-tuple-element.39), channel_id=1, source_target_pairs={{0,1},{1,2},{2,3},{3,0},{4,5},{5,6},{6,7},{7,4},{8,9},{9,10},{10,1... | collective-permute-start | bytes 1105928 | tf_op jit(solution)/shard_map/ppermute | solution.py:22
  20.2 12.0 %collective-permute-start.4 = (bf16[144,1280]{1,0:T(8,128)(2,1)S(1)}, bf16[144,1280]{1,0:T(8,128)(2,1)S(1)}, u32[]{:S(2)}, u32[]{:S(2)}) collective-permute-start(bf16[144,1280]{1,0:T(8,128)(2,1)S(1)} %get-tuple-element.40), channel_id=1, source_target_pairs={{0,3},{1,0},{2,1},{3,2},{4,7},{5,4},{6,5},{7,6},{8,11},{9,8},{10,9... | collective-permute-start | bytes 1105928 | tf_op jit(solution)/shard_map/ppermute | solution.py:22
  22.5 10.0 %collective-permute-start.11 = (bf16[144,1280]{1,0:T(8,128)(2,1)S(1)}, bf16[144,1280]{1,0:T(8,128)(2,1)S(1)}, u32[]{:S(2)}, u32[]{:S(2)}) collective-permute-start(bf16[144,1280]{1,0:T(8,128)(2,1)S(1)} %get-tuple-element.46), channel_id=1, source_target_pairs={{0,2},{1,3},{2,0},{3,1},{4,6},{5,7},{6,4},{7,5},{8,10},{9,11},{10,... | collective-permute-start | bytes 1105928 | tf_op jit(solution)/shard_map/ppermute | solution.py:22
  22.7 9.5 %collective-permute-start.5 = (bf16[144,1280]{1,0:T(8,128)(2,1)S(1)}, bf16[144,1280]{1,0:T(8,128)(2,1)S(1)}, u32[]{:S(2)}, u32[]{:S(2)}) collective-permute-start(bf16[144,1280]{1,0:T(8,128)(2,1)S(1)} %collective-permute-done.refs_0_.refs_5_), channel_id=1, source_target_pairs={{0,4},{1,5},{2,6},{3,7},{4,0},{5,1},{6,2},{7,3},{8,12},{9,13},{10,... | collective-permute-start | bytes 1105928 | tf_op jit(solution)/shard_map/ppermute | solution.py:32
  24.3 13.5 %copy-start.1 = (bf16[1,9,16,5120]{3,2,1,0:T(8,128)(2,1)S(1)}, bf16[1,9,16,5120]{3,2,1,0:T(8,128)(2,1)}, u32[]{:S(2)}) copy-start(bf16[1,9,16,5120]{3,2,1,0:T(8,128)(2,1)} %param.10) | copy-start | bytes 4423684
  24.4 10.2 %collective-permute-start.13 = (bf16[144,1280]{1,0:T(8,128)(2,1)S(1)}, bf16[144,1280]{1,0:T(8,128)(2,1)S(1)}, u32[]{:S(2)}, u32[]{:S(2)}) collective-permute-start(bf16[144,1280]{1,0:T(8,128)(2,1)S(1)} %get-tuple-element.47.refs_12_), channel_id=1, source_target_pairs={{0,4},{1,5},{2,6},{3,7},{4,0},{5,1},{6,2},{7,3},{8,12},{9,13},{10,... | collective-permute-start | bytes 1105928 | tf_op jit(solution)/shard_map/ppermute | solution.py:32
  34.8 28.1 %collective-permute-start.19 = (bf16[576,768]{1,0:T(8,128)(2,1)S(1)}, bf16[576,768]{1,0:T(8,128)(2,1)S(1)}, u32[]{:S(2)}, u32[]{:S(2)}) collective-permute-start(bf16[576,768]{1,0:T(8,128)(2,1)S(1)} %stack.3), channel_id=1, source_target_pairs={{0,4},{1,5},{2,6},{3,7},{4,0},{5,1},{6,2},{7,3},{8,12},{9,13},{10,... | collective-permute-start | bytes 2654216 | tf_op jit(solution)/shard_map/ppermute | solution.py:32
  36.8 23.7 %collective-permute-start.10 = (bf16[144,1280]{1,0:T(8,128)(2,1)S(1)}, bf16[144,1280]{1,0:T(8,128)(2,1)S(1)}, u32[]{:S(2)}, u32[]{:S(2)}) collective-permute-start(bf16[144,1280]{1,0:T(8,128)(2,1)S(1)} %collective-permute-done.1.refs_1_.refs_6_), channel_id=1, source_target_pairs={{0,4},{1,5},{2,6},{3,7},{4,0},{5,1},{6,2},{7,3},{8,12},{9,13},{10,... | collective-permute-start | bytes 1105928 | tf_op jit(solution)/shard_map/ppermute | solution.py:32
  38.7 24.3 %copy-start.6 = (bf16[144,1280]{1,0:T(8,128)(2,1)S(1)}, bf16[144,1280]{1,0:T(8,128)(2,1)}, u32[]{:S(2)}) copy-start(bf16[144,1280]{1,0:T(8,128)(2,1)} %copy-done.5) | copy-start | bytes 1105924
  38.7 24.2 %collective-permute-start.6 = (bf16[144,1280]{1,0:T(8,128)(2,1)S(1)}, bf16[144,1280]{1,0:T(8,128)(2,1)S(1)}, u32[]{:S(2)}, u32[]{:S(2)}) collective-permute-start(bf16[144,1280]{1,0:T(8,128)(2,1)S(1)} %get-tuple-element.42), channel_id=1, source_target_pairs={{0,1},{1,2},{2,3},{3,0},{4,5},{5,6},{6,7},{7,4},{8,9},{9,10},{10,1... | collective-permute-start | bytes 1105928 | tf_op jit(solution)/shard_map/ppermute | solution.py:22
  39.2 23.8 %collective-permute-start.7 = (bf16[144,1280]{1,0:T(8,128)(2,1)S(1)}, bf16[144,1280]{1,0:T(8,128)(2,1)S(1)}, u32[]{:S(2)}, u32[]{:S(2)}) collective-permute-start(bf16[144,1280]{1,0:T(8,128)(2,1)S(1)} %get-tuple-element.43), channel_id=1, source_target_pairs={{0,3},{1,0},{2,1},{3,2},{4,7},{5,4},{6,5},{7,6},{8,11},{9,8},{10,9... | collective-permute-start | bytes 1105928 | tf_op jit(solution)/shard_map/ppermute | solution.py:22
  41.6 21.3 %collective-permute-start.8 = (bf16[144,1280]{1,0:T(8,128)(2,1)S(1)}, bf16[144,1280]{1,0:T(8,128)(2,1)S(1)}, u32[]{:S(2)}, u32[]{:S(2)}) collective-permute-start(bf16[144,1280]{1,0:T(8,128)(2,1)S(1)} %get-tuple-element.44), channel_id=1, source_target_pairs={{0,2},{1,3},{2,0},{3,1},{4,6},{5,7},{6,4},{7,5},{8,10},{9,11},{10,... | collective-permute-start | bytes 1105928 | tf_op jit(solution)/shard_map/ppermute | solution.py:22
  60.7 17.9 %collective-permute-start.12 = (bf16[576,512]{1,0:T(8,128)(2,1)S(1)}, bf16[576,512]{1,0:T(8,128)(2,1)S(1)}, u32[]{:S(2)}, u32[]{:S(2)}) collective-permute-start(bf16[576,512]{1,0:T(8,128)(2,1)S(1)} %stack.2), channel_id=1, source_target_pairs={{0,4},{1,5},{2,6},{3,7},{4,0},{5,1},{6,2},{7,3},{8,12},{9,13},{10,... | collective-permute-start | bytes 1769480 | tf_op jit(solution)/shard_map/ppermute | solution.py:32
  73.5 13.8 %collective-permute-start.20 = (bf16[144,768]{1,0:T(8,128)(2,1)S(1)}, bf16[144,768]{1,0:T(8,128)(2,1)S(1)}, u32[]{:S(2)}, u32[]{:S(2)}) collective-permute-start(bf16[144,768]{1,0:T(8,128)(2,1)S(1)} %get-tuple-element.57), channel_id=1, source_target_pairs={{0,3},{1,0},{2,1},{3,2},{4,7},{5,4},{6,5},{7,6},{8,11},{9,8},{10,9... | collective-permute-start | bytes 663560 | tf_op jit(solution)/shard_map/ppermute | solution.py:22
  76.1 12.2 %collective-permute-start.21 = (bf16[144,768]{1,0:T(8,128)(2,1)S(1)}, bf16[144,768]{1,0:T(8,128)(2,1)S(1)}, u32[]{:S(2)}, u32[]{:S(2)}) collective-permute-start(bf16[144,768]{1,0:T(8,128)(2,1)S(1)} %get-tuple-element.58), channel_id=1, source_target_pairs={{0,1},{1,2},{2,3},{3,0},{4,5},{5,6},{6,7},{7,4},{8,9},{9,10},{10,1... | collective-permute-start | bytes 663560 | tf_op jit(solution)/shard_map/ppermute | solution.py:22
  76.1 12.2 %copy-start = (f32[144,3072]{1,0:T(8,128)S(1)}, f32[144,3072]{1,0:T(8,128)}, u32[]{:S(2)}) copy-start(f32[144,3072]{1,0:T(8,128)} %get-tuple-element.55.later_ref) | copy-start | bytes 5308420
  76.1 12.2 %copy-start.7 = (f32[5120]{0:T(1024)S(1)}, f32[5120]{0:T(1024)}, u32[]{:S(2)}) copy-start(f32[5120]{0:T(1024)} %param.16) | copy-start | bytes 61444
  76.1 12.2 %collective-permute-start.22 = (bf16[144,768]{1,0:T(8,128)(2,1)S(1)}, bf16[144,768]{1,0:T(8,128)(2,1)S(1)}, u32[]{:S(2)}, u32[]{:S(2)}) collective-permute-start(bf16[144,768]{1,0:T(8,128)(2,1)S(1)} %get-tuple-element.59), channel_id=1, source_target_pairs={{0,2},{1,3},{2,0},{3,1},{4,6},{5,7},{6,4},{7,5},{8,10},{9,11},{10,... | collective-permute-start | bytes 663560 | tf_op jit(solution)/shard_map/ppermute | solution.py:22
  85.7 18.3 %copy-start.4 = (f32[144,2048]{1,0:T(8,128)S(1)}, f32[144,2048]{1,0:T(8,128)}, u32[]{:S(2)}) copy-start(f32[144,2048]{1,0:T(8,128)} %get-tuple-element.35.later_ref) | copy-start | bytes 3538948
  85.8 18.3 %collective-permute-start.14 = (bf16[144,512]{1,0:T(8,128)(2,1)S(1)}, bf16[144,512]{1,0:T(8,128)(2,1)S(1)}, u32[]{:S(2)}, u32[]{:S(2)}) collective-permute-start(bf16[144,512]{1,0:T(8,128)(2,1)S(1)} %get-tuple-element.49), channel_id=1, source_target_pairs={{0,3},{1,0},{2,1},{3,2},{4,7},{5,4},{6,5},{7,6},{8,11},{9,8},{10,9... | collective-permute-start | bytes 442376 | tf_op jit(solution)/shard_map/ppermute | solution.py:22
  86.5 17.5 %collective-permute-start.15 = (bf16[144,512]{1,0:T(8,128)(2,1)S(1)}, bf16[144,512]{1,0:T(8,128)(2,1)S(1)}, u32[]{:S(2)}, u32[]{:S(2)}) collective-permute-start(bf16[144,512]{1,0:T(8,128)(2,1)S(1)} %get-tuple-element.50), channel_id=1, source_target_pairs={{0,1},{1,2},{2,3},{3,0},{4,5},{5,6},{6,7},{7,4},{8,9},{9,10},{10,1... | collective-permute-start | bytes 442376 | tf_op jit(solution)/shard_map/ppermute | solution.py:22
  87.3 16.7 %collective-permute-start.16 = (bf16[144,512]{1,0:T(8,128)(2,1)S(1)}, bf16[144,512]{1,0:T(8,128)(2,1)S(1)}, u32[]{:S(2)}, u32[]{:S(2)}) collective-permute-start(bf16[144,512]{1,0:T(8,128)(2,1)S(1)} %get-tuple-element.51), channel_id=1, source_target_pairs={{0,2},{1,3},{2,0},{3,1},{4,6},{5,7},{6,4},{7,5},{8,10},{9,11},{10,... | collective-permute-start | bytes 442376 | tf_op jit(solution)/shard_map/ppermute | solution.py:22
  89.4 28.8 %copy-start.8 = (s32[32]{0:T(128)S(1)}, s32[32]{0:T(128)}, u32[]{:S(2)}) copy-start(s32[32]{0:T(128)} %overlaps_ref.3) | copy-start | bytes 388
  89.5 20.4 %collective-permute-start.23 = (bf16[64,3072]{1,0:T(8,128)(2,1)S(1)}, bf16[64,3072]{1,0:T(8,128)(2,1)S(1)}, u32[]{:S(2)}, u32[]{:S(2)}) collective-permute-start(bf16[64,3072]{1,0:T(8,128)(2,1)S(1)} %get-tuple-element.62.refs_2_), channel_id=1, source_target_pairs={{0,8},{8,16},{16,24},{24,32},{32,40},{40,48},{48,56},{56,64},{64,7... | collective-permute-start | bytes 1179656 | tf_op jit(solution)/shard_map/ppermute | solution.py:401
  104.0 14.2 %collective-permute-start.24 = (bf16[64,3072]{1,0:T(8,128)(2,1)S(1)}, bf16[64,3072]{1,0:T(8,128)(2,1)S(1)}, u32[]{:S(2)}, u32[]{:S(2)}) collective-permute-start(bf16[64,3072]{1,0:T(8,128)(2,1)S(1)} %get-tuple-element.60.refs_0_), channel_id=1, source_target_pairs={{0,248},{8,0},{16,8},{24,16},{32,24},{40,32},{48,40},{56,48},{64,5... | collective-permute-start | bytes 1179656 | tf_op jit(solution)/shard_map/ppermute | solution.py:401
  104.6 16.4 %collective-permute-start.17 = (bf16[64,2048]{1,0:T(8,128)(2,1)S(1)}, bf16[64,2048]{1,0:T(8,128)(2,1)S(1)}, u32[]{:S(2)}, u32[]{:S(2)}) collective-permute-start(bf16[64,2048]{1,0:T(8,128)(2,1)S(1)} %get-tuple-element.54.refs_2_), channel_id=1, source_target_pairs={{0,8},{8,16},{16,24},{24,32},{32,40},{40,48},{48,56},{56,64},{64,7... | collective-permute-start | bytes 786440 | tf_op jit(solution)/shard_map/ppermute | solution.py:401
  109.8 11.3 %collective-permute-start.18 = (bf16[64,2048]{1,0:T(8,128)(2,1)S(1)}, bf16[64,2048]{1,0:T(8,128)(2,1)S(1)}, u32[]{:S(2)}, u32[]{:S(2)}) collective-permute-start(bf16[64,2048]{1,0:T(8,128)(2,1)S(1)} %get-tuple-element.52.refs_0_), channel_id=1, source_target_pairs={{0,248},{8,0},{16,8},{24,16},{32,24},{40,32},{48,40},{56,48},{64,5... | collective-permute-start | bytes 786440 | tf_op jit(solution)/shard_map/ppermute | solution.py:401
where the time goes:
time: 123 us
  starting transfers between devices  52.2 us (42%)
  Pallas kernels  34.1 us (28%)
  waiting for transfers between devices  33.6 us (27%)
  local copies, waits for them, and re-layouts  2.77 us (2%)
    ppermute x15, starting transfers between devices, send(): return lax.ppermute(value, 'token', pairs)  21.4 us
    ppermute x4, starting transfers between devices, shift(): return lax.ppermute(value, 'window', pairs)  19.8 us
    ppermute x6, waiting for transfers between devices, across(): return lax.ppermute(value, 'token', pairs)  18.4 us
    pallas_call x2, Pallas kernels, attend(): pl.pallas_call(body, name='attend', out_shape=[jax.ShapeDtypeStruct((rows...  17.6 us
    ppermute x6, starting transfers between devices, across(): return lax.ppermute(value, 'token', pairs)  11 us
    ppermute x4, waiting for transfers between devices, shift(): return lax.ppermute(value, 'window', pairs)  8.44 us
    pallas_call x1, Pallas kernels, hide(): pl.pallas_call(body, name='hide', grid=(frames // step,), out_shape=[jax....  7.25 us
    ppermute x15, waiting for transfers between devices, send(): return lax.ppermute(value, 'token', pairs)  6.8 us
  transfers between devices with their start and end apart: 25, of which 5 were waited for; matrix products, arithmetic and copies ran while one was open for 0% of the time, Pallas kernels for 25%

commit v1 on v0

v1 whole, which is shorter than its diff:
```python
import math

import jax
import jax.numpy as jnp
from jax import lax
from jax.experimental import pallas as pl
from jax.experimental.pallas import tpu as pltpu
from jax.sharding import PartitionSpec as P

HEAD_DIM = 128
MAXOV = 4
XS, YS = 2, 4
MOVES = (0, 1, 3, 2)
ANY = pl.BlockSpec(memory_space=pl.ANY)
SMEM = pl.BlockSpec(memory_space=pltpu.SMEM)
VMEM = pl.BlockSpec(memory_space=pltpu.VMEM)
VMEM_BYTES = 56 * 2**20
PARTS = (6, 4)


def send(value, move):
    pairs = [(x * YS + y, x * YS + (y + move) % YS) for x in range(XS) for y in range(YS)]
    return lax.ppermute(value, "token", pairs)


def send_back(value, move):
    return send(value, YS - move)


def across(value):
    half = XS // 2
    pairs = [(x * YS + y, (x + half) % XS * YS + y) for x in range(XS) for y in range(YS)]
    return lax.ppermute(value, "token", pairs)


def owner(move):
    return lax.rem(lax.axis_index("token") + move, YS)


def lanes(start, size):
    return pl.ds(pl.multiple_of(start, HEAD_DIM), size)


def whole(refs, sems):
    copies = [pltpu.make_async_copy(a, b, sems.at[i]) for i, (a, b) in enumerate(refs)]
    for copy in copies:
        copy.start()
    return copies


def pack(value, wide, moves, after=()):
    rows = value.shape[0]
    count = len(moves)

    def body(value_ref, *refs):
        outs, sems = refs[len(after) : -1], refs[-1]
        copies = whole(
            [
                (value_ref.at[:, lanes(owner(move) * wide, wide)], out)
                for move, out in zip(moves, outs)
            ],
            sems,
        )
        for copy in copies:
            copy.wait()

    return pl.pallas_call(
        body,
        name="pack",
        out_shape=[jax.ShapeDtypeStruct((rows, wide), value.dtype)] * count,
        in_specs=[ANY] * (1 + len(after)),
        out_specs=[VMEM] * count,
        scratch_shapes=[pltpu.SemaphoreType.DMA((count,))],
        compiler_params=pltpu.CompilerParams(vmem_limit_bytes=4 * 2**20),
        cost_estimate=pl.CostEstimate(
            flops=0, bytes_accessed=4 * count * rows * wide, transcendentals=0
        ),
    )(value, *after)


def stack(pieces, skip, take, after=()):
    rows = pieces[0].shape[0]
    count = len(pieces)

    def body(*refs):
        sources = refs[:count]
        out, held, in_sems, out_sem = refs[count + len(after) :]
        arriving = whole(
            [
                (source.at[:, pl.ds(skip, take)], held.at[pl.ds(i * rows, rows)])
                for i, source in enumerate(sources)
            ],
            in_sems,
        )
        for copy in arriving:
            copy.wait()
        leaving = pltpu.make_async_copy(held, out, out_sem)
        leaving.start()
        leaving.wait()

    return pl.pallas_call(
        body,
        name="stack",
        out_shape=jax.ShapeDtypeStruct((count * rows, take), pieces[0].dtype),
        in_specs=[ANY] * (count + len(after)),
        out_specs=ANY,
        scratch_shapes=[
            pltpu.VMEM((count * rows, take), pieces[0].dtype),
            pltpu.SemaphoreType.DMA((count,)),
            pltpu.SemaphoreType.DMA,
        ],
        compiler_params=pltpu.CompilerParams(vmem_limit_bytes=4 * 2**20),
        cost_estimate=pl.CostEstimate(
            flops=0, bytes_accessed=4 * count * rows * take, transcendentals=0
        ),
    )(*pieces, *after)


def hold(values, after):
    count = len(values)

    def body(*refs):
        del refs

    return pl.pallas_call(
        body,
        name="hold",
        out_shape=[jax.ShapeDtypeStruct(value.shape, value.dtype) for value in values],
        in_specs=[ANY] * (count + len(after)),
        out_specs=[ANY] * count,
        input_output_aliases={i: i for i in range(count)},
        compiler_params=pltpu.CompilerParams(vmem_limit_bytes=2**20),
    )(*values, *after)


def mixes(plan_ref, refresh_ref, blocks):
    chosen = refresh_ref[lax.axis_index("window")]
    plan = [plan_ref[b].astype(jnp.float32) for b in range(blocks)]
    before = [jnp.where(b < chosen, plan[b], 0.0) for b in range(blocks)]
    after = [jnp.where(b > chosen, plan[b], 0.0) for b in range(blocks)]
    return before, after


def prepare(latents, cached, plan, refresh, gain, wide, after):
    blocks = cached.shape[0]
    frames, spots, width = latents.shape
    count = len(MOVES)
    step = 3
    rows = step * spots

    def body(plan_ref, refresh_ref, latents_ref, cached_ref, gain_ref, *refs):
        outs, values_ref = refs[len(after) : -1], refs[-1]
        before, _ = mixes(plan_ref, refresh_ref, blocks)
        for i in range(step):
            hidden = latents_ref[i].astype(jnp.float32)
            for b in range(blocks):
                hidden = hidden + before[b] * cached_ref[b, i].astype(jnp.float32)
            mean_square = jnp.mean(hidden * hidden, axis=-1, keepdims=True)
            values = hidden * lax.rsqrt(mean_square + 1e-06) * gain_ref[...]
            values_ref[pl.ds(i * spots, spots), :] = values.astype(values_ref.dtype)
        for move, out in zip(MOVES, outs):
            out[...] = values_ref[:, lanes(owner(move) * wide, wide)]

    return pl.pallas_call(
        body,
        name="prepare",
        grid=(frames // step,),
        out_shape=[jax.ShapeDtypeStruct((frames * spots, wide), jnp.bfloat16)] * count,
        in_specs=[
            SMEM,
            SMEM,
            pl.BlockSpec((step, spots, width), lambda f: (f, 0, 0)),
            pl.BlockSpec((blocks, step, spots, width), lambda f: (0, f, 0, 0)),
            pl.BlockSpec((1, width), lambda f: (0, 0)),
        ]
        + [ANY] * len(after),
        out_specs=[pl.BlockSpec((rows, wide), lambda f: (f, 0))] * count,
        scratch_shapes=[pltpu.VMEM((rows, width), jnp.bfloat16)],
        compiler_params=pltpu.CompilerParams(vmem_limit_bytes=16 * 2**20),
        cost_estimate=pl.CostEstimate(
            flops=20 * latents.size, bytes_accessed=12 * latents.size, transcendentals=0
        ),
    )(plan, refresh, latents, cached, gain, *after)


def add(latents, cached, plan, refresh, wide, parts):
    blocks = cached.shape[0]
    frames, spots, width = latents.shape
    count = len(MOVES)
    step = 3
    rows = step * spots

    def body(plan_ref, refresh_ref, latents_ref, cached_ref, *refs):
        laters, later_ref = refs[:-1], refs[-1]
        before, after = mixes(plan_ref, refresh_ref, blocks)
        for i in range(step):
            later = latents_ref[i].astype(jnp.float32)
            for b in range(blocks):
                later = later + (before[b] + after[b]) * cached_ref[b, i].astype(jnp.float32)
            later_ref[pl.ds(i * spots, spots), :] = later
        for i, move in enumerate(MOVES):
            start = owner(move) * wide
            for take, later in zip(parts, laters):
                later[:, pl.ds(i * take, take)] = later_ref[:, lanes(start, take)]
                start += take

    return pl.pallas_call(
        body,
        name="add",
        grid=(frames // step,),
        out_shape=[
            jax.ShapeDtypeStruct((frames * spots, count * take), jnp.float32) for take in parts
        ],
        in_specs=[
            SMEM,
            SMEM,
            pl.BlockSpec((step, spots, width), lambda f: (f, 0, 0)),
            pl.BlockSpec((blocks, step, spots, width), lambda f: (0, f, 0, 0)),
        ],
        out_specs=[pl.BlockSpec((rows, count * take), lambda f: (f, 0)) for take in parts],
        scratch_shapes=[pltpu.VMEM((rows, width), jnp.float32)],
        compiler_params=pltpu.CompilerParams(vmem_limit_bytes=24 * 2**20),
        cost_estimate=pl.CostEstimate(
            flops=10 * latents.size, bytes_accessed=14 * latents.size, transcendentals=0
        ),
    )(plan, refresh, latents, cached)


def attend(asked, keys, values, skip, take):
    rows = asked[0].shape[0]
    count, places = len(asked), len(keys)
    pieces = [(piece, 0, skip) for piece in asked] + keys + values
    arrays = list({id(piece[0]): piece[0] for piece in pieces}.values())
    index = {id(array): i for i, array in enumerate(arrays)}
    where = [(index[id(array)], row, col) for array, row, col in pieces]
    scale = math.log2(math.e) / math.sqrt(HEAD_DIM)
    unroll = 2

    def body(*refs):
        sources, outs = refs[: len(arrays)], refs[len(arrays) :]

        def rows_of(chosen, first):
            return jnp.concatenate(
                [
                    sources[i][pl.ds(row, rows), lanes(col + first, HEAD_DIM)]
                    for i, row, col in chosen
                ],
                axis=0,
            )

        @pl.loop(0, take // (unroll * HEAD_DIM))
        def _(step):
            for u in range(unroll):
                first = (step * unroll + u) * HEAD_DIM
                query = rows_of(where[:count], first)
                key = rows_of(where[count : count + places], first)
                value = rows_of(where[count + places :], first)
                scores = lax.dot_general(
                    query, key, (((1,), (1,)), ((), ())), preferred_element_type=jnp.float32
                )
                peak = jnp.max(scores, axis=1, keepdims=True)
                weights = jnp.exp2((scores - peak) * scale).astype(jnp.bfloat16)
                both = jnp.concatenate([value, jnp.ones_like(value)], axis=1)
                total = jnp.dot(weights, both, preferred_element_type=jnp.float32)
                result = (total[:, :HEAD_DIM] / total[:, HEAD_DIM:]).astype(jnp.bfloat16)
                for i, out in enumerate(outs):
                    out[:, lanes(first, HEAD_DIM)] = result[i * rows : (i + 1) * rows]

    work = count * rows * places * rows * take
    return pl.pallas_call(
        body,
        name="attend",
        out_shape=[jax.ShapeDtypeStruct((rows, take), jnp.bfloat16)] * count,
        in_specs=[VMEM] * len(arrays),
        out_specs=[VMEM] * count,
        compiler_params=pltpu.CompilerParams(vmem_limit_bytes=24 * 2**20),
        cost_estimate=pl.CostEstimate(
            flops=8 * work,
            bytes_accessed=12 * places * rows * take,
            transcendentals=work // HEAD_DIM,
        ),
    )(*arrays)


def join(later, gate, attended, frames, wide, skip):
    count = len(MOVES)
    rows, take = attended[0].shape
    spots = rows // frames
    ends = MAXOV * spots
    sizes = (ends, rows - 2 * ends, ends)

    def body(later_ref, gate_ref, *refs):
        pieces, outs = refs[:count], refs[count:]
        for i, move in enumerate(MOVES):
            span = pl.ds(i * take, take)
            gates = gate_ref[:, lanes(owner(move) * wide + skip, take)]
            pre = later_ref[:, span] + gates * pieces[i][...].astype(jnp.float32)
            pre, start = pre.astype(jnp.bfloat16), 0
            for out, size in zip(outs, sizes):
                out[:, span] = pre[start : start + size]
                start += size

    return pl.pallas_call(
        body,
        name="join",
        out_shape=[jax.ShapeDtypeStruct((size, count * take), jnp.bfloat16) for size in sizes],
        in_specs=[VMEM] * (2 + count),
        out_specs=[VMEM] * 3,
        compiler_params=pltpu.CompilerParams(vmem_limit_bytes=8 * 2**20),
        cost_estimate=pl.CostEstimate(
            flops=2 * later.size, bytes_accessed=8 * later.size, transcendentals=0
        ),
    )(later, gate, *attended)


def blend(intersections, first, middle, last, from_prev, from_next, frames, wide, skip, before):
    count = len(MOVES)
    take = first.shape[1] // count
    ends = first.shape[0]
    spots = ends // MAXOV
    rows = frames * spots

    def body(overlaps_ref, *refs):
        first_ref, middle_ref, last_ref, prev, after = refs[:5]
        out_ref, result, out_sems = refs[-3:]
        window, windows = lax.axis_index("window"), lax.axis_size("window")
        ov_next = overlaps_ref[window]
        ov_prev = overlaps_ref[lax.rem(window + windows - 1, windows)]
        result[pl.ds(ends, rows - 2 * ends), :] = middle_ref[...]
        for f in range(MAXOV):
            ramp = jnp.where(
                f < ov_prev, jnp.float32(f + 1) / (ov_prev + 1).astype(jnp.float32), 1.0
            )
            other = jnp.clip(MAXOV - ov_prev + f, 0, MAXOV - 1) * spots
            mixed = (1.0 - ramp) * prev[pl.ds(pl.multiple_of(other, 16), spots), :].astype(
                jnp.float32
            ) + ramp * first_ref[pl.ds(f * spots, spots), :].astype(jnp.float32)
            result[pl.ds(f * spots, spots), :] = mixed.astype(result.dtype)
        for f in range(frames - MAXOV, frames):
            tail = f - frames + ov_next
            ramp = jnp.where(
                tail >= 0,
                (tail + 1).astype(jnp.float32) / (ov_next + 1).astype(jnp.float32),
                0.0,
            )
            other = jnp.clip(tail, 0, MAXOV - 1) * spots
            own = pl.ds((f - frames + MAXOV) * spots, spots)
            mixed = (1.0 - ramp) * last_ref[own, :].astype(jnp.float32) + ramp * after[
                pl.ds(pl.multiple_of(other, 16), spots), :
            ].astype(jnp.float32)
            result[pl.ds(f * spots, spots), :] = mixed.astype(result.dtype)
        leaving = whole(
            [
                (
                    result.at[:, pl.ds(i * take, take)],
                    out_ref.at[:, lanes(owner(move) * wide + skip, take)],
                )
                for i, move in enumerate(MOVES)
            ],
            out_sems,
        )
        for copy in leaving:
            copy.wait()

    extra = () if before is None else (before,)
    return pl.pallas_call(
        body,
        name="blend",
        out_shape=jax.ShapeDtypeStruct((rows, count * wide), jnp.bfloat16),
        in_specs=[SMEM] + [VMEM] * 5 + [ANY] * len(extra),
        out_specs=ANY,
        input_output_aliases={6: 0} if extra else {},
        scratch_shapes=[
            pltpu.VMEM((rows, count * take), jnp.bfloat16),
            pltpu.SemaphoreType.DMA((count,)),
        ],
        compiler_params=pltpu.CompilerParams(vmem_limit_bytes=6 * 2**20),
        cost_estimate=pl.CostEstimate(
            flops=4 * rows * count * take,
            bytes_accessed=8 * rows * count * take,
            transcendentals=0,
        ),
    )(intersections, first, middle, last, from_prev, from_next, *extra)


def shift(value, steps):
    count = lax.axis_size("window")
    pairs = [(source, (source + steps) % count) for source in range(count)]
    return lax.ppermute(value, "window", pairs)


def spread(pieces, how):
    return [how(piece, move) if move else piece for piece, move in zip(pieces, MOVES)]


def on_device(
    latents, queries, attn_keys, cached, plan, refresh, value_gain, attn_gate, intersections
):
    _, frames, spots, width = latents.shape
    rows = frames * spots
    wide = width // len(MOVES)
    parts = [heads * HEAD_DIM for heads in PARTS]
    skips = [sum(parts[:i]) for i in range(len(parts))]
    queries = queries.reshape(rows, width)
    gate = attn_gate.reshape(1, width)
    latents, cached = latents[0], cached[:, 0]
    attn_keys = attn_keys.reshape(rows, width)
    packed = pack(attn_keys, wide, MOVES)
    value, *values = prepare(
        latents, cached, plan, refresh, value_gain.reshape(1, width), wide, packed[:1]
    )
    far_keys = [across(packed[0])]
    keys = spread(packed, send)
    keys[1:3] = hold(keys[1:3], (value,))
    far_value = across(value)
    far_keys += [across(key) for key in keys[1:3]]
    near = hold(values[:2], (*keys[1:3], far_keys[0]))
    values = spread([value, *near, *hold(values[2:], (keys[3], far_value))], send)
    asked = spread(pack(queries, wide, MOVES, (*values[1:3], far_keys[1])), send)
    laters = add(latents, cached, plan, refresh, wide, parts)
    moved = [keys[3], *values[1:]]
    afters = ((*far_keys[1:], far_value, *laters), ())
    rests = [
        across(stack(moved, skip, take, after))
        for skip, take, after in zip(skips, parts, afters)
    ]
    out = None
    for later, rest, skip, take in zip(laters, rests, skips, parts):
        key_places = [(key, 0, skip) for key in keys + far_keys] + [(rest, 0, 0)]
        value_places = [(value, 0, skip) for value in [*values, far_value]] + [
            (rest, i * rows, 0) for i in (1, 2, 3)
        ]
        attended = spread(attend(asked, key_places, value_places, skip, take), send_back)
        first, middle, last = join(later, gate, attended, frames, wide, skip)
        from_prev = shift(last, 1)
        from_next = shift(first, -1)
        out = blend(
            intersections, first, middle, last, from_prev, from_next, frames, wide, skip, out
        )
    return out.reshape(1, frames, spots, width)


def solution(mesh):
    in_specs = (
        P("window", None, "token", None),
        P("window", None, "token", None),
        P("window", None, "token", None),
        P(None, "window", None, "token", None),
        P(),
        P(),
        P(),
        P(),
        P(),
    )
    out_specs = P("window", None, "token", None)
    return jax.shard_map(
        on_device, mesh=mesh, in_specs=in_specs, out_specs=out_specs, check_vma=False
    )
```

time: 123 us -> 107 us (0.87)
  starting transfers between devices: 52.2 us -> 37.9 us
  Pallas kernels: 34.1 us -> 21.6 us
  waiting for transfers between devices: 33.6 us -> 41.6 us
  local copies, waits for them, and re-layouts: 2.77 us -> 4.91 us
    ppermute x4, starting transfers between devices: 19.8 us -> 10.9 us  [shift(): return lax.ppermute(value, 'window', pairs)]
    ppermute x15, waiting for transfers between devices: 6.8 us -> 13.5 us  [send(): return lax.ppermute(value, 'token', pairs)]
    pallas_call x2, Pallas kernels: 17.6 us -> 11 us  [attend(): pl.pallas_call(body, name='attend', out_shape=[jax.ShapeDtypeStruct((rows...]
    ppermute x15, starting transfers between devices: 21.4 us -> 17 us  [send(): return lax.ppermute(value, 'token', pairs)]
    pallas_call x3 -> x2, Pallas kernels: 2.47 us -> 0.33 us  [pack(): pl.pallas_call(body, name='pack', out_shape=[jax.ShapeDtypeStruct((rows,...]
    unnamed x18 -> x20, local copies, waits for them, and re-layouts: 2.77 us -> 4.91 us
    pallas_call x1 -> x5, Pallas kernels: 7.25 us -> 5.89 us  [the longest x1 2.98 us: prepare(): pl.pallas_call(body, name='prepare', grid=(frames // step,), out_shape=[j...]
  transfers between devices with their start and end apart: 25 -> 25, of which waited for: 5 -> 11; matrix products, arithmetic and copies ran while one was open for 0% -> 0% of each run, Pallas kernels for 25% -> 18%
where the time goes in v1:
time: 107 us; the launch traced here: 106 us
  waiting for transfers between devices  41.6 us (39%)
  starting transfers between devices  37.9 us (35%)
  Pallas kernels  21.6 us (20%)
  local copies, waits for them, and re-layouts  4.91 us (5%)
    ppermute x6, waiting for transfers between devices, across(): return lax.ppermute(value, 'token', pairs)  19.5 us
    ppermute x15, starting transfers between devices, send(): return lax.ppermute(value, 'token', pairs)  17 us
    ppermute x15, waiting for transfers between devices, send(): return lax.ppermute(value, 'token', pairs)  13.5 us
    pallas_call x2, Pallas kernels, attend(): pl.pallas_call(body, name='attend', out_shape=[jax.ShapeDtypeStruct((rows...  11 us
    ppermute x4, starting transfers between devices, shift(): return lax.ppermute(value, 'window', pairs)  10.9 us
    ppermute x6, starting transfers between devices, across(): return lax.ppermute(value, 'token', pairs)  10 us
    ppermute x4, waiting for transfers between devices, shift(): return lax.ppermute(value, 'window', pairs)  8.61 us
    unnamed x20, local copies, waits for them, and re-layouts  4.91 us
  transfers between devices with their start and end apart: 25, of which 11 were waited for; matrix products, arithmetic and copies ran while one was open for 0% of the time, Pallas kernels for 18%

profile of v1, /device:TPU:1, one launch (start us, length us, event | category | flops | bytes accessed | tf_op | source)
XLA Modules:
  0.0 106.3 jit_solution(8690901048835829085)
XLA Ops:
  0.0 1.5 %copy-done.4 = bf16[1,9,16,5120]{3,2,1,0:T(8,128)(2,1)S(1)} copy-done((bf16[1,9,16,5120]{3,2,1,0:T(8,128)(2,1)S(1)}, bf16[1,9,16,5120]{3,2,1,0:T(8,128)(2,1)}, u32[]{:S(2)}) %copy-start.4) | copy-done | bytes 1474584
  1.5 0.2 pack.2
  1.7 2.2 %collective-permute-start = (bf16[144,1280]{1,0:T(8,128)(2,1)S(1)}, bf16[144,1280]{1,0:T(8,128)(2,1)S(1)}, u32[]{:S(2)}, u32[]{:S(2)}) collective-permute-start(bf16[144,1280]{1,0:T(8,128)(2,1)S(1)} %get-tuple-element.41), channel_id=1, source_target_pairs={{0,1},{1,2},{2,3},{3,0},{4,5},{5,6},{6,7},{7,4},{8,9},{9,10},{10,1... | collective-permute-start | bytes 1105928 | tf_op jit(solution)/shard_map/ppermute | solution.py:23
  3.9 1.5 %collective-permute-start.1 = (bf16[144,1280]{1,0:T(8,128)(2,1)S(1)}, bf16[144,1280]{1,0:T(8,128)(2,1)S(1)}, u32[]{:S(2)}, u32[]{:S(2)}) collective-permute-start(bf16[144,1280]{1,0:T(8,128)(2,1)S(1)} %get-tuple-element.42), channel_id=1, source_target_pairs={{0,3},{1,0},{2,1},{3,2},{4,7},{5,4},{6,5},{7,6},{8,11},{9,8},{10,9... | collective-permute-start | bytes 1105928 | tf_op jit(solution)/shard_map/ppermute | solution.py:23
  5.4 1.6 %collective-permute-start.9 = (bf16[144,1280]{1,0:T(8,128)(2,1)S(1)}, bf16[144,1280]{1,0:T(8,128)(2,1)S(1)}, u32[]{:S(2)}, u32[]{:S(2)}) collective-permute-start(bf16[144,1280]{1,0:T(8,128)(2,1)S(1)} %get-tuple-element.52), channel_id=1, source_target_pairs={{0,2},{1,3},{2,0},{3,1},{4,6},{5,7},{6,4},{7,5},{8,10},{9,11},{10,... | collective-permute-start | bytes 1105928 | tf_op jit(solution)/shard_map/ppermute | solution.py:23
  7.0 2.7 %collective-permute-start.2 = (bf16[144,1280]{1,0:T(8,128)(2,1)S(1)}, bf16[144,1280]{1,0:T(8,128)(2,1)S(1)}, u32[]{:S(2)}, u32[]{:S(2)}) collective-permute-start(bf16[144,1280]{1,0:T(8,128)(2,1)S(1)} %get-tuple-element.38.refs_0_.refs_4_), channel_id=1, source_target_pairs={{0,4},{1,5},{2,6},{3,7},{4,0},{5,1},{6,2},{7,3},{8,12},{9,13},{10,... | collective-permute-start | bytes 1105928 | tf_op jit(solution)/shard_map/ppermute | solution.py:33
  9.7 2.7 %copy-done = bf16[4,1,9,16,5120]{4,3,2,1,0:T(8,128)(2,1)S(1)} copy-done((bf16[4,1,9,16,5120]{4,3,2,1,0:T(8,128)(2,1)S(1)}, bf16[4,1,9,16,5120]{4,3,2,1,0:T(8,128)(2,1)}, u32[]{:S(2)}) %copy-start) | copy-done | bytes 5898264
  12.4 0.7 copy-done.6
  13.1 3.0 %prepare.1 = (bf16[144,1280]{1,0:T(8,128)(2,1)S(1)}, bf16[144,1280]{1,0:T(8,128)(2,1)S(1)}, bf16[144,1280]{1,0:T(8,128)(2,1)S(1)}, bf16[144,1280]{1,0:T(8,128)(2,1)S(1)}) custom-call(s32[4]{0:T(128)S(1)} %copy-done.7, s32[32]{0:T(128)S(1)} %copy-done.8, bf16[9,16,5120]{2,1,0:T(8,128)(2,1)S(1)} %bitcast.9, bf16[4,9,16,5120]{3,2,1,0:T(8,128)(2,1)S(1)} %bitcast.7, ...), custom_call_target="tpu_custom_call" | custom-call | flops 14745600 | bytes 8847360 | tf_op jit(solution)/shard_map/prepare/pallas_call | solution.py:164
  16.1 0.3 collective-permute-start.11
  16.4 0.0 collective-permute-done.refs_0_
  16.4 0.0 collective-permute-done.1.refs_1_
  16.4 2.7 %collective-permute-start.5 = (bf16[144,1280]{1,0:T(8,128)(2,1)S(1)}, bf16[144,1280]{1,0:T(8,128)(2,1)S(1)}, u32[]{:S(2)}, u32[]{:S(2)}) collective-permute-start(bf16[144,1280]{1,0:T(8,128)(2,1)S(1)} %get-tuple-element.44.refs_2_.refs_5_), channel_id=1, source_target_pairs={{0,4},{1,5},{2,6},{3,7},{4,0},{5,1},{6,2},{7,3},{8,12},{9,13},{10,... | collective-permute-start | bytes 1105928 | tf_op jit(solution)/shard_map/ppermute | solution.py:33
  19.2 0.3 collective-permute-start.10
  19.4 0.0 collective-permute-done.2.refs_4_.refs_8_
  19.4 0.4 collective-permute-start.3
  19.8 2.6 %collective-permute-done.9.refs_1_.refs_0_.refs_7_ = bf16[144,1280]{1,0:T(8,128)(2,1)S(1)} collective-permute-done((bf16[144,1280]{1,0:T(8,128)(2,1)S(1)}, bf16[144,1280]{1,0:T(8,128)(2,1)S(1)}, u32[]{:S(2)}, u32[]{:S(2)}) %collective-permute-start.9) | collective-permute-done | bytes 368672 | tf_op jit(solution)/shard_map/ppermute | solution.py:23
  22.4 0.7 collective-permute-start.4
  23.1 2.9 %collective-permute-done.11.refs_2_.refs_16_.refs_6_ = bf16[144,1280]{1,0:T(8,128)(2,1)S(1)} collective-permute-done((bf16[144,1280]{1,0:T(8,128)(2,1)S(1)}, bf16[144,1280]{1,0:T(8,128)(2,1)S(1)}, u32[]{:S(2)}, u32[]{:S(2)}) %collective-permute-start.11) | collective-permute-done | bytes 368672 | tf_op jit(solution)/shard_map/ppermute | solution.py:33
  26.0 1.6 %collective-permute-start.12 = (bf16[144,1280]{1,0:T(8,128)(2,1)S(1)}, bf16[144,1280]{1,0:T(8,128)(2,1)S(1)}, u32[]{:S(2)}, u32[]{:S(2)}) collective-permute-start(bf16[144,1280]{1,0:T(8,128)(2,1)S(1)} %hold.5), channel_id=1, source_target_pairs={{0,2},{1,3},{2,0},{3,1},{4,6},{5,7},{6,4},{7,5},{8,10},{9,11},{10,... | collective-permute-start | bytes 1105928 | tf_op jit(solution)/shard_map/ppermute | solution.py:23
  27.5 2.9 %add.1 = (f32[144,3072]{1,0:T(8,128)S(1)}, f32[144,2048]{1,0:T(8,128)S(1)}) custom-call(s32[4]{0:T(128)S(1)} %copy-done.7, s32[32]{0:T(128)S(1)} %copy-done.8, bf16[9,16,5120]{2,1,0:T(8,128)(2,1)S(1)} %bitcast.10, bf16[4,9,16,5120]{3,2,1,0:T(8,128)(2,1)S(1)} %bitcast.8), custom_call_target="tpu_custom_call" | custom-call | flops 7372800 | bytes 10321920 | tf_op jit(solution)/shard_map/add/pallas_call | solution.py:207
  30.4 0.0 collective-permute-done.3.refs_0_.refs_1_.refs_13_
  30.5 0.0 collective-permute-done.4.refs_1_.refs_2_.refs_14_
  30.5 3.4 %collective-permute-done.5.refs_2_.refs_9_.refs_4_ = bf16[144,1280]{1,0:T(8,128)(2,1)S(1)} collective-permute-done((bf16[144,1280]{1,0:T(8,128)(2,1)S(1)}, bf16[144,1280]{1,0:T(8,128)(2,1)S(1)}, u32[]{:S(2)}, u32[]{:S(2)}) %collective-permute-start.5) | collective-permute-done | bytes 368672 | tf_op jit(solution)/shard_map/ppermute | solution.py:33
  33.9 7.9 %collective-permute-done.10.refs_10_.refs_5_ = bf16[144,1280]{1,0:T(8,128)(2,1)S(1)} collective-permute-done((bf16[144,1280]{1,0:T(8,128)(2,1)S(1)}, bf16[144,1280]{1,0:T(8,128)(2,1)S(1)}, u32[]{:S(2)}, u32[]{:S(2)}) %collective-permute-start.10) | collective-permute-done | bytes 368672 | tf_op jit(solution)/shard_map/ppermute | solution.py:33
  41.8 0.0 collective-permute-done.12.refs_3_.refs_15_
  41.8 0.3 stack.3
  42.1 2.7 %collective-permute-start.19 = (bf16[576,768]{1,0:T(8,128)(2,1)S(1)}, bf16[576,768]{1,0:T(8,128)(2,1)S(1)}, u32[]{:S(2)}, u32[]{:S(2)}) collective-permute-start(bf16[576,768]{1,0:T(8,128)(2,1)S(1)} %stack.3), channel_id=1, source_target_pairs={{0,4},{1,5},{2,6},{3,7},{4,0},{5,1},{6,2},{7,3},{8,12},{9,13},{10,... | collective-permute-start | bytes 2654216 | tf_op jit(solution)/shard_map/ppermute | solution.py:33
  44.8 0.2 pack.3
  45.0 0.5 collective-permute-start.6
  45.4 2.3 %collective-permute-start.7 = (bf16[144,1280]{1,0:T(8,128)(2,1)S(1)}, bf16[144,1280]{1,0:T(8,128)(2,1)S(1)}, u32[]{:S(2)}, u32[]{:S(2)}) collective-permute-start(bf16[144,1280]{1,0:T(8,128)(2,1)S(1)} %get-tuple-element.50), channel_id=1, source_target_pairs={{0,3},{1,0},{2,1},{3,2},{4,7},{5,4},{6,5},{7,6},{8,11},{9,8},{10,9... | collective-permute-start | bytes 1105928 | tf_op jit(solution)/shard_map/ppermute | solution.py:23
  47.7 0.0 collective-permute-start.8
  47.7 0.2 stack.2
  47.9 1.2 %collective-permute-start.13 = (bf16[576,512]{1,0:T(8,128)(2,1)S(1)}, bf16[576,512]{1,0:T(8,128)(2,1)S(1)}, u32[]{:S(2)}, u32[]{:S(2)}) collective-permute-start(bf16[576,512]{1,0:T(8,128)(2,1)S(1)} %stack.2), channel_id=1, source_target_pairs={{0,4},{1,5},{2,6},{3,7},{4,0},{5,1},{6,2},{7,3},{8,12},{9,13},{10,... | collective-permute-start | bytes 1769480 | tf_op jit(solution)/shard_map/ppermute | solution.py:33
  49.2 8.0 %collective-permute-done.6.refs_1_ = bf16[144,1280]{1,0:T(8,128)(2,1)S(1)} collective-permute-done((bf16[144,1280]{1,0:T(8,128)(2,1)S(1)}, bf16[144,1280]{1,0:T(8,128)(2,1)S(1)}, u32[]{:S(2)}, u32[]{:S(2)}) %collective-permute-start.6) | collective-permute-done | bytes 368672 | tf_op jit(solution)/shard_map/ppermute | solution.py:23
  57.2 0.0 collective-permute-done.7.refs_2_
  57.2 2.6 %collective-permute-done.8.refs_3_ = bf16[144,1280]{1,0:T(8,128)(2,1)S(1)} collective-permute-done((bf16[144,1280]{1,0:T(8,128)(2,1)S(1)}, bf16[144,1280]{1,0:T(8,128)(2,1)S(1)}, u32[]{:S(2)}, u32[]{:S(2)}) %collective-permute-start.8) | collective-permute-done | bytes 368672 | tf_op jit(solution)/shard_map/ppermute | solution.py:23
  59.8 2.4 %collective-permute-done.19.refs_11_ = bf16[576,768]{1,0:T(8,128)(2,1)S(1)} collective-permute-done((bf16[576,768]{1,0:T(8,128)(2,1)S(1)}, bf16[576,768]{1,0:T(8,128)(2,1)S(1)}, u32[]{:S(2)}, u32[]{:S(2)}) %collective-permute-start.19) | collective-permute-done | bytes 884768 | tf_op jit(solution)/shard_map/ppermute | solution.py:33
  62.2 6.6 %attend.3 = (bf16[144,768]{1,0:T(8,128)(2,1)S(1)}, bf16[144,768]{1,0:T(8,128)(2,1)S(1)}, bf16[144,768]{1,0:T(8,128)(2,1)S(1)}, bf16[144,768]{1,0:T(8,128)(2,1)S(1)}) custom-call(bf16[144,1280]{1,0:T(8,128)(2,1)S(1)} %get-tuple-element.48.refs_0_, bf16[144,1280]{1,0:T(8,128)(2,1)S(1)} %collective-permute-done.6.refs_1_, ...), custom_call_target="tpu_custom_call" | custom-call | flops 4076863488 | bytes 10616832 | tf_op jit(solution)/shard_map/attend/pallas_call | solution.py:270
  68.8 1.6 %collective-permute-start.20 = (bf16[144,768]{1,0:T(8,128)(2,1)S(1)}, bf16[144,768]{1,0:T(8,128)(2,1)S(1)}, u32[]{:S(2)}, u32[]{:S(2)}) collective-permute-start(bf16[144,768]{1,0:T(8,128)(2,1)S(1)} %get-tuple-element.63), channel_id=1, source_target_pairs={{0,3},{1,0},{2,1},{3,2},{4,7},{5,4},{6,5},{7,6},{8,11},{9,8},{10,9... | collective-permute-start | bytes 663560 | tf_op jit(solution)/shard_map/ppermute | solution.py:23
  70.5 0.0 collective-permute-start.21
  70.5 1.5 %collective-permute-start.22 = (bf16[144,768]{1,0:T(8,128)(2,1)S(1)}, bf16[144,768]{1,0:T(8,128)(2,1)S(1)}, u32[]{:S(2)}, u32[]{:S(2)}) collective-permute-start(bf16[144,768]{1,0:T(8,128)(2,1)S(1)} %get-tuple-element.65), channel_id=1, source_target_pairs={{0,2},{1,3},{2,0},{3,1},{4,6},{5,7},{6,4},{7,5},{8,10},{9,11},{10,... | collective-permute-start | bytes 663560 | tf_op jit(solution)/shard_map/ppermute | solution.py:23
  72.0 2.9 %collective-permute-done.13.refs_11_ = bf16[576,512]{1,0:T(8,128)(2,1)S(1)} collective-permute-done((bf16[576,512]{1,0:T(8,128)(2,1)S(1)}, bf16[576,512]{1,0:T(8,128)(2,1)S(1)}, u32[]{:S(2)}, u32[]{:S(2)}) %collective-permute-start.13) | collective-permute-done | bytes 589856 | tf_op jit(solution)/shard_map/ppermute | solution.py:33
  74.8 4.4 %attend.2 = (bf16[144,512]{1,0:T(8,128)(2,1)S(1)}, bf16[144,512]{1,0:T(8,128)(2,1)S(1)}, bf16[144,512]{1,0:T(8,128)(2,1)S(1)}, bf16[144,512]{1,0:T(8,128)(2,1)S(1)}) custom-call(bf16[144,1280]{1,0:T(8,128)(2,1)S(1)} %get-tuple-element.48.refs_0_, bf16[144,1280]{1,0:T(8,128)(2,1)S(1)} %collective-permute-done.6.refs_1_, ...), custom_call_target="tpu_custom_call" | custom-call | flops 2717908992 | bytes 7077888 | tf_op jit(solution)/shard_map/attend/pallas_call | solution.py:270
  79.3 0.7 collective-permute-start.14
  80.0 0.8 collective-permute-start.15
  80.8 0.0 collective-permute-done.20.refs_1_
  80.8 1.6 %collective-permute-start.16 = (bf16[144,512]{1,0:T(8,128)(2,1)S(1)}, bf16[144,512]{1,0:T(8,128)(2,1)S(1)}, u32[]{:S(2)}, u32[]{:S(2)}) collective-permute-start(bf16[144,512]{1,0:T(8,128)(2,1)S(1)} %get-tuple-element.57), channel_id=1, source_target_pairs={{0,2},{1,3},{2,0},{3,1},{4,6},{5,7},{6,4},{7,5},{8,10},{9,11},{10,... | collective-permute-start | bytes 442376 | tf_op jit(solution)/shard_map/ppermute | solution.py:23
  82.4 0.0 collective-permute-done.21.refs_2_
  82.4 0.0 collective-permute-done.22.refs_3_
  82.4 0.2 join.3
  82.6 0.0 copy-start.9
  82.7 5.5 %collective-permute-start.24 = (bf16[64,3072]{1,0:T(8,128)(2,1)S(1)}, bf16[64,3072]{1,0:T(8,128)(2,1)S(1)}, u32[]{:S(2)}, u32[]{:S(2)}) collective-permute-start(bf16[64,3072]{1,0:T(8,128)(2,1)S(1)} %get-tuple-element.66.refs_0_), channel_id=1, source_target_pairs={{0,248},{8,0},{16,8},{24,16},{32,24},{40,32},{48,40},{56,48},{64,5... | collective-permute-start | bytes 1179656 | tf_op jit(solution)/shard_map/ppermute | solution.py:389
  88.1 0.3 collective-permute-start.23
  88.4 0.0 collective-permute-done.14.refs_1_
  88.4 0.3 collective-permute-done.15.refs_2_
  88.7 0.0 collective-permute-done.16.refs_3_
  88.7 0.2 join.2
  88.9 4.8 %collective-permute-start.18 = (bf16[64,2048]{1,0:T(8,128)(2,1)S(1)}, bf16[64,2048]{1,0:T(8,128)(2,1)S(1)}, u32[]{:S(2)}, u32[]{:S(2)}) collective-permute-start(bf16[64,2048]{1,0:T(8,128)(2,1)S(1)} %get-tuple-element.58.refs_0_), channel_id=1, source_target_pairs={{0,248},{8,0},{16,8},{24,16},{32,24},{40,32},{48,40},{56,48},{64,5... | collective-permute-start | bytes 786440 | tf_op jit(solution)/shard_map/ppermute | solution.py:389
  93.8 0.3 collective-permute-start.17
  94.0 6.1 %collective-permute-done.23.refs_3_ = bf16[64,3072]{1,0:T(8,128)(2,1)S(1)} collective-permute-done((bf16[64,3072]{1,0:T(8,128)(2,1)S(1)}, bf16[64,3072]{1,0:T(8,128)(2,1)S(1)}, u32[]{:S(2)}, u32[]{:S(2)}) %collective-permute-start.23) | collective-permute-done | bytes 393248 | tf_op jit(solution)/shard_map/ppermute | solution.py:389
  100.2 1.8 %blend.2.refs_5_ = bf16[144,5120]{1,0:T(8,128)(2,1)} custom-call(s32[32]{0:T(128)S(1)} %copy-done.9, bf16[64,3072]{1,0:T(8,128)(2,1)S(1)} %get-tuple-element.66.refs_0_, bf16[16,3072]{1,0:T(8,128)(2,1)S(1)} %get-tuple-element.67.refs_1_, bf16[64,3072]{1,0:T(8,128)(2,1)S(1)} %get-tuple-element.68.refs_2_, ...), custom_call_target="tpu_custom_call" | custom-call | flops 1769472 | bytes 3538944 | tf_op jit(solution)/shard_map/blend/pallas_call | solution.py:366
  102.0 2.5 %collective-permute-done.18.refs_4_ = bf16[64,2048]{1,0:T(8,128)(2,1)S(1)} collective-permute-done((bf16[64,2048]{1,0:T(8,128)(2,1)S(1)}, bf16[64,2048]{1,0:T(8,128)(2,1)S(1)}, u32[]{:S(2)}, u32[]{:S(2)}) %collective-permute-start.18) | collective-permute-done | bytes 262176 | tf_op jit(solution)/shard_map/ppermute | solution.py:389
  104.5 1.6 %blend.3 = bf16[144,5120]{1,0:T(8,128)(2,1)} custom-call(s32[32]{0:T(128)S(1)} %copy-done.9, bf16[64,2048]{1,0:T(8,128)(2,1)S(1)} %get-tuple-element.58.refs_0_, bf16[16,2048]{1,0:T(8,128)(2,1)S(1)} %get-tuple-element.59.refs_1_, bf16[64,2048]{1,0:T(8,128)(2,1)S(1)} %get-tuple-element.60.refs_2_, ...), custom_call_target="tpu_custom_call", output_to_operand_aliasing={{}: (6, {})} | custom-call | flops 1179648 | bytes 2359296 | tf_op jit(solution)/shard_map/blend/pallas_call | solution.py:366
  (21 shorter events, 0.0 us)
Async XLA Ops:
  0.0 9.7 %copy-start.2 = (bf16[1,9,16,5120]{3,2,1,0:T(8,128)(2,1)S(1)}, bf16[1,9,16,5120]{3,2,1,0:T(8,128)(2,1)}, u32[]{:S(2)}) copy-start(bf16[1,9,16,5120]{3,2,1,0:T(8,128)(2,1)} %param.9) | copy-start | bytes 4423684
  0.0 1.5 %copy-start.4 = (bf16[1,9,16,5120]{3,2,1,0:T(8,128)(2,1)S(1)}, bf16[1,9,16,5120]{3,2,1,0:T(8,128)(2,1)}, u32[]{:S(2)}) copy-start(bf16[1,9,16,5120]{3,2,1,0:T(8,128)(2,1)} %param.11) | copy-start | bytes 4423684
  1.5 8.2 %copy-start.7 = (s32[4]{0:T(128)S(1)}, s32[4]{0:T(128)}, u32[]{:S(2)}) copy-start(s32[4]{0:T(128)} %plan_ref.3) | copy-start | bytes 52
  1.5 8.2 %copy-start.8 = (s32[32]{0:T(128)S(1)}, s32[32]{0:T(128)}, u32[]{:S(2)}) copy-start(s32[32]{0:T(128)} %refresh_ref.3) | copy-start | bytes 388
  1.7 14.7 %collective-permute-start = (bf16[144,1280]{1,0:T(8,128)(2,1)S(1)}, bf16[144,1280]{1,0:T(8,128)(2,1)S(1)}, u32[]{:S(2)}, u32[]{:S(2)}) collective-permute-start(bf16[144,1280]{1,0:T(8,128)(2,1)S(1)} %get-tuple-element.41), channel_id=1, source_target_pairs={{0,1},{1,2},{2,3},{3,0},{4,5},{5,6},{6,7},{7,4},{8,9},{9,10},{10,1... | collective-permute-start | bytes 1105928 | tf_op jit(solution)/shard_map/ppermute | solution.py:23
  3.9 12.5 %collective-permute-start.1 = (bf16[144,1280]{1,0:T(8,128)(2,1)S(1)}, bf16[144,1280]{1,0:T(8,128)(2,1)S(1)}, u32[]{:S(2)}, u32[]{:S(2)}) collective-permute-start(bf16[144,1280]{1,0:T(8,128)(2,1)S(1)} %get-tuple-element.42), channel_id=1, source_target_pairs={{0,3},{1,0},{2,1},{3,2},{4,7},{5,4},{6,5},{7,6},{8,11},{9,8},{10,9... | collective-permute-start | bytes 1105928 | tf_op jit(solution)/shard_map/ppermute | solution.py:23
  5.4 17.0 %collective-permute-start.9 = (bf16[144,1280]{1,0:T(8,128)(2,1)S(1)}, bf16[144,1280]{1,0:T(8,128)(2,1)S(1)}, u32[]{:S(2)}, u32[]{:S(2)}) collective-permute-start(bf16[144,1280]{1,0:T(8,128)(2,1)S(1)} %get-tuple-element.52), channel_id=1, source_target_pairs={{0,2},{1,3},{2,0},{3,1},{4,6},{5,7},{6,4},{7,5},{8,10},{9,11},{10,... | collective-permute-start | bytes 1105928 | tf_op jit(solution)/shard_map/ppermute | solution.py:23
  7.0 12.5 %collective-permute-start.2 = (bf16[144,1280]{1,0:T(8,128)(2,1)S(1)}, bf16[144,1280]{1,0:T(8,128)(2,1)S(1)}, u32[]{:S(2)}, u32[]{:S(2)}) collective-permute-start(bf16[144,1280]{1,0:T(8,128)(2,1)S(1)} %get-tuple-element.38.refs_0_.refs_4_), channel_id=1, source_target_pairs={{0,4},{1,5},{2,6},{3,7},{4,0},{5,1},{6,2},{7,3},{8,12},{9,13},{10,... | collective-permute-start | bytes 1105928 | tf_op jit(solution)/shard_map/ppermute | solution.py:33
  9.7 2.7 %copy-start = (bf16[4,1,9,16,5120]{4,3,2,1,0:T(8,128)(2,1)S(1)}, bf16[4,1,9,16,5120]{4,3,2,1,0:T(8,128)(2,1)}, u32[]{:S(2)}) copy-start(bf16[4,1,9,16,5120]{4,3,2,1,0:T(8,128)(2,1)} %param.12) | copy-start | bytes 17694724
  12.4 0.7 copy-start.6
  13.1 14.4 %copy-start.1 = (bf16[4,1,9,16,5120]{4,3,2,1,0:T(8,128)(2,1)S(1)}, bf16[4,1,9,16,5120]{4,3,2,1,0:T(8,128)(2,1)}, u32[]{:S(2)}) copy-start(bf16[4,1,9,16,5120]{4,3,2,1,0:T(8,128)(2,1)} %param.12) | copy-start | bytes 17694724
  16.1 9.9 %collective-permute-start.11 = (bf16[144,1280]{1,0:T(8,128)(2,1)S(1)}, bf16[144,1280]{1,0:T(8,128)(2,1)S(1)}, u32[]{:S(2)}, u32[]{:S(2)}) collective-permute-start(bf16[144,1280]{1,0:T(8,128)(2,1)S(1)} %get-tuple-element.43.refs_2_.refs_12_), channel_id=1, source_target_pairs={{0,4},{1,5},{2,6},{3,7},{4,0},{5,1},{6,2},{7,3},{8,12},{9,13},{10,... | collective-permute-start | bytes 1105928 | tf_op jit(solution)/shard_map/ppermute | solution.py:33
  16.4 17.5 %collective-permute-start.5 = (bf16[144,1280]{1,0:T(8,128)(2,1)S(1)}, bf16[144,1280]{1,0:T(8,128)(2,1)S(1)}, u32[]{:S(2)}, u32[]{:S(2)}) collective-permute-start(bf16[144,1280]{1,0:T(8,128)(2,1)S(1)} %get-tuple-element.44.refs_2_.refs_5_), channel_id=1, source_target_pairs={{0,4},{1,5},{2,6},{3,7},{4,0},{5,1},{6,2},{7,3},{8,12},{9,13},{10,... | collective-permute-start | bytes 1105928 | tf_op jit(solution)/shard_map/ppermute | solution.py:33
  19.2 22.6 %collective-permute-start.10 = (bf16[144,1280]{1,0:T(8,128)(2,1)S(1)}, bf16[144,1280]{1,0:T(8,128)(2,1)S(1)}, u32[]{:S(2)}, u32[]{:S(2)}) collective-permute-start(bf16[144,1280]{1,0:T(8,128)(2,1)S(1)} %get-tuple-element.45.refs_3_.refs_6_), channel_id=1, source_target_pairs={{0,4},{1,5},{2,6},{3,7},{4,0},{5,1},{6,2},{7,3},{8,12},{9,13},{10,... | collective-permute-start | bytes 1105928 | tf_op jit(solution)/shard_map/ppermute | solution.py:33
  19.4 11.0 %collective-permute-start.3 = (bf16[144,1280]{1,0:T(8,128)(2,1)S(1)}, bf16[144,1280]{1,0:T(8,128)(2,1)S(1)}, u32[]{:S(2)}, u32[]{:S(2)}) collective-permute-start(bf16[144,1280]{1,0:T(8,128)(2,1)S(1)} %get-tuple-element.46), channel_id=1, source_target_pairs={{0,1},{1,2},{2,3},{3,0},{4,5},{5,6},{6,7},{7,4},{8,9},{9,10},{10,1... | collective-permute-start | bytes 1105928 | tf_op jit(solution)/shard_map/ppermute | solution.py:23
  22.4 8.1 %collective-permute-start.4 = (bf16[144,1280]{1,0:T(8,128)(2,1)S(1)}, bf16[144,1280]{1,0:T(8,128)(2,1)S(1)}, u32[]{:S(2)}, u32[]{:S(2)}) collective-permute-start(bf16[144,1280]{1,0:T(8,128)(2,1)S(1)} %get-tuple-element.47), channel_id=1, source_target_pairs={{0,3},{1,0},{2,1},{3,2},{4,7},{5,4},{6,5},{7,6},{8,11},{9,8},{10,9... | collective-permute-start | bytes 1105928 | tf_op jit(solution)/shard_map/ppermute | solution.py:23
  26.0 15.8 %collective-permute-start.12 = (bf16[144,1280]{1,0:T(8,128)(2,1)S(1)}, bf16[144,1280]{1,0:T(8,128)(2,1)S(1)}, u32[]{:S(2)}, u32[]{:S(2)}) collective-permute-start(bf16[144,1280]{1,0:T(8,128)(2,1)S(1)} %hold.5), channel_id=1, source_target_pairs={{0,2},{1,3},{2,0},{3,1},{4,6},{5,7},{6,4},{7,5},{8,10},{9,11},{10,... | collective-permute-start | bytes 1105928 | tf_op jit(solution)/shard_map/ppermute | solution.py:23
  41.8 3.0 %copy-start.3 = (bf16[1,9,16,5120]{3,2,1,0:T(8,128)(2,1)S(1)}, bf16[1,9,16,5120]{3,2,1,0:T(8,128)(2,1)}, u32[]{:S(2)}) copy-start(bf16[1,9,16,5120]{3,2,1,0:T(8,128)(2,1)} %param.10) | copy-start | bytes 4423684
  42.1 20.1 %collective-permute-start.19 = (bf16[576,768]{1,0:T(8,128)(2,1)S(1)}, bf16[576,768]{1,0:T(8,128)(2,1)S(1)}, u32[]{:S(2)}, u32[]{:S(2)}) collective-permute-start(bf16[576,768]{1,0:T(8,128)(2,1)S(1)} %stack.3), channel_id=1, source_target_pairs={{0,4},{1,5},{2,6},{3,7},{4,0},{5,1},{6,2},{7,3},{8,12},{9,13},{10,... | collective-permute-start | bytes 2654216 | tf_op jit(solution)/shard_map/ppermute | solution.py:33
  45.0 12.2 %collective-permute-start.6 = (bf16[144,1280]{1,0:T(8,128)(2,1)S(1)}, bf16[144,1280]{1,0:T(8,128)(2,1)S(1)}, u32[]{:S(2)}, u32[]{:S(2)}) collective-permute-start(bf16[144,1280]{1,0:T(8,128)(2,1)S(1)} %get-tuple-element.49), channel_id=1, source_target_pairs={{0,1},{1,2},{2,3},{3,0},{4,5},{5,6},{6,7},{7,4},{8,9},{9,10},{10,1... | collective-permute-start | bytes 1105928 | tf_op jit(solution)/shard_map/ppermute | solution.py:23
  45.4 11.7 %collective-permute-start.7 = (bf16[144,1280]{1,0:T(8,128)(2,1)S(1)}, bf16[144,1280]{1,0:T(8,128)(2,1)S(1)}, u32[]{:S(2)}, u32[]{:S(2)}) collective-permute-start(bf16[144,1280]{1,0:T(8,128)(2,1)S(1)} %get-tuple-element.50), channel_id=1, source_target_pairs={{0,3},{1,0},{2,1},{3,2},{4,7},{5,4},{6,5},{7,6},{8,11},{9,8},{10,9... | collective-permute-start | bytes 1105928 | tf_op jit(solution)/shard_map/ppermute | solution.py:23
  47.7 12.1 %collective-permute-start.8 = (bf16[144,1280]{1,0:T(8,128)(2,1)S(1)}, bf16[144,1280]{1,0:T(8,128)(2,1)S(1)}, u32[]{:S(2)}, u32[]{:S(2)}) collective-permute-start(bf16[144,1280]{1,0:T(8,128)(2,1)S(1)} %get-tuple-element.51), channel_id=1, source_target_pairs={{0,2},{1,3},{2,0},{3,1},{4,6},{5,7},{6,4},{7,5},{8,10},{9,11},{10,... | collective-permute-start | bytes 1105928 | tf_op jit(solution)/shard_map/ppermute | solution.py:23
  47.9 26.9 %collective-permute-start.13 = (bf16[576,512]{1,0:T(8,128)(2,1)S(1)}, bf16[576,512]{1,0:T(8,128)(2,1)S(1)}, u32[]{:S(2)}, u32[]{:S(2)}) collective-permute-start(bf16[576,512]{1,0:T(8,128)(2,1)S(1)} %stack.2), channel_id=1, source_target_pairs={{0,4},{1,5},{2,6},{3,7},{4,0},{5,1},{6,2},{7,3},{8,12},{9,13},{10,... | collective-permute-start | bytes 1769480 | tf_op jit(solution)/shard_map/ppermute | solution.py:33
  68.8 12.0 %collective-permute-start.20 = (bf16[144,768]{1,0:T(8,128)(2,1)S(1)}, bf16[144,768]{1,0:T(8,128)(2,1)S(1)}, u32[]{:S(2)}, u32[]{:S(2)}) collective-permute-start(bf16[144,768]{1,0:T(8,128)(2,1)S(1)} %get-tuple-element.63), channel_id=1, source_target_pairs={{0,3},{1,0},{2,1},{3,2},{4,7},{5,4},{6,5},{7,6},{8,11},{9,8},{10,9... | collective-permute-start | bytes 663560 | tf_op jit(solution)/shard_map/ppermute | solution.py:23
  70.5 11.9 %collective-permute-start.21 = (bf16[144,768]{1,0:T(8,128)(2,1)S(1)}, bf16[144,768]{1,0:T(8,128)(2,1)S(1)}, u32[]{:S(2)}, u32[]{:S(2)}) collective-permute-start(bf16[144,768]{1,0:T(8,128)(2,1)S(1)} %get-tuple-element.64), channel_id=1, source_target_pairs={{0,1},{1,2},{2,3},{3,0},{4,5},{5,6},{6,7},{7,4},{8,9},{9,10},{10,1... | collective-permute-start | bytes 663560 | tf_op jit(solution)/shard_map/ppermute | solution.py:23
  70.5 11.9 %copy-start.5 = (f32[5120]{0:T(1024)S(1)}, f32[5120]{0:T(1024)}, u32[]{:S(2)}) copy-start(f32[5120]{0:T(1024)} %param.16) | copy-start | bytes 61444
  70.5 11.9 %collective-permute-start.22 = (bf16[144,768]{1,0:T(8,128)(2,1)S(1)}, bf16[144,768]{1,0:T(8,128)(2,1)S(1)}, u32[]{:S(2)}, u32[]{:S(2)}) collective-permute-start(bf16[144,768]{1,0:T(8,128)(2,1)S(1)} %get-tuple-element.65), channel_id=1, source_target_pairs={{0,2},{1,3},{2,0},{3,1},{4,6},{5,7},{6,4},{7,5},{8,10},{9,11},{10,... | collective-permute-start | bytes 663560 | tf_op jit(solution)/shard_map/ppermute | solution.py:23
  79.3 9.2 %collective-permute-start.14 = (bf16[144,512]{1,0:T(8,128)(2,1)S(1)}, bf16[144,512]{1,0:T(8,128)(2,1)S(1)}, u32[]{:S(2)}, u32[]{:S(2)}) collective-permute-start(bf16[144,512]{1,0:T(8,128)(2,1)S(1)} %get-tuple-element.55), channel_id=1, source_target_pairs={{0,3},{1,0},{2,1},{3,2},{4,7},{5,4},{6,5},{7,6},{8,11},{9,8},{10,9... | collective-permute-start | bytes 442376 | tf_op jit(solution)/shard_map/ppermute | solution.py:23
  80.0 8.7 %collective-permute-start.15 = (bf16[144,512]{1,0:T(8,128)(2,1)S(1)}, bf16[144,512]{1,0:T(8,128)(2,1)S(1)}, u32[]{:S(2)}, u32[]{:S(2)}) collective-permute-start(bf16[144,512]{1,0:T(8,128)(2,1)S(1)} %get-tuple-element.56), channel_id=1, source_target_pairs={{0,1},{1,2},{2,3},{3,0},{4,5},{5,6},{6,7},{7,4},{8,9},{9,10},{10,1... | collective-permute-start | bytes 442376 | tf_op jit(solution)/shard_map/ppermute | solution.py:23
  80.8 7.9 %collective-permute-start.16 = (bf16[144,512]{1,0:T(8,128)(2,1)S(1)}, bf16[144,512]{1,0:T(8,128)(2,1)S(1)}, u32[]{:S(2)}, u32[]{:S(2)}) collective-permute-start(bf16[144,512]{1,0:T(8,128)(2,1)S(1)} %get-tuple-element.57), channel_id=1, source_target_pairs={{0,2},{1,3},{2,0},{3,1},{4,6},{5,7},{6,4},{7,5},{8,10},{9,11},{10,... | collective-permute-start | bytes 442376 | tf_op jit(solution)/shard_map/ppermute | solution.py:23
  82.6 17.5 %copy-start.9 = (s32[32]{0:T(128)S(1)}, s32[32]{0:T(128)}, u32[]{:S(2)}) copy-start(s32[32]{0:T(128)} %overlaps_ref.3) | copy-start | bytes 388
  82.7 11.4 %collective-permute-start.24 = (bf16[64,3072]{1,0:T(8,128)(2,1)S(1)}, bf16[64,3072]{1,0:T(8,128)(2,1)S(1)}, u32[]{:S(2)}, u32[]{:S(2)}) collective-permute-start(bf16[64,3072]{1,0:T(8,128)(2,1)S(1)} %get-tuple-element.66.refs_0_), channel_id=1, source_target_pairs={{0,248},{8,0},{16,8},{24,16},{32,24},{40,32},{48,40},{56,48},{64,5... | collective-permute-start | bytes 1179656 | tf_op jit(solution)/shard_map/ppermute | solution.py:389
  88.1 12.0 %collective-permute-start.23 = (bf16[64,3072]{1,0:T(8,128)(2,1)S(1)}, bf16[64,3072]{1,0:T(8,128)(2,1)S(1)}, u32[]{:S(2)}, u32[]{:S(2)}) collective-permute-start(bf16[64,3072]{1,0:T(8,128)(2,1)S(1)} %get-tuple-element.68.refs_2_), channel_id=1, source_target_pairs={{0,8},{8,16},{16,24},{24,32},{32,40},{40,48},{48,56},{56,64},{64,7... | collective-permute-start | bytes 1179656 | tf_op jit(solution)/shard_map/ppermute | solution.py:389
  88.9 15.6 %collective-permute-start.18 = (bf16[64,2048]{1,0:T(8,128)(2,1)S(1)}, bf16[64,2048]{1,0:T(8,128)(2,1)S(1)}, u32[]{:S(2)}, u32[]{:S(2)}) collective-permute-start(bf16[64,2048]{1,0:T(8,128)(2,1)S(1)} %get-tuple-element.58.refs_0_), channel_id=1, source_target_pairs={{0,248},{8,0},{16,8},{24,16},{32,24},{40,32},{48,40},{56,48},{64,5... | collective-permute-start | bytes 786440 | tf_op jit(solution)/shard_map/ppermute | solution.py:389
  93.8 10.8 %collective-permute-start.17 = (bf16[64,2048]{1,0:T(8,128)(2,1)S(1)}, bf16[64,2048]{1,0:T(8,128)(2,1)S(1)}, u32[]{:S(2)}, u32[]{:S(2)}) collective-permute-start(bf16[64,2048]{1,0:T(8,128)(2,1)S(1)} %get-tuple-element.60.refs_2_), channel_id=1, source_target_pairs={{0,8},{8,16},{16,24},{24,32},{32,40},{40,48},{48,56},{56,64},{64,7... | collective-permute-start | bytes 786440 | tf_op jit(solution)/shard_map/ppermute | solution.py:389

commit v2 on v1

--- a/solution.py
+++ b/solution.py
@@ -405,31 +405,36 @@
     gate = attn_gate.reshape(1, width)
     latents, cached = latents[0], cached[:, 0]
     attn_keys = attn_keys.reshape(rows, width)
-    packed = pack(attn_keys, wide, MOVES)
+    packed = [*pack(attn_keys, wide, MOVES[:1])]
+    packed += pack(attn_keys, wide, MOVES[1:], packed)
     value, *values = prepare(
         latents, cached, plan, refresh, value_gain.reshape(1, width), wide, packed[:1]
     )
     far_keys = [across(packed[0])]
     keys = spread(packed, send)
+    far_value = across(value)
     keys[1:3] = hold(keys[1:3], (value,))
-    far_value = across(value)
     far_keys += [across(key) for key in keys[1:3]]
-    near = hold(values[:2], (*keys[1:3], far_keys[0]))
-    values = spread([value, *near, *hold(values[2:], (keys[3], far_value))], send)
-    asked = spread(pack(queries, wide, MOVES, (*values[1:3], far_keys[1])), send)
+    values[:2] = hold(values[:2], (keys[1], far_keys[0]))
+    values[2:] = hold(values[2:], (far_value,))
+    values = spread([value, *values], send)
+    asked = spread(pack(queries, wide, MOVES, (*values[1:3], *far_keys[1:2])), send)
     laters = add(latents, cached, plan, refresh, wide, parts)
     moved = [keys[3], *values[1:]]
-    afters = ((*far_keys[1:], far_value, *laters), ())
+    sends = [
+        (
+            across(stack(moved[:1], skips[0], parts[0], (far_keys[1], far_value, *laters))),
+            across(stack(moved[1:], skips[0], parts[0], far_keys[2:])),
+        ),
+        *((across(stack(moved, skip, take, asked[1:2])),) for skip, take in zip(skips[1:], parts[1:])),
+    ]
     rests = [
-        across(stack(moved, skip, take, after))
-        for skip, take, after in zip(skips, parts, afters)
+        [(rest, row, 0) for rest in sent for row in range(0, rest.shape[0], rows)] for sent in sends
     ]
     out = None
     for later, rest, skip, take in zip(laters, rests, skips, parts):
-        key_places = [(key, 0, skip) for key in keys + far_keys] + [(rest, 0, 0)]
-        value_places = [(value, 0, skip) for value in [*values, far_value]] + [
-            (rest, i * rows, 0) for i in (1, 2, 3)
-        ]
+        key_places = [(key, 0, skip) for key in keys + far_keys] + rest[:1]
+        value_places = [(value, 0, skip) for value in [*values, far_value]] + rest[1:]
         attended = spread(attend(asked, key_places, value_places, skip, take), send_back)
         first, middle, last = join(later, gate, attended, frames, wide, skip)
         from_prev = shift(last, 1)

time: 107 us -> 104 us (0.972)
  waiting for transfers between devices: 41.6 us -> 39.9 us
    ppermute x15, waiting for transfers between devices: 13.5 us -> 10.1 us  [send(): return lax.ppermute(value, 'token', pairs)]
    ppermute x6 -> x7, starting transfers between devices: 10 us -> 7.03 us  [across(): return lax.ppermute(value, 'token', pairs)]
    ppermute x15, starting transfers between devices: 17 us -> 19.1 us  [send(): return lax.ppermute(value, 'token', pairs)]
    ppermute x4, waiting for transfers between devices: 8.61 us -> 10.2 us  [shift(): return lax.ppermute(value, 'window', pairs)]
    unnamed x20 -> x22, local copies, waits for them, and re-layouts: 4.91 us -> 4.08 us
    ppermute x6 -> x7, waiting for transfers between devices: 19.5 us -> 19.6 us  [across(): return lax.ppermute(value, 'token', pairs)]
  transfers between devices with their start and end apart: 25 -> 26, of which waited for: 11 -> 10; matrix products, arithmetic and copies ran while one was open for 0% -> 0% of each run, Pallas kernels for 18% -> 19%
where the time goes in v2:
time: 104 us
  waiting for transfers between devices  39.9 us (38%)
  starting transfers between devices  38 us (37%)
  Pallas kernels  22 us (21%)
  local copies, waits for them, and re-layouts  4.08 us (4%)
    ppermute x7, waiting for transfers between devices, across(): return lax.ppermute(value, 'token', pairs)  19.6 us
    ppermute x15, starting transfers between devices, send(): return lax.ppermute(value, 'token', pairs)  19.1 us
    ppermute x4, starting transfers between devices, shift(): return lax.ppermute(value, 'window', pairs)  11.9 us
    pallas_call x2, Pallas kernels, attend(): pl.pallas_call(body, name='attend', out_shape=[jax.ShapeDtypeStruct((rows...  11 us
    ppermute x4, waiting for transfers between devices, shift(): return lax.ppermute(value, 'window', pairs)  10.2 us
    ppermute x15, waiting for transfers between devices, send(): return lax.ppermute(value, 'token', pairs)  10.1 us
    ppermute x7, starting transfers between devices, across(): return lax.ppermute(value, 'token', pairs)  7.03 us
    unnamed x22, local copies, waits for them, and re-layouts  4.08 us
  transfers between devices with their start and end apart: 26, of which 10 were waited for; matrix products, arithmetic and copies ran while one was open for 0% of the time, Pallas kernels for 19%

profile of v2, /device:TPU:1, one launch (start us, length us, event | category | flops | bytes accessed | tf_op | source)
XLA Modules:
  0.0 104.3 jit_solution(9435041905996795265)
XLA Ops:
  0.0 1.4 %copy-done.1 = bf16[1,9,16,5120]{3,2,1,0:T(8,128)(2,1)S(1)} copy-done((bf16[1,9,16,5120]{3,2,1,0:T(8,128)(2,1)S(1)}, bf16[1,9,16,5120]{3,2,1,0:T(8,128)(2,1)}, u32[]{:S(2)}) %copy-start.1) | copy-done | bytes 1474584
  1.4 0.1 pack.3.refs_0_.refs_4_
  1.4 3.7 %collective-permute-start.2 = (bf16[144,1280]{1,0:T(8,128)(2,1)S(1)}, bf16[144,1280]{1,0:T(8,128)(2,1)S(1)}, u32[]{:S(2)}, u32[]{:S(2)}) collective-permute-start(bf16[144,1280]{1,0:T(8,128)(2,1)S(1)} %pack.3.refs_0_.refs_4_), channel_id=1, source_target_pairs={{0,4},{1,5},{2,6},{3,7},{4,0},{5,1},{6,2},{7,3},{8,12},{9,13},{10,... | collective-permute-start | bytes 1105928 | tf_op jit(solution)/shard_map/ppermute | solution.py:33
  5.1 0.1 pack.4
  5.2 1.4 %collective-permute-start = (bf16[144,1280]{1,0:T(8,128)(2,1)S(1)}, bf16[144,1280]{1,0:T(8,128)(2,1)S(1)}, u32[]{:S(2)}, u32[]{:S(2)}) collective-permute-start(bf16[144,1280]{1,0:T(8,128)(2,1)S(1)} %get-tuple-element.39), channel_id=1, source_target_pairs={{0,1},{1,2},{2,3},{3,0},{4,5},{5,6},{6,7},{7,4},{8,9},{9,10},{10,1... | collective-permute-start | bytes 1105928 | tf_op jit(solution)/shard_map/ppermute | solution.py:23
  6.6 1.5 %collective-permute-start.1 = (bf16[144,1280]{1,0:T(8,128)(2,1)S(1)}, bf16[144,1280]{1,0:T(8,128)(2,1)S(1)}, u32[]{:S(2)}, u32[]{:S(2)}) collective-permute-start(bf16[144,1280]{1,0:T(8,128)(2,1)S(1)} %get-tuple-element.40), channel_id=1, source_target_pairs={{0,3},{1,0},{2,1},{3,2},{4,7},{5,4},{6,5},{7,6},{8,11},{9,8},{10,9... | collective-permute-start | bytes 1105928 | tf_op jit(solution)/shard_map/ppermute | solution.py:23
  8.2 0.0 copy-start
  8.2 2.7 %copy-done = bf16[4,1,9,16,5120]{4,3,2,1,0:T(8,128)(2,1)S(1)} copy-done((bf16[4,1,9,16,5120]{4,3,2,1,0:T(8,128)(2,1)S(1)}, bf16[4,1,9,16,5120]{4,3,2,1,0:T(8,128)(2,1)}, u32[]{:S(2)}) %copy-start) | copy-done | bytes 5898264
  10.8 3.0 %prepare.1 = (bf16[144,1280]{1,0:T(8,128)(2,1)S(1)}, bf16[144,1280]{1,0:T(8,128)(2,1)S(1)}, bf16[144,1280]{1,0:T(8,128)(2,1)S(1)}, bf16[144,1280]{1,0:T(8,128)(2,1)S(1)}) custom-call(s32[4]{0:T(128)S(1)} %copy-done.6, s32[32]{0:T(128)S(1)} %copy-done.7, bf16[9,16,5120]{2,1,0:T(8,128)(2,1)S(1)} %bitcast.13, bf16[4,9,16,5120]{3,2,1,0:T(8,128)(2,1)S(1)} %bitcast.7, ...), custom_call_target="tpu_custom_call" | custom-call | flops 14745600 | bytes 8847360 | tf_op jit(solution)/shard_map/prepare/pallas_call | solution.py:164
  13.8 0.0 slice-start.1
  13.8 0.3 collective-permute-start.11
  14.2 1.6 %collective-permute-done.refs_0_ = bf16[144,1280]{1,0:T(8,128)(2,1)S(1)} collective-permute-done((bf16[144,1280]{1,0:T(8,128)(2,1)S(1)}, bf16[144,1280]{1,0:T(8,128)(2,1)S(1)}, u32[]{:S(2)}, u32[]{:S(2)}) %collective-permute-start) | collective-permute-done | bytes 368672 | tf_op jit(solution)/shard_map/ppermute | solution.py:23
  15.8 0.0 collective-permute-done.1.refs_1_
  15.8 0.0 collective-permute-done.2.refs_3_.refs_8_
  15.8 0.9 collective-permute-start.3
  16.8 1.8 %collective-permute-start.4 = (bf16[144,1280]{1,0:T(8,128)(2,1)S(1)}, bf16[144,1280]{1,0:T(8,128)(2,1)S(1)}, u32[]{:S(2)}, u32[]{:S(2)}) collective-permute-start(bf16[144,1280]{1,0:T(8,128)(2,1)S(1)} %get-tuple-element.44), channel_id=1, source_target_pairs={{0,3},{1,0},{2,1},{3,2},{4,7},{5,4},{6,5},{7,6},{8,11},{9,8},{10,9... | collective-permute-start | bytes 1105928 | tf_op jit(solution)/shard_map/ppermute | solution.py:23
  18.6 1.1 %collective-permute-start.10 = (bf16[144,1280]{1,0:T(8,128)(2,1)S(1)}, bf16[144,1280]{1,0:T(8,128)(2,1)S(1)}, u32[]{:S(2)}, u32[]{:S(2)}) collective-permute-start(bf16[144,1280]{1,0:T(8,128)(2,1)S(1)} %get-tuple-element.49.refs_6_), channel_id=1, source_target_pairs={{0,4},{1,5},{2,6},{3,7},{4,0},{5,1},{6,2},{7,3},{8,12},{9,13},{10,... | collective-permute-start | bytes 1105928 | tf_op jit(solution)/shard_map/ppermute | solution.py:33
  19.7 4.5 %collective-permute-done.11.refs_1_.refs_16_.refs_2_ = bf16[144,1280]{1,0:T(8,128)(2,1)S(1)} collective-permute-done((bf16[144,1280]{1,0:T(8,128)(2,1)S(1)}, bf16[144,1280]{1,0:T(8,128)(2,1)S(1)}, u32[]{:S(2)}, u32[]{:S(2)}) %collective-permute-start.11) | collective-permute-done | bytes 368672 | tf_op jit(solution)/shard_map/ppermute | solution.py:33
  24.1 1.4 %collective-permute-start.12 = (bf16[144,1280]{1,0:T(8,128)(2,1)S(1)}, bf16[144,1280]{1,0:T(8,128)(2,1)S(1)}, u32[]{:S(2)}, u32[]{:S(2)}) collective-permute-start(bf16[144,1280]{1,0:T(8,128)(2,1)S(1)} %hold.5), channel_id=1, source_target_pairs={{0,2},{1,3},{2,0},{3,1},{4,6},{5,7},{6,4},{7,5},{8,10},{9,11},{10,... | collective-permute-start | bytes 1105928 | tf_op jit(solution)/shard_map/ppermute | solution.py:23
  25.5 0.7 collective-permute-start.5
  26.2 0.0 collective-permute-done.3.refs_0_.refs_1_.refs_13_
  26.2 0.0 collective-permute-done.4.refs_1_.refs_2_.refs_14_
  26.2 5.8 %collective-permute-done.10.refs_10_.refs_3_ = bf16[144,1280]{1,0:T(8,128)(2,1)S(1)} collective-permute-done((bf16[144,1280]{1,0:T(8,128)(2,1)S(1)}, bf16[144,1280]{1,0:T(8,128)(2,1)S(1)}, u32[]{:S(2)}, u32[]{:S(2)}) %collective-permute-start.10) | collective-permute-done | bytes 368672 | tf_op jit(solution)/shard_map/ppermute | solution.py:33
  32.0 0.6 collective-permute-done.12.refs_3_.refs_15_.refs_2_
  32.6 0.3 stack.5
  32.9 0.2 collective-permute-start.20
  33.2 1.6 %collective-permute-start.9 = (bf16[144,1280]{1,0:T(8,128)(2,1)S(1)}, bf16[144,1280]{1,0:T(8,128)(2,1)S(1)}, u32[]{:S(2)}, u32[]{:S(2)}) collective-permute-start(bf16[144,1280]{1,0:T(8,128)(2,1)S(1)} %get-tuple-element.50), channel_id=1, source_target_pairs={{0,2},{1,3},{2,0},{3,1},{4,6},{5,7},{6,4},{7,5},{8,10},{9,11},{10,... | collective-permute-start | bytes 1105928 | tf_op jit(solution)/shard_map/ppermute | solution.py:23
  34.8 5.2 %collective-permute-done.5.refs_2_.refs_9_.refs_1_ = bf16[144,1280]{1,0:T(8,128)(2,1)S(1)} collective-permute-done((bf16[144,1280]{1,0:T(8,128)(2,1)S(1)}, bf16[144,1280]{1,0:T(8,128)(2,1)S(1)}, u32[]{:S(2)}, u32[]{:S(2)}) %collective-permute-start.5) | collective-permute-done | bytes 368672 | tf_op jit(solution)/shard_map/ppermute | solution.py:33
  39.9 0.2 pack.5
  40.1 0.1 collective-permute-start.6
  40.2 2.7 %collective-permute-start.7 = (bf16[144,1280]{1,0:T(8,128)(2,1)S(1)}, bf16[144,1280]{1,0:T(8,128)(2,1)S(1)}, u32[]{:S(2)}, u32[]{:S(2)}) collective-permute-start(bf16[144,1280]{1,0:T(8,128)(2,1)S(1)} %get-tuple-element.47), channel_id=1, source_target_pairs={{0,3},{1,0},{2,1},{3,2},{4,7},{5,4},{6,5},{7,6},{8,11},{9,8},{10,9... | collective-permute-start | bytes 1105928 | tf_op jit(solution)/shard_map/ppermute | solution.py:23
  42.9 0.2 collective-permute-start.8
  43.1 2.9 %add.1 = (f32[144,3072]{1,0:T(8,128)S(1)}, f32[144,2048]{1,0:T(8,128)S(1)}) custom-call(s32[4]{0:T(128)S(1)} %copy-done.6, s32[32]{0:T(128)S(1)} %copy-done.7, bf16[9,16,5120]{2,1,0:T(8,128)(2,1)S(1)} %bitcast.14, bf16[4,9,16,5120]{3,2,1,0:T(8,128)(2,1)S(1)} %bitcast.10), custom_call_target="tpu_custom_call" | custom-call | flops 7372800 | bytes 10321920 | tf_op jit(solution)/shard_map/add/pallas_call | solution.py:207
  46.0 0.0 collective-permute-done.9.refs_0_.refs_7_
  46.0 0.3 stack.4
  46.3 0.8 collective-permute-start.19
  47.1 7.2 %collective-permute-done.6.refs_4_.refs_1_ = bf16[144,1280]{1,0:T(8,128)(2,1)S(1)} collective-permute-done((bf16[144,1280]{1,0:T(8,128)(2,1)S(1)}, bf16[144,1280]{1,0:T(8,128)(2,1)S(1)}, u32[]{:S(2)}, u32[]{:S(2)}) %collective-permute-start.6) | collective-permute-done | bytes 368672 | tf_op jit(solution)/shard_map/ppermute | solution.py:23
  54.3 0.2 stack.3
  54.5 0.3 collective-permute-start.13
  54.8 4.1 %collective-permute-done.19.refs_11_ = bf16[144,768]{1,0:T(8,128)(2,1)S(1)} collective-permute-done((bf16[144,768]{1,0:T(8,128)(2,1)S(1)}, bf16[144,768]{1,0:T(8,128)(2,1)S(1)}, u32[]{:S(2)}, u32[]{:S(2)}) %collective-permute-start.19) | collective-permute-done | bytes 221216 | tf_op jit(solution)/shard_map/ppermute | solution.py:33
  58.9 0.0 collective-permute-done.7.refs_2_
  58.9 0.7 collective-permute-done.8.refs_3_
  59.6 0.0 collective-permute-done.20.refs_17_
  59.6 6.6 %attend.3 = (bf16[144,768]{1,0:T(8,128)(2,1)S(1)}, bf16[144,768]{1,0:T(8,128)(2,1)S(1)}, bf16[144,768]{1,0:T(8,128)(2,1)S(1)}, bf16[144,768]{1,0:T(8,128)(2,1)S(1)}) custom-call(bf16[144,1280]{1,0:T(8,128)(2,1)S(1)} %get-tuple-element.45.refs_0_, bf16[144,1280]{1,0:T(8,128)(2,1)S(1)} %collective-permute-done.6.refs_4_.refs_1_, ...), custom_call_target="tpu_custom_call" | custom-call | flops 4076863488 | bytes 10616832 | tf_op jit(solution)/shard_map/attend/pallas_call | solution.py:270
  66.2 1.7 %collective-permute-start.21 = (bf16[144,768]{1,0:T(8,128)(2,1)S(1)}, bf16[144,768]{1,0:T(8,128)(2,1)S(1)}, u32[]{:S(2)}, u32[]{:S(2)}) collective-permute-start(bf16[144,768]{1,0:T(8,128)(2,1)S(1)} %get-tuple-element.61), channel_id=1, source_target_pairs={{0,3},{1,0},{2,1},{3,2},{4,7},{5,4},{6,5},{7,6},{8,11},{9,8},{10,9... | collective-permute-start | bytes 663560 | tf_op jit(solution)/shard_map/ppermute | solution.py:23
  67.9 0.0 collective-permute-start.22
  67.9 1.3 %collective-permute-start.23 = (bf16[144,768]{1,0:T(8,128)(2,1)S(1)}, bf16[144,768]{1,0:T(8,128)(2,1)S(1)}, u32[]{:S(2)}, u32[]{:S(2)}) collective-permute-start(bf16[144,768]{1,0:T(8,128)(2,1)S(1)} %get-tuple-element.63), channel_id=1, source_target_pairs={{0,2},{1,3},{2,0},{3,1},{4,6},{5,7},{6,4},{7,5},{8,10},{9,11},{10,... | collective-permute-start | bytes 663560 | tf_op jit(solution)/shard_map/ppermute | solution.py:23
  69.2 0.0 collective-permute-done.13.refs_11_
  69.2 4.4 %attend.2 = (bf16[144,512]{1,0:T(8,128)(2,1)S(1)}, bf16[144,512]{1,0:T(8,128)(2,1)S(1)}, bf16[144,512]{1,0:T(8,128)(2,1)S(1)}, bf16[144,512]{1,0:T(8,128)(2,1)S(1)}) custom-call(bf16[144,1280]{1,0:T(8,128)(2,1)S(1)} %get-tuple-element.45.refs_0_, bf16[144,1280]{1,0:T(8,128)(2,1)S(1)} %collective-permute-done.6.refs_4_.refs_1_, ...), custom_call_target="tpu_custom_call" | custom-call | flops 2717908992 | bytes 7077888 | tf_op jit(solution)/shard_map/attend/pallas_call | solution.py:270
  73.6 3.3 %collective-permute-start.14 = (bf16[144,512]{1,0:T(8,128)(2,1)S(1)}, bf16[144,512]{1,0:T(8,128)(2,1)S(1)}, u32[]{:S(2)}, u32[]{:S(2)}) collective-permute-start(bf16[144,512]{1,0:T(8,128)(2,1)S(1)} %get-tuple-element.53), channel_id=1, source_target_pairs={{0,3},{1,0},{2,1},{3,2},{4,7},{5,4},{6,5},{7,6},{8,11},{9,8},{10,9... | collective-permute-start | bytes 442376 | tf_op jit(solution)/shard_map/ppermute | solution.py:23
  76.8 0.0 collective-permute-start.15
  76.8 0.0 collective-permute-done.21.refs_1_
  76.8 1.3 %collective-permute-start.16 = (bf16[144,512]{1,0:T(8,128)(2,1)S(1)}, bf16[144,512]{1,0:T(8,128)(2,1)S(1)}, u32[]{:S(2)}, u32[]{:S(2)}) collective-permute-start(bf16[144,512]{1,0:T(8,128)(2,1)S(1)} %get-tuple-element.55), channel_id=1, source_target_pairs={{0,2},{1,3},{2,0},{3,1},{4,6},{5,7},{6,4},{7,5},{8,10},{9,11},{10,... | collective-permute-start | bytes 442376 | tf_op jit(solution)/shard_map/ppermute | solution.py:23
  78.1 0.0 collective-permute-done.22.refs_2_
  78.1 0.2 join.3
  78.4 0.0 copy-start.8
  78.4 7.1 %collective-permute-start.24 = (bf16[64,3072]{1,0:T(8,128)(2,1)S(1)}, bf16[64,3072]{1,0:T(8,128)(2,1)S(1)}, u32[]{:S(2)}, u32[]{:S(2)}) collective-permute-start(bf16[64,3072]{1,0:T(8,128)(2,1)S(1)} %get-tuple-element.66.refs_2_), channel_id=1, source_target_pairs={{0,8},{8,16},{16,24},{24,32},{32,40},{40,48},{48,56},{56,64},{64,7... | collective-permute-start | bytes 1179656 | tf_op jit(solution)/shard_map/ppermute | solution.py:389
  85.5 0.0 collective-permute-done.16.refs_3_
  85.5 0.2 join.2
  85.7 4.8 %collective-permute-start.17 = (bf16[64,2048]{1,0:T(8,128)(2,1)S(1)}, bf16[64,2048]{1,0:T(8,128)(2,1)S(1)}, u32[]{:S(2)}, u32[]{:S(2)}) collective-permute-start(bf16[64,2048]{1,0:T(8,128)(2,1)S(1)} %get-tuple-element.58.refs_2_), channel_id=1, source_target_pairs={{0,8},{8,16},{16,24},{24,32},{32,40},{40,48},{48,56},{56,64},{64,7... | collective-permute-start | bytes 786440 | tf_op jit(solution)/shard_map/ppermute | solution.py:389
  90.5 9.2 %collective-permute-done.25.refs_4_ = bf16[64,3072]{1,0:T(8,128)(2,1)S(1)} collective-permute-done((bf16[64,3072]{1,0:T(8,128)(2,1)S(1)}, bf16[64,3072]{1,0:T(8,128)(2,1)S(1)}, u32[]{:S(2)}, u32[]{:S(2)}) %collective-permute-start.25) | collective-permute-done | bytes 393248 | tf_op jit(solution)/shard_map/ppermute | solution.py:389
  99.7 1.8 %blend.2.refs_5_ = bf16[144,5120]{1,0:T(8,128)(2,1)} custom-call(s32[32]{0:T(128)S(1)} %copy-done.8, bf16[64,3072]{1,0:T(8,128)(2,1)S(1)} %get-tuple-element.64.refs_0_, bf16[16,3072]{1,0:T(8,128)(2,1)S(1)} %get-tuple-element.65.refs_1_, bf16[64,3072]{1,0:T(8,128)(2,1)S(1)} %get-tuple-element.66.refs_2_, ...), custom_call_target="tpu_custom_call" | custom-call | flops 1769472 | bytes 3538944 | tf_op jit(solution)/shard_map/blend/pallas_call | solution.py:366
  101.6 0.9 collective-permute-done.18.refs_4_
  102.5 1.6 %blend.3 = bf16[144,5120]{1,0:T(8,128)(2,1)} custom-call(s32[32]{0:T(128)S(1)} %copy-done.8, bf16[64,2048]{1,0:T(8,128)(2,1)S(1)} %get-tuple-element.56.refs_0_, bf16[16,2048]{1,0:T(8,128)(2,1)S(1)} %get-tuple-element.57.refs_1_, bf16[64,2048]{1,0:T(8,128)(2,1)S(1)} %get-tuple-element.58.refs_2_, ...), custom_call_target="tpu_custom_call", output_to_operand_aliasing={{}: (6, {})} | custom-call | flops 1179648 | bytes 2359296 | tf_op jit(solution)/shard_map/blend/pallas_call | solution.py:366
  (28 shorter events, 0.1 us)
Async XLA Ops:
  0.0 1.4 %copy-start.1 = (bf16[1,9,16,5120]{3,2,1,0:T(8,128)(2,1)S(1)}, bf16[1,9,16,5120]{3,2,1,0:T(8,128)(2,1)}, u32[]{:S(2)}) copy-start(bf16[1,9,16,5120]{3,2,1,0:T(8,128)(2,1)} %param.11) | copy-start | bytes 4423684
  1.4 6.8 %copy-start.2 = (bf16[1,9,16,5120]{3,2,1,0:T(8,128)(2,1)S(1)}, bf16[1,9,16,5120]{3,2,1,0:T(8,128)(2,1)}, u32[]{:S(2)}) copy-start(bf16[1,9,16,5120]{3,2,1,0:T(8,128)(2,1)} %param.9) | copy-start | bytes 4423684
  1.4 6.8 %copy-start.5 = (f32[5120]{0:T(1024)S(1)}, f32[5120]{0:T(1024)}, u32[]{:S(2)}) copy-start(f32[5120]{0:T(1024)} %param.15) | copy-start | bytes 61444
  1.4 6.8 %copy-start.6 = (s32[4]{0:T(128)S(1)}, s32[4]{0:T(128)}, u32[]{:S(2)}) copy-start(s32[4]{0:T(128)} %plan_ref.3) | copy-start | bytes 52
  1.4 6.8 %copy-start.7 = (s32[32]{0:T(128)S(1)}, s32[32]{0:T(128)}, u32[]{:S(2)}) copy-start(s32[32]{0:T(128)} %refresh_ref.3) | copy-start | bytes 388
  1.4 14.4 %collective-permute-start.2 = (bf16[144,1280]{1,0:T(8,128)(2,1)S(1)}, bf16[144,1280]{1,0:T(8,128)(2,1)S(1)}, u32[]{:S(2)}, u32[]{:S(2)}) collective-permute-start(bf16[144,1280]{1,0:T(8,128)(2,1)S(1)} %pack.3.refs_0_.refs_4_), channel_id=1, source_target_pairs={{0,4},{1,5},{2,6},{3,7},{4,0},{5,1},{6,2},{7,3},{8,12},{9,13},{10,... | collective-permute-start | bytes 1105928 | tf_op jit(solution)/shard_map/ppermute | solution.py:33
  5.2 10.6 %collective-permute-start = (bf16[144,1280]{1,0:T(8,128)(2,1)S(1)}, bf16[144,1280]{1,0:T(8,128)(2,1)S(1)}, u32[]{:S(2)}, u32[]{:S(2)}) collective-permute-start(bf16[144,1280]{1,0:T(8,128)(2,1)S(1)} %get-tuple-element.39), channel_id=1, source_target_pairs={{0,1},{1,2},{2,3},{3,0},{4,5},{5,6},{6,7},{7,4},{8,9},{9,10},{10,1... | collective-permute-start | bytes 1105928 | tf_op jit(solution)/shard_map/ppermute | solution.py:23
  6.6 9.2 %collective-permute-start.1 = (bf16[144,1280]{1,0:T(8,128)(2,1)S(1)}, bf16[144,1280]{1,0:T(8,128)(2,1)S(1)}, u32[]{:S(2)}, u32[]{:S(2)}) collective-permute-start(bf16[144,1280]{1,0:T(8,128)(2,1)S(1)} %get-tuple-element.40), channel_id=1, source_target_pairs={{0,3},{1,0},{2,1},{3,2},{4,7},{5,4},{6,5},{7,6},{8,11},{9,8},{10,9... | collective-permute-start | bytes 1105928 | tf_op jit(solution)/shard_map/ppermute | solution.py:23
  8.2 2.7 %copy-start = (bf16[4,1,9,16,5120]{4,3,2,1,0:T(8,128)(2,1)S(1)}, bf16[4,1,9,16,5120]{4,3,2,1,0:T(8,128)(2,1)}, u32[]{:S(2)}) copy-start(bf16[4,1,9,16,5120]{4,3,2,1,0:T(8,128)(2,1)} %param.12) | copy-start | bytes 17694724
  10.8 32.2 %slice-start = ((s8[5898240]{0:T(1024)(128)(4,1)}), s8[4194304]{0:T(1024)(128)(4,1)S(1)}, s32[]{:S(2)}) async-start(s8[5898240]{0:T(1024)(128)(4,1)} %bitcast.8), calls=%async_computation | async-start | bytes 8388608
  13.8 29.2 %slice-start.1 = ((s8[5898240]{0:T(1024)(128)(4,1)}), s8[1703936]{0:T(1024)(128)(4,1)S(1)}, s32[]{:S(2)}) async-start(s8[5898240]{0:T(1024)(128)(4,1)} %bitcast.8), calls=%async_computation.1 | async-start | bytes 3407872
  13.8 10.3 %collective-permute-start.11 = (bf16[144,1280]{1,0:T(8,128)(2,1)S(1)}, bf16[144,1280]{1,0:T(8,128)(2,1)S(1)}, u32[]{:S(2)}, u32[]{:S(2)}) collective-permute-start(bf16[144,1280]{1,0:T(8,128)(2,1)S(1)} %get-tuple-element.41.refs_2_.refs_12_), channel_id=1, source_target_pairs={{0,4},{1,5},{2,6},{3,7},{4,0},{5,1},{6,2},{7,3},{8,12},{9,13},{10,... | collective-permute-start | bytes 1105928 | tf_op jit(solution)/shard_map/ppermute | solution.py:33
  15.8 10.4 %collective-permute-start.3 = (bf16[144,1280]{1,0:T(8,128)(2,1)S(1)}, bf16[144,1280]{1,0:T(8,128)(2,1)S(1)}, u32[]{:S(2)}, u32[]{:S(2)}) collective-permute-start(bf16[144,1280]{1,0:T(8,128)(2,1)S(1)} %get-tuple-element.43), channel_id=1, source_target_pairs={{0,1},{1,2},{2,3},{3,0},{4,5},{5,6},{6,7},{7,4},{8,9},{9,10},{10,1... | collective-permute-start | bytes 1105928 | tf_op jit(solution)/shard_map/ppermute | solution.py:23
  16.8 9.5 %collective-permute-start.4 = (bf16[144,1280]{1,0:T(8,128)(2,1)S(1)}, bf16[144,1280]{1,0:T(8,128)(2,1)S(1)}, u32[]{:S(2)}, u32[]{:S(2)}) collective-permute-start(bf16[144,1280]{1,0:T(8,128)(2,1)S(1)} %get-tuple-element.44), channel_id=1, source_target_pairs={{0,3},{1,0},{2,1},{3,2},{4,7},{5,4},{6,5},{7,6},{8,11},{9,8},{10,9... | collective-permute-start | bytes 1105928 | tf_op jit(solution)/shard_map/ppermute | solution.py:23
  18.6 13.5 %collective-permute-start.10 = (bf16[144,1280]{1,0:T(8,128)(2,1)S(1)}, bf16[144,1280]{1,0:T(8,128)(2,1)S(1)}, u32[]{:S(2)}, u32[]{:S(2)}) collective-permute-start(bf16[144,1280]{1,0:T(8,128)(2,1)S(1)} %get-tuple-element.49.refs_6_), channel_id=1, source_target_pairs={{0,4},{1,5},{2,6},{3,7},{4,0},{5,1},{6,2},{7,3},{8,12},{9,13},{10,... | collective-permute-start | bytes 1105928 | tf_op jit(solution)/shard_map/ppermute | solution.py:33
  24.1 15.8 %copy-start.3 = (bf16[1,9,16,5120]{3,2,1,0:T(8,128)(2,1)S(1)}, bf16[1,9,16,5120]{3,2,1,0:T(8,128)(2,1)}, u32[]{:S(2)}) copy-start(bf16[1,9,16,5120]{3,2,1,0:T(8,128)(2,1)} %param.10) | copy-start | bytes 4423684
  24.1 8.5 %collective-permute-start.12 = (bf16[144,1280]{1,0:T(8,128)(2,1)S(1)}, bf16[144,1280]{1,0:T(8,128)(2,1)S(1)}, u32[]{:S(2)}, u32[]{:S(2)}) collective-permute-start(bf16[144,1280]{1,0:T(8,128)(2,1)S(1)} %hold.5), channel_id=1, source_target_pairs={{0,2},{1,3},{2,0},{3,1},{4,6},{5,7},{6,4},{7,5},{8,10},{9,11},{10,... | collective-permute-start | bytes 1105928 | tf_op jit(solution)/shard_map/ppermute | solution.py:23
  25.5 14.4 %collective-permute-start.5 = (bf16[144,1280]{1,0:T(8,128)(2,1)S(1)}, bf16[144,1280]{1,0:T(8,128)(2,1)S(1)}, u32[]{:S(2)}, u32[]{:S(2)}) collective-permute-start(bf16[144,1280]{1,0:T(8,128)(2,1)S(1)} %get-tuple-element.42.refs_2_.refs_5_), channel_id=1, source_target_pairs={{0,4},{1,5},{2,6},{3,7},{4,0},{5,1},{6,2},{7,3},{8,12},{9,13},{10,... | collective-permute-start | bytes 1105928 | tf_op jit(solution)/shard_map/ppermute | solution.py:33
  32.9 26.6 %collective-permute-start.20 = (bf16[432,768]{1,0:T(8,128)(2,1)S(1)}, bf16[432,768]{1,0:T(8,128)(2,1)S(1)}, u32[]{:S(2)}, u32[]{:S(2)}) collective-permute-start(bf16[432,768]{1,0:T(8,128)(2,1)S(1)} %stack.5), channel_id=1, source_target_pairs={{0,4},{1,5},{2,6},{3,7},{4,0},{5,1},{6,2},{7,3},{8,12},{9,13},{10,... | collective-permute-start | bytes 1990664 | tf_op jit(solution)/shard_map/ppermute | solution.py:33
  33.2 12.8 %collective-permute-start.9 = (bf16[144,1280]{1,0:T(8,128)(2,1)S(1)}, bf16[144,1280]{1,0:T(8,128)(2,1)S(1)}, u32[]{:S(2)}, u32[]{:S(2)}) collective-permute-start(bf16[144,1280]{1,0:T(8,128)(2,1)S(1)} %get-tuple-element.50), channel_id=1, source_target_pairs={{0,2},{1,3},{2,0},{3,1},{4,6},{5,7},{6,4},{7,5},{8,10},{9,11},{10,... | collective-permute-start | bytes 1105928 | tf_op jit(solution)/shard_map/ppermute | solution.py:23
  40.1 14.2 %collective-permute-start.6 = (bf16[144,1280]{1,0:T(8,128)(2,1)S(1)}, bf16[144,1280]{1,0:T(8,128)(2,1)S(1)}, u32[]{:S(2)}, u32[]{:S(2)}) collective-permute-start(bf16[144,1280]{1,0:T(8,128)(2,1)S(1)} %get-tuple-element.46), channel_id=1, source_target_pairs={{0,1},{1,2},{2,3},{3,0},{4,5},{5,6},{6,7},{7,4},{8,9},{9,10},{10,1... | collective-permute-start | bytes 1105928 | tf_op jit(solution)/shard_map/ppermute | solution.py:23
  40.2 18.7 %collective-permute-start.7 = (bf16[144,1280]{1,0:T(8,128)(2,1)S(1)}, bf16[144,1280]{1,0:T(8,128)(2,1)S(1)}, u32[]{:S(2)}, u32[]{:S(2)}) collective-permute-start(bf16[144,1280]{1,0:T(8,128)(2,1)S(1)} %get-tuple-element.47), channel_id=1, source_target_pairs={{0,3},{1,0},{2,1},{3,2},{4,7},{5,4},{6,5},{7,6},{8,11},{9,8},{10,9... | collective-permute-start | bytes 1105928 | tf_op jit(solution)/shard_map/ppermute | solution.py:23
  42.9 16.7 %collective-permute-start.8 = (bf16[144,1280]{1,0:T(8,128)(2,1)S(1)}, bf16[144,1280]{1,0:T(8,128)(2,1)S(1)}, u32[]{:S(2)}, u32[]{:S(2)}) collective-permute-start(bf16[144,1280]{1,0:T(8,128)(2,1)S(1)} %get-tuple-element.48), channel_id=1, source_target_pairs={{0,2},{1,3},{2,0},{3,1},{4,6},{5,7},{6,4},{7,5},{8,10},{9,11},{10,... | collective-permute-start | bytes 1105928 | tf_op jit(solution)/shard_map/ppermute | solution.py:23
  46.3 12.6 %collective-permute-start.19 = (bf16[144,768]{1,0:T(8,128)(2,1)S(1)}, bf16[144,768]{1,0:T(8,128)(2,1)S(1)}, u32[]{:S(2)}, u32[]{:S(2)}) collective-permute-start(bf16[144,768]{1,0:T(8,128)(2,1)S(1)} %stack.4), channel_id=1, source_target_pairs={{0,4},{1,5},{2,6},{3,7},{4,0},{5,1},{6,2},{7,3},{8,12},{9,13},{10,... | collective-permute-start | bytes 663560 | tf_op jit(solution)/shard_map/ppermute | solution.py:33
  54.5 14.7 %collective-permute-start.13 = (bf16[576,512]{1,0:T(8,128)(2,1)S(1)}, bf16[576,512]{1,0:T(8,128)(2,1)S(1)}, u32[]{:S(2)}, u32[]{:S(2)}) collective-permute-start(bf16[576,512]{1,0:T(8,128)(2,1)S(1)} %stack.3), channel_id=1, source_target_pairs={{0,4},{1,5},{2,6},{3,7},{4,0},{5,1},{6,2},{7,3},{8,12},{9,13},{10,... | collective-permute-start | bytes 1769480 | tf_op jit(solution)/shard_map/ppermute | solution.py:33
  66.2 10.6 %collective-permute-start.21 = (bf16[144,768]{1,0:T(8,128)(2,1)S(1)}, bf16[144,768]{1,0:T(8,128)(2,1)S(1)}, u32[]{:S(2)}, u32[]{:S(2)}) collective-permute-start(bf16[144,768]{1,0:T(8,128)(2,1)S(1)} %get-tuple-element.61), channel_id=1, source_target_pairs={{0,3},{1,0},{2,1},{3,2},{4,7},{5,4},{6,5},{7,6},{8,11},{9,8},{10,9... | collective-permute-start | bytes 663560 | tf_op jit(solution)/shard_map/ppermute | solution.py:23
  67.9 10.2 %collective-permute-start.22 = (bf16[144,768]{1,0:T(8,128)(2,1)S(1)}, bf16[144,768]{1,0:T(8,128)(2,1)S(1)}, u32[]{:S(2)}, u32[]{:S(2)}) collective-permute-start(bf16[144,768]{1,0:T(8,128)(2,1)S(1)} %get-tuple-element.62), channel_id=1, source_target_pairs={{0,1},{1,2},{2,3},{3,0},{4,5},{5,6},{6,7},{7,4},{8,9},{9,10},{10,1... | collective-permute-start | bytes 663560 | tf_op jit(solution)/shard_map/ppermute | solution.py:23
  67.9 10.2 %copy-start.4 = (f32[5120]{0:T(1024)S(1)}, f32[5120]{0:T(1024)}, u32[]{:S(2)}) copy-start(f32[5120]{0:T(1024)} %param.16) | copy-start | bytes 61444
  67.9 10.2 %collective-permute-start.23 = (bf16[144,768]{1,0:T(8,128)(2,1)S(1)}, bf16[144,768]{1,0:T(8,128)(2,1)S(1)}, u32[]{:S(2)}, u32[]{:S(2)}) collective-permute-start(bf16[144,768]{1,0:T(8,128)(2,1)S(1)} %get-tuple-element.63), channel_id=1, source_target_pairs={{0,2},{1,3},{2,0},{3,1},{4,6},{5,7},{6,4},{7,5},{8,10},{9,11},{10,... | collective-permute-start | bytes 663560 | tf_op jit(solution)/shard_map/ppermute | solution.py:23
  73.6 11.9 %collective-permute-start.14 = (bf16[144,512]{1,0:T(8,128)(2,1)S(1)}, bf16[144,512]{1,0:T(8,128)(2,1)S(1)}, u32[]{:S(2)}, u32[]{:S(2)}) collective-permute-start(bf16[144,512]{1,0:T(8,128)(2,1)S(1)} %get-tuple-element.53), channel_id=1, source_target_pairs={{0,3},{1,0},{2,1},{3,2},{4,7},{5,4},{6,5},{7,6},{8,11},{9,8},{10,9... | collective-permute-start | bytes 442376 | tf_op jit(solution)/shard_map/ppermute | solution.py:23
  76.8 8.7 %collective-permute-start.15 = (bf16[144,512]{1,0:T(8,128)(2,1)S(1)}, bf16[144,512]{1,0:T(8,128)(2,1)S(1)}, u32[]{:S(2)}, u32[]{:S(2)}) collective-permute-start(bf16[144,512]{1,0:T(8,128)(2,1)S(1)} %get-tuple-element.54), channel_id=1, source_target_pairs={{0,1},{1,2},{2,3},{3,0},{4,5},{5,6},{6,7},{7,4},{8,9},{9,10},{10,1... | collective-permute-start | bytes 442376 | tf_op jit(solution)/shard_map/ppermute | solution.py:23
  76.8 8.7 %collective-permute-start.16 = (bf16[144,512]{1,0:T(8,128)(2,1)S(1)}, bf16[144,512]{1,0:T(8,128)(2,1)S(1)}, u32[]{:S(2)}, u32[]{:S(2)}) collective-permute-start(bf16[144,512]{1,0:T(8,128)(2,1)S(1)} %get-tuple-element.55), channel_id=1, source_target_pairs={{0,2},{1,3},{2,0},{3,1},{4,6},{5,7},{6,4},{7,5},{8,10},{9,11},{10,... | collective-permute-start | bytes 442376 | tf_op jit(solution)/shard_map/ppermute | solution.py:23
  78.4 21.4 %copy-start.8 = (s32[32]{0:T(128)S(1)}, s32[32]{0:T(128)}, u32[]{:S(2)}) copy-start(s32[32]{0:T(128)} %overlaps_ref.3) | copy-start | bytes 388
  78.4 12.1 %collective-permute-start.24 = (bf16[64,3072]{1,0:T(8,128)(2,1)S(1)}, bf16[64,3072]{1,0:T(8,128)(2,1)S(1)}, u32[]{:S(2)}, u32[]{:S(2)}) collective-permute-start(bf16[64,3072]{1,0:T(8,128)(2,1)S(1)} %get-tuple-element.66.refs_2_), channel_id=1, source_target_pairs={{0,8},{8,16},{16,24},{24,32},{32,40},{40,48},{48,56},{56,64},{64,7... | collective-permute-start | bytes 1179656 | tf_op jit(solution)/shard_map/ppermute | solution.py:389
  85.5 14.2 %collective-permute-start.25 = (bf16[64,3072]{1,0:T(8,128)(2,1)S(1)}, bf16[64,3072]{1,0:T(8,128)(2,1)S(1)}, u32[]{:S(2)}, u32[]{:S(2)}) collective-permute-start(bf16[64,3072]{1,0:T(8,128)(2,1)S(1)} %get-tuple-element.64.refs_0_), channel_id=1, source_target_pairs={{0,248},{8,0},{16,8},{24,16},{32,24},{40,32},{48,40},{56,48},{64,5... | collective-permute-start | bytes 1179656 | tf_op jit(solution)/shard_map/ppermute | solution.py:389
  85.7 15.9 %collective-permute-start.17 = (bf16[64,2048]{1,0:T(8,128)(2,1)S(1)}, bf16[64,2048]{1,0:T(8,128)(2,1)S(1)}, u32[]{:S(2)}, u32[]{:S(2)}) collective-permute-start(bf16[64,2048]{1,0:T(8,128)(2,1)S(1)} %get-tuple-element.58.refs_2_), channel_id=1, source_target_pairs={{0,8},{8,16},{16,24},{24,32},{32,40},{40,48},{48,56},{56,64},{64,7... | collective-permute-start | bytes 786440 | tf_op jit(solution)/shard_map/ppermute | solution.py:389
  90.5 12.1 %collective-permute-start.18 = (bf16[64,2048]{1,0:T(8,128)(2,1)S(1)}, bf16[64,2048]{1,0:T(8,128)(2,1)S(1)}, u32[]{:S(2)}, u32[]{:S(2)}) collective-permute-start(bf16[64,2048]{1,0:T(8,128)(2,1)S(1)} %get-tuple-element.56.refs_0_), channel_id=1, source_target_pairs={{0,248},{8,0},{16,8},{24,16},{32,24},{40,32},{48,40},{56,48},{64,5... | collective-permute-start | bytes 786440 | tf_op jit(solution)/shard_map/ppermute | solution.py:389

commit v3 on v2

--- a/solution.py
+++ b/solution.py
@@ -423,8 +423,8 @@
     moved = [keys[3], *values[1:]]
     sends = [
         (
-            across(stack(moved[:1], skips[0], parts[0], (far_keys[1], far_value, *laters))),
-            across(stack(moved[1:], skips[0], parts[0], far_keys[2:])),
+            across(stack(moved[:1], skips[0], parts[0], (far_keys[1], far_value))),
+            across(stack(moved[1:], skips[0], parts[0], (*far_keys[2:], *laters))),
         ),
         *((across(stack(moved, skip, take, asked[1:2])),) for skip, take in zip(skips[1:], parts[1:])),
     ]

time: 104 us -> 103 us (level)
  waiting for transfers between devices: 39.9 us -> 38.6 us
    ppermute x7, waiting for transfers between devices: 19.6 us -> 16.6 us  [across(): return lax.ppermute(value, 'token', pairs)]
    ppermute x15, waiting for transfers between devices: 10.1 us -> 12.9 us  [send(): return lax.ppermute(value, 'token', pairs)]
    ppermute x4, waiting for transfers between devices: 10.2 us -> 9.14 us  [shift(): return lax.ppermute(value, 'window', pairs)]
    unnamed x22 -> x20, local copies, waits for them, and re-layouts: 4.08 us -> 4.07 us
  transfers between devices with their start and end apart: 26 -> 26, of which waited for: 10 -> 11; matrix products, arithmetic and copies ran while one was open for 0% -> 0% of each run, Pallas kernels for 19% -> 20%
where the time goes in v3:
time: 103 us
  waiting for transfers between devices  38.6 us (37%)
  starting transfers between devices  38.3 us (37%)
  Pallas kernels  22 us (21%)
  local copies, waits for them, and re-layouts  4.07 us (4%)
    ppermute x15, starting transfers between devices, send(): return lax.ppermute(value, 'token', pairs)  19.1 us
    ppermute x7, waiting for transfers between devices, across(): return lax.ppermute(value, 'token', pairs)  16.6 us
    ppermute x15, waiting for transfers between devices, send(): return lax.ppermute(value, 'token', pairs)  12.9 us
    ppermute x4, starting transfers between devices, shift(): return lax.ppermute(value, 'window', pairs)  12 us
    pallas_call x2, Pallas kernels, attend(): pl.pallas_call(body, name='attend', out_shape=[jax.ShapeDtypeStruct((rows...  11 us
    ppermute x4, waiting for transfers between devices, shift(): return lax.ppermute(value, 'window', pairs)  9.14 us
    ppermute x7, starting transfers between devices, across(): return lax.ppermute(value, 'token', pairs)  7.24 us
    unnamed x20, local copies, waits for them, and re-layouts  4.07 us
  transfers between devices with their start and end apart: 26, of which 11 were waited for; matrix products, arithmetic and copies ran while one was open for 0% of the time, Pallas kernels for 20%

profile of v3, /device:TPU:1, one launch (start us, length us, event | category | flops | bytes accessed | tf_op | source)
XLA Modules:
  0.0 103.3 jit_solution(558701078439972421)
XLA Ops:
  0.0 1.4 %copy-done.2 = bf16[1,9,16,5120]{3,2,1,0:T(8,128)(2,1)S(1)} copy-done((bf16[1,9,16,5120]{3,2,1,0:T(8,128)(2,1)S(1)}, bf16[1,9,16,5120]{3,2,1,0:T(8,128)(2,1)}, u32[]{:S(2)}) %copy-start.2) | copy-done | bytes 1474584
  1.4 0.1 pack.3.refs_0_.refs_4_
  1.4 3.7 %collective-permute-start.2 = (bf16[144,1280]{1,0:T(8,128)(2,1)S(1)}, bf16[144,1280]{1,0:T(8,128)(2,1)S(1)}, u32[]{:S(2)}, u32[]{:S(2)}) collective-permute-start(bf16[144,1280]{1,0:T(8,128)(2,1)S(1)} %pack.3.refs_0_.refs_4_), channel_id=1, source_target_pairs={{0,4},{1,5},{2,6},{3,7},{4,0},{5,1},{6,2},{7,3},{8,12},{9,13},{10,... | collective-permute-start | bytes 1105928 | tf_op jit(solution)/shard_map/ppermute | solution.py:33
  5.1 0.1 pack.4
  5.2 1.4 %collective-permute-start = (bf16[144,1280]{1,0:T(8,128)(2,1)S(1)}, bf16[144,1280]{1,0:T(8,128)(2,1)S(1)}, u32[]{:S(2)}, u32[]{:S(2)}) collective-permute-start(bf16[144,1280]{1,0:T(8,128)(2,1)S(1)} %get-tuple-element.39), channel_id=1, source_target_pairs={{0,1},{1,2},{2,3},{3,0},{4,5},{5,6},{6,7},{7,4},{8,9},{9,10},{10,1... | collective-permute-start | bytes 1105928 | tf_op jit(solution)/shard_map/ppermute | solution.py:23
  6.6 1.5 %collective-permute-start.1 = (bf16[144,1280]{1,0:T(8,128)(2,1)S(1)}, bf16[144,1280]{1,0:T(8,128)(2,1)S(1)}, u32[]{:S(2)}, u32[]{:S(2)}) collective-permute-start(bf16[144,1280]{1,0:T(8,128)(2,1)S(1)} %get-tuple-element.40), channel_id=1, source_target_pairs={{0,3},{1,0},{2,1},{3,2},{4,7},{5,4},{6,5},{7,6},{8,11},{9,8},{10,9... | collective-permute-start | bytes 1105928 | tf_op jit(solution)/shard_map/ppermute | solution.py:23
  8.2 0.0 copy-start
  8.2 2.7 %copy-done = bf16[4,1,9,16,5120]{4,3,2,1,0:T(8,128)(2,1)S(1)} copy-done((bf16[4,1,9,16,5120]{4,3,2,1,0:T(8,128)(2,1)S(1)}, bf16[4,1,9,16,5120]{4,3,2,1,0:T(8,128)(2,1)}, u32[]{:S(2)}) %copy-start) | copy-done | bytes 5898264
  10.8 3.0 %prepare.1 = (bf16[144,1280]{1,0:T(8,128)(2,1)S(1)}, bf16[144,1280]{1,0:T(8,128)(2,1)S(1)}, bf16[144,1280]{1,0:T(8,128)(2,1)S(1)}, bf16[144,1280]{1,0:T(8,128)(2,1)S(1)}) custom-call(s32[4]{0:T(128)S(1)} %copy-done.7, s32[32]{0:T(128)S(1)} %copy-done.8, bf16[9,16,5120]{2,1,0:T(8,128)(2,1)S(1)} %bitcast.11, bf16[4,9,16,5120]{3,2,1,0:T(8,128)(2,1)S(1)} %bitcast.7, ...), custom_call_target="tpu_custom_call" | custom-call | flops 14745600 | bytes 8847360 | tf_op jit(solution)/shard_map/prepare/pallas_call | solution.py:164
  13.8 0.3 collective-permute-start.11
  14.1 1.7 %collective-permute-done.refs_0_ = bf16[144,1280]{1,0:T(8,128)(2,1)S(1)} collective-permute-done((bf16[144,1280]{1,0:T(8,128)(2,1)S(1)}, bf16[144,1280]{1,0:T(8,128)(2,1)S(1)}, u32[]{:S(2)}, u32[]{:S(2)}) %collective-permute-start) | collective-permute-done | bytes 368672 | tf_op jit(solution)/shard_map/ppermute | solution.py:23
  15.8 0.0 collective-permute-done.1.refs_1_
  15.8 0.0 collective-permute-done.2.refs_3_.refs_8_
  15.8 0.9 collective-permute-start.3
  16.8 1.8 %collective-permute-start.4 = (bf16[144,1280]{1,0:T(8,128)(2,1)S(1)}, bf16[144,1280]{1,0:T(8,128)(2,1)S(1)}, u32[]{:S(2)}, u32[]{:S(2)}) collective-permute-start(bf16[144,1280]{1,0:T(8,128)(2,1)S(1)} %get-tuple-element.44), channel_id=1, source_target_pairs={{0,3},{1,0},{2,1},{3,2},{4,7},{5,4},{6,5},{7,6},{8,11},{9,8},{10,9... | collective-permute-start | bytes 1105928 | tf_op jit(solution)/shard_map/ppermute | solution.py:23
  18.6 1.1 %collective-permute-start.10 = (bf16[144,1280]{1,0:T(8,128)(2,1)S(1)}, bf16[144,1280]{1,0:T(8,128)(2,1)S(1)}, u32[]{:S(2)}, u32[]{:S(2)}) collective-permute-start(bf16[144,1280]{1,0:T(8,128)(2,1)S(1)} %get-tuple-element.49.refs_6_), channel_id=1, source_target_pairs={{0,4},{1,5},{2,6},{3,7},{4,0},{5,1},{6,2},{7,3},{8,12},{9,13},{10,... | collective-permute-start | bytes 1105928 | tf_op jit(solution)/shard_map/ppermute | solution.py:33
  19.7 4.5 %collective-permute-done.11.refs_1_.refs_16_.refs_2_ = bf16[144,1280]{1,0:T(8,128)(2,1)S(1)} collective-permute-done((bf16[144,1280]{1,0:T(8,128)(2,1)S(1)}, bf16[144,1280]{1,0:T(8,128)(2,1)S(1)}, u32[]{:S(2)}, u32[]{:S(2)}) %collective-permute-start.11) | collective-permute-done | bytes 368672 | tf_op jit(solution)/shard_map/ppermute | solution.py:33
  24.1 1.4 %collective-permute-start.12 = (bf16[144,1280]{1,0:T(8,128)(2,1)S(1)}, bf16[144,1280]{1,0:T(8,128)(2,1)S(1)}, u32[]{:S(2)}, u32[]{:S(2)}) collective-permute-start(bf16[144,1280]{1,0:T(8,128)(2,1)S(1)} %hold.5), channel_id=1, source_target_pairs={{0,2},{1,3},{2,0},{3,1},{4,6},{5,7},{6,4},{7,5},{8,10},{9,11},{10,... | collective-permute-start | bytes 1105928 | tf_op jit(solution)/shard_map/ppermute | solution.py:23
  25.5 0.7 collective-permute-start.5
  26.2 2.9 %add.1 = (f32[144,3072]{1,0:T(8,128)S(1)}, f32[144,2048]{1,0:T(8,128)S(1)}) custom-call(s32[4]{0:T(128)S(1)} %copy-done.7, s32[32]{0:T(128)S(1)} %copy-done.8, bf16[9,16,5120]{2,1,0:T(8,128)(2,1)S(1)} %bitcast.12, bf16[4,9,16,5120]{3,2,1,0:T(8,128)(2,1)S(1)} %bitcast.8), custom_call_target="tpu_custom_call" | custom-call | flops 7372800 | bytes 10321920 | tf_op jit(solution)/shard_map/add/pallas_call | solution.py:207
  29.2 0.0 collective-permute-done.4.refs_1_.refs_2_.refs_14_
  29.2 2.8 %collective-permute-done.10.refs_10_.refs_3_ = bf16[144,1280]{1,0:T(8,128)(2,1)S(1)} collective-permute-done((bf16[144,1280]{1,0:T(8,128)(2,1)S(1)}, bf16[144,1280]{1,0:T(8,128)(2,1)S(1)}, u32[]{:S(2)}, u32[]{:S(2)}) %collective-permute-start.10) | collective-permute-done | bytes 368672 | tf_op jit(solution)/shard_map/ppermute | solution.py:33
  32.0 0.6 collective-permute-done.12.refs_3_.refs_15_.refs_2_
  32.6 0.3 stack.5
  32.9 0.2 collective-permute-start.20
  33.2 1.6 %collective-permute-start.9 = (bf16[144,1280]{1,0:T(8,128)(2,1)S(1)}, bf16[144,1280]{1,0:T(8,128)(2,1)S(1)}, u32[]{:S(2)}, u32[]{:S(2)}) collective-permute-start(bf16[144,1280]{1,0:T(8,128)(2,1)S(1)} %get-tuple-element.50), channel_id=1, source_target_pairs={{0,2},{1,3},{2,0},{3,1},{4,6},{5,7},{6,4},{7,5},{8,10},{9,11},{10,... | collective-permute-start | bytes 1105928 | tf_op jit(solution)/shard_map/ppermute | solution.py:23
  34.8 5.1 %collective-permute-done.5.refs_2_.refs_9_.refs_1_ = bf16[144,1280]{1,0:T(8,128)(2,1)S(1)} collective-permute-done((bf16[144,1280]{1,0:T(8,128)(2,1)S(1)}, bf16[144,1280]{1,0:T(8,128)(2,1)S(1)}, u32[]{:S(2)}, u32[]{:S(2)}) %collective-permute-start.5) | collective-permute-done | bytes 368672 | tf_op jit(solution)/shard_map/ppermute | solution.py:33
  39.9 0.2 pack.5
  40.1 0.1 collective-permute-start.6
  40.2 2.7 %collective-permute-start.7 = (bf16[144,1280]{1,0:T(8,128)(2,1)S(1)}, bf16[144,1280]{1,0:T(8,128)(2,1)S(1)}, u32[]{:S(2)}, u32[]{:S(2)}) collective-permute-start(bf16[144,1280]{1,0:T(8,128)(2,1)S(1)} %get-tuple-element.47), channel_id=1, source_target_pairs={{0,3},{1,0},{2,1},{3,2},{4,7},{5,4},{6,5},{7,6},{8,11},{9,8},{10,9... | collective-permute-start | bytes 1105928 | tf_op jit(solution)/shard_map/ppermute | solution.py:23
  42.9 0.2 collective-permute-start.8
  43.0 0.3 stack.4
  43.4 0.9 collective-permute-start.19
  44.3 9.9 %collective-permute-done.6.refs_4_.refs_1_ = bf16[144,1280]{1,0:T(8,128)(2,1)S(1)} collective-permute-done((bf16[144,1280]{1,0:T(8,128)(2,1)S(1)}, bf16[144,1280]{1,0:T(8,128)(2,1)S(1)}, u32[]{:S(2)}, u32[]{:S(2)}) %collective-permute-start.6) | collective-permute-done | bytes 368672 | tf_op jit(solution)/shard_map/ppermute | solution.py:23
  54.3 0.2 stack.3
  54.5 0.3 collective-permute-start.13
  54.8 4.1 %collective-permute-done.19.refs_11_ = bf16[144,768]{1,0:T(8,128)(2,1)S(1)} collective-permute-done((bf16[144,768]{1,0:T(8,128)(2,1)S(1)}, bf16[144,768]{1,0:T(8,128)(2,1)S(1)}, u32[]{:S(2)}, u32[]{:S(2)}) %collective-permute-start.19) | collective-permute-done | bytes 221216 | tf_op jit(solution)/shard_map/ppermute | solution.py:33
  58.9 0.7 collective-permute-done.8.refs_3_
  59.5 6.6 %attend.3 = (bf16[144,768]{1,0:T(8,128)(2,1)S(1)}, bf16[144,768]{1,0:T(8,128)(2,1)S(1)}, bf16[144,768]{1,0:T(8,128)(2,1)S(1)}, bf16[144,768]{1,0:T(8,128)(2,1)S(1)}) custom-call(bf16[144,1280]{1,0:T(8,128)(2,1)S(1)} %get-tuple-element.45.refs_0_, bf16[144,1280]{1,0:T(8,128)(2,1)S(1)} %collective-permute-done.6.refs_4_.refs_1_, ...), custom_call_target="tpu_custom_call" | custom-call | flops 4076863488 | bytes 10616832 | tf_op jit(solution)/shard_map/attend/pallas_call | solution.py:270
  66.2 1.7 %collective-permute-start.21 = (bf16[144,768]{1,0:T(8,128)(2,1)S(1)}, bf16[144,768]{1,0:T(8,128)(2,1)S(1)}, u32[]{:S(2)}, u32[]{:S(2)}) collective-permute-start(bf16[144,768]{1,0:T(8,128)(2,1)S(1)} %get-tuple-element.61), channel_id=1, source_target_pairs={{0,3},{1,0},{2,1},{3,2},{4,7},{5,4},{6,5},{7,6},{8,11},{9,8},{10,9... | collective-permute-start | bytes 663560 | tf_op jit(solution)/shard_map/ppermute | solution.py:23
  67.9 0.0 collective-permute-start.22
  67.9 1.3 %collective-permute-start.23 = (bf16[144,768]{1,0:T(8,128)(2,1)S(1)}, bf16[144,768]{1,0:T(8,128)(2,1)S(1)}, u32[]{:S(2)}, u32[]{:S(2)}) collective-permute-start(bf16[144,768]{1,0:T(8,128)(2,1)S(1)} %get-tuple-element.63), channel_id=1, source_target_pairs={{0,2},{1,3},{2,0},{3,1},{4,6},{5,7},{6,4},{7,5},{8,10},{9,11},{10,... | collective-permute-start | bytes 663560 | tf_op jit(solution)/shard_map/ppermute | solution.py:23
  69.1 0.0 collective-permute-done.13.refs_11_
  69.2 4.4 %attend.2 = (bf16[144,512]{1,0:T(8,128)(2,1)S(1)}, bf16[144,512]{1,0:T(8,128)(2,1)S(1)}, bf16[144,512]{1,0:T(8,128)(2,1)S(1)}, bf16[144,512]{1,0:T(8,128)(2,1)S(1)}) custom-call(bf16[144,1280]{1,0:T(8,128)(2,1)S(1)} %get-tuple-element.45.refs_0_, bf16[144,1280]{1,0:T(8,128)(2,1)S(1)} %collective-permute-done.6.refs_4_.refs_1_, ...), custom_call_target="tpu_custom_call" | custom-call | flops 2717908992 | bytes 7077888 | tf_op jit(solution)/shard_map/attend/pallas_call | solution.py:270
  73.6 3.3 %collective-permute-start.14 = (bf16[144,512]{1,0:T(8,128)(2,1)S(1)}, bf16[144,512]{1,0:T(8,128)(2,1)S(1)}, u32[]{:S(2)}, u32[]{:S(2)}) collective-permute-start(bf16[144,512]{1,0:T(8,128)(2,1)S(1)} %get-tuple-element.53), channel_id=1, source_target_pairs={{0,3},{1,0},{2,1},{3,2},{4,7},{5,4},{6,5},{7,6},{8,11},{9,8},{10,9... | collective-permute-start | bytes 442376 | tf_op jit(solution)/shard_map/ppermute | solution.py:23
  76.8 1.3 %collective-permute-start.16 = (bf16[144,512]{1,0:T(8,128)(2,1)S(1)}, bf16[144,512]{1,0:T(8,128)(2,1)S(1)}, u32[]{:S(2)}, u32[]{:S(2)}) collective-permute-start(bf16[144,512]{1,0:T(8,128)(2,1)S(1)} %get-tuple-element.55), channel_id=1, source_target_pairs={{0,2},{1,3},{2,0},{3,1},{4,6},{5,7},{6,4},{7,5},{8,10},{9,11},{10,... | collective-permute-start | bytes 442376 | tf_op jit(solution)/shard_map/ppermute | solution.py:23
  78.1 0.0 collective-permute-done.22.refs_2_
  78.1 0.0 collective-permute-done.23.refs_3_
  78.1 0.2 join.3
  78.3 0.0 copy-start.9
  78.4 6.9 %collective-permute-start.25 = (bf16[64,3072]{1,0:T(8,128)(2,1)S(1)}, bf16[64,3072]{1,0:T(8,128)(2,1)S(1)}, u32[]{:S(2)}, u32[]{:S(2)}) collective-permute-start(bf16[64,3072]{1,0:T(8,128)(2,1)S(1)} %get-tuple-element.64.refs_0_), channel_id=1, source_target_pairs={{0,248},{8,0},{16,8},{24,16},{32,24},{40,32},{48,40},{56,48},{64,5... | collective-permute-start | bytes 1179656 | tf_op jit(solution)/shard_map/ppermute | solution.py:389
  85.3 0.3 collective-permute-start.24
  85.6 0.0 collective-permute-done.14.refs_1_
  85.6 0.0 collective-permute-done.15.refs_2_
  85.6 0.0 collective-permute-done.16.refs_3_
  85.6 0.2 join.2
  85.8 3.3 %collective-permute-start.18 = (bf16[64,2048]{1,0:T(8,128)(2,1)S(1)}, bf16[64,2048]{1,0:T(8,128)(2,1)S(1)}, u32[]{:S(2)}, u32[]{:S(2)}) collective-permute-start(bf16[64,2048]{1,0:T(8,128)(2,1)S(1)} %get-tuple-element.56.refs_0_), channel_id=1, source_target_pairs={{0,248},{8,0},{16,8},{24,16},{32,24},{40,32},{48,40},{56,48},{64,5... | collective-permute-start | bytes 786440 | tf_op jit(solution)/shard_map/ppermute | solution.py:389
  89.1 1.5 %collective-permute-start.17 = (bf16[64,2048]{1,0:T(8,128)(2,1)S(1)}, bf16[64,2048]{1,0:T(8,128)(2,1)S(1)}, u32[]{:S(2)}, u32[]{:S(2)}) collective-permute-start(bf16[64,2048]{1,0:T(8,128)(2,1)S(1)} %get-tuple-element.58.refs_2_), channel_id=1, source_target_pairs={{0,8},{8,16},{16,24},{24,32},{32,40},{40,48},{48,56},{56,64},{64,7... | collective-permute-start | bytes 786440 | tf_op jit(solution)/shard_map/ppermute | solution.py:389
  90.5 0.4 collective-permute-done.25.refs_4_
  90.9 6.4 %collective-permute-done.24.refs_3_ = bf16[64,3072]{1,0:T(8,128)(2,1)S(1)} collective-permute-done((bf16[64,3072]{1,0:T(8,128)(2,1)S(1)}, bf16[64,3072]{1,0:T(8,128)(2,1)S(1)}, u32[]{:S(2)}, u32[]{:S(2)}) %collective-permute-start.24) | collective-permute-done | bytes 393248 | tf_op jit(solution)/shard_map/ppermute | solution.py:389
  97.3 1.8 %blend.2.refs_5_ = bf16[144,5120]{1,0:T(8,128)(2,1)} custom-call(s32[32]{0:T(128)S(1)} %copy-done.9, bf16[64,3072]{1,0:T(8,128)(2,1)S(1)} %get-tuple-element.64.refs_0_, bf16[16,3072]{1,0:T(8,128)(2,1)S(1)} %get-tuple-element.65.refs_1_, bf16[64,3072]{1,0:T(8,128)(2,1)S(1)} %get-tuple-element.66.refs_2_, ...), custom_call_target="tpu_custom_call" | custom-call | flops 1769472 | bytes 3538944 | tf_op jit(solution)/shard_map/blend/pallas_call | solution.py:366
  99.2 2.4 %collective-permute-done.18.refs_4_ = bf16[64,2048]{1,0:T(8,128)(2,1)S(1)} collective-permute-done((bf16[64,2048]{1,0:T(8,128)(2,1)S(1)}, bf16[64,2048]{1,0:T(8,128)(2,1)S(1)}, u32[]{:S(2)}, u32[]{:S(2)}) %collective-permute-start.18) | collective-permute-done | bytes 262176 | tf_op jit(solution)/shard_map/ppermute | solution.py:389
  101.5 0.0 collective-permute-done.17.refs_3_
  101.5 1.6 %blend.3 = bf16[144,5120]{1,0:T(8,128)(2,1)} custom-call(s32[32]{0:T(128)S(1)} %copy-done.9, bf16[64,2048]{1,0:T(8,128)(2,1)S(1)} %get-tuple-element.56.refs_0_, bf16[16,2048]{1,0:T(8,128)(2,1)S(1)} %get-tuple-element.57.refs_1_, bf16[64,2048]{1,0:T(8,128)(2,1)S(1)} %get-tuple-element.58.refs_2_, ...), custom_call_target="tpu_custom_call", output_to_operand_aliasing={{}: (6, {})} | custom-call | flops 1179648 | bytes 2359296 | tf_op jit(solution)/shard_map/blend/pallas_call | solution.py:366
  (25 shorter events, 0.0 us)
Async XLA Ops:
  0.0 1.4 %copy-start.2 = (bf16[1,9,16,5120]{3,2,1,0:T(8,128)(2,1)S(1)}, bf16[1,9,16,5120]{3,2,1,0:T(8,128)(2,1)}, u32[]{:S(2)}) copy-start(bf16[1,9,16,5120]{3,2,1,0:T(8,128)(2,1)} %param.11) | copy-start | bytes 4423684
  1.4 6.8 %copy-start.3 = (bf16[1,9,16,5120]{3,2,1,0:T(8,128)(2,1)S(1)}, bf16[1,9,16,5120]{3,2,1,0:T(8,128)(2,1)}, u32[]{:S(2)}) copy-start(bf16[1,9,16,5120]{3,2,1,0:T(8,128)(2,1)} %param.9) | copy-start | bytes 4423684
  1.4 6.8 %copy-start.6 = (f32[5120]{0:T(1024)S(1)}, f32[5120]{0:T(1024)}, u32[]{:S(2)}) copy-start(f32[5120]{0:T(1024)} %param.15) | copy-start | bytes 61444
  1.4 6.8 %copy-start.7 = (s32[4]{0:T(128)S(1)}, s32[4]{0:T(128)}, u32[]{:S(2)}) copy-start(s32[4]{0:T(128)} %plan_ref.3) | copy-start | bytes 52
  1.4 6.8 %copy-start.8 = (s32[32]{0:T(128)S(1)}, s32[32]{0:T(128)}, u32[]{:S(2)}) copy-start(s32[32]{0:T(128)} %refresh_ref.3) | copy-start | bytes 388
  1.4 14.4 %collective-permute-start.2 = (bf16[144,1280]{1,0:T(8,128)(2,1)S(1)}, bf16[144,1280]{1,0:T(8,128)(2,1)S(1)}, u32[]{:S(2)}, u32[]{:S(2)}) collective-permute-start(bf16[144,1280]{1,0:T(8,128)(2,1)S(1)} %pack.3.refs_0_.refs_4_), channel_id=1, source_target_pairs={{0,4},{1,5},{2,6},{3,7},{4,0},{5,1},{6,2},{7,3},{8,12},{9,13},{10,... | collective-permute-start | bytes 1105928 | tf_op jit(solution)/shard_map/ppermute | solution.py:33
  5.2 10.6 %collective-permute-start = (bf16[144,1280]{1,0:T(8,128)(2,1)S(1)}, bf16[144,1280]{1,0:T(8,128)(2,1)S(1)}, u32[]{:S(2)}, u32[]{:S(2)}) collective-permute-start(bf16[144,1280]{1,0:T(8,128)(2,1)S(1)} %get-tuple-element.39), channel_id=1, source_target_pairs={{0,1},{1,2},{2,3},{3,0},{4,5},{5,6},{6,7},{7,4},{8,9},{9,10},{10,1... | collective-permute-start | bytes 1105928 | tf_op jit(solution)/shard_map/ppermute | solution.py:23
  6.6 9.2 %collective-permute-start.1 = (bf16[144,1280]{1,0:T(8,128)(2,1)S(1)}, bf16[144,1280]{1,0:T(8,128)(2,1)S(1)}, u32[]{:S(2)}, u32[]{:S(2)}) collective-permute-start(bf16[144,1280]{1,0:T(8,128)(2,1)S(1)} %get-tuple-element.40), channel_id=1, source_target_pairs={{0,3},{1,0},{2,1},{3,2},{4,7},{5,4},{6,5},{7,6},{8,11},{9,8},{10,9... | collective-permute-start | bytes 1105928 | tf_op jit(solution)/shard_map/ppermute | solution.py:23
  8.2 2.7 %copy-start = (bf16[4,1,9,16,5120]{4,3,2,1,0:T(8,128)(2,1)S(1)}, bf16[4,1,9,16,5120]{4,3,2,1,0:T(8,128)(2,1)}, u32[]{:S(2)}) copy-start(bf16[4,1,9,16,5120]{4,3,2,1,0:T(8,128)(2,1)} %param.12) | copy-start | bytes 17694724
  10.8 15.4 %copy-start.1 = (bf16[4,1,9,16,5120]{4,3,2,1,0:T(8,128)(2,1)S(1)}, bf16[4,1,9,16,5120]{4,3,2,1,0:T(8,128)(2,1)}, u32[]{:S(2)}) copy-start(bf16[4,1,9,16,5120]{4,3,2,1,0:T(8,128)(2,1)} %param.12) | copy-start | bytes 17694724
  13.8 10.3 %collective-permute-start.11 = (bf16[144,1280]{1,0:T(8,128)(2,1)S(1)}, bf16[144,1280]{1,0:T(8,128)(2,1)S(1)}, u32[]{:S(2)}, u32[]{:S(2)}) collective-permute-start(bf16[144,1280]{1,0:T(8,128)(2,1)S(1)} %get-tuple-element.41.refs_2_.refs_12_), channel_id=1, source_target_pairs={{0,4},{1,5},{2,6},{3,7},{4,0},{5,1},{6,2},{7,3},{8,12},{9,13},{10,... | collective-permute-start | bytes 1105928 | tf_op jit(solution)/shard_map/ppermute | solution.py:33
  15.8 13.4 %collective-permute-start.3 = (bf16[144,1280]{1,0:T(8,128)(2,1)S(1)}, bf16[144,1280]{1,0:T(8,128)(2,1)S(1)}, u32[]{:S(2)}, u32[]{:S(2)}) collective-permute-start(bf16[144,1280]{1,0:T(8,128)(2,1)S(1)} %get-tuple-element.43), channel_id=1, source_target_pairs={{0,1},{1,2},{2,3},{3,0},{4,5},{5,6},{6,7},{7,4},{8,9},{9,10},{10,1... | collective-permute-start | bytes 1105928 | tf_op jit(solution)/shard_map/ppermute | solution.py:23
  16.8 12.4 %collective-permute-start.4 = (bf16[144,1280]{1,0:T(8,128)(2,1)S(1)}, bf16[144,1280]{1,0:T(8,128)(2,1)S(1)}, u32[]{:S(2)}, u32[]{:S(2)}) collective-permute-start(bf16[144,1280]{1,0:T(8,128)(2,1)S(1)} %get-tuple-element.44), channel_id=1, source_target_pairs={{0,3},{1,0},{2,1},{3,2},{4,7},{5,4},{6,5},{7,6},{8,11},{9,8},{10,9... | collective-permute-start | bytes 1105928 | tf_op jit(solution)/shard_map/ppermute | solution.py:23
  18.6 13.5 %collective-permute-start.10 = (bf16[144,1280]{1,0:T(8,128)(2,1)S(1)}, bf16[144,1280]{1,0:T(8,128)(2,1)S(1)}, u32[]{:S(2)}, u32[]{:S(2)}) collective-permute-start(bf16[144,1280]{1,0:T(8,128)(2,1)S(1)} %get-tuple-element.49.refs_6_), channel_id=1, source_target_pairs={{0,4},{1,5},{2,6},{3,7},{4,0},{5,1},{6,2},{7,3},{8,12},{9,13},{10,... | collective-permute-start | bytes 1105928 | tf_op jit(solution)/shard_map/ppermute | solution.py:33
  24.1 8.5 %collective-permute-start.12 = (bf16[144,1280]{1,0:T(8,128)(2,1)S(1)}, bf16[144,1280]{1,0:T(8,128)(2,1)S(1)}, u32[]{:S(2)}, u32[]{:S(2)}) collective-permute-start(bf16[144,1280]{1,0:T(8,128)(2,1)S(1)} %hold.5), channel_id=1, source_target_pairs={{0,2},{1,3},{2,0},{3,1},{4,6},{5,7},{6,4},{7,5},{8,10},{9,11},{10,... | collective-permute-start | bytes 1105928 | tf_op jit(solution)/shard_map/ppermute | solution.py:23
  25.5 14.4 %collective-permute-start.5 = (bf16[144,1280]{1,0:T(8,128)(2,1)S(1)}, bf16[144,1280]{1,0:T(8,128)(2,1)S(1)}, u32[]{:S(2)}, u32[]{:S(2)}) collective-permute-start(bf16[144,1280]{1,0:T(8,128)(2,1)S(1)} %get-tuple-element.42.refs_2_.refs_5_), channel_id=1, source_target_pairs={{0,4},{1,5},{2,6},{3,7},{4,0},{5,1},{6,2},{7,3},{8,12},{9,13},{10,... | collective-permute-start | bytes 1105928 | tf_op jit(solution)/shard_map/ppermute | solution.py:33
  32.6 7.3 %copy-start.4 = (bf16[1,9,16,5120]{3,2,1,0:T(8,128)(2,1)S(1)}, bf16[1,9,16,5120]{3,2,1,0:T(8,128)(2,1)}, u32[]{:S(2)}) copy-start(bf16[1,9,16,5120]{3,2,1,0:T(8,128)(2,1)} %param.10) | copy-start | bytes 4423684
  32.9 26.6 %collective-permute-start.20 = (bf16[432,768]{1,0:T(8,128)(2,1)S(1)}, bf16[432,768]{1,0:T(8,128)(2,1)S(1)}, u32[]{:S(2)}, u32[]{:S(2)}) collective-permute-start(bf16[432,768]{1,0:T(8,128)(2,1)S(1)} %stack.5), channel_id=1, source_target_pairs={{0,4},{1,5},{2,6},{3,7},{4,0},{5,1},{6,2},{7,3},{8,12},{9,13},{10,... | collective-permute-start | bytes 1990664 | tf_op jit(solution)/shard_map/ppermute | solution.py:33
  33.2 9.9 %collective-permute-start.9 = (bf16[144,1280]{1,0:T(8,128)(2,1)S(1)}, bf16[144,1280]{1,0:T(8,128)(2,1)S(1)}, u32[]{:S(2)}, u32[]{:S(2)}) collective-permute-start(bf16[144,1280]{1,0:T(8,128)(2,1)S(1)} %get-tuple-element.50), channel_id=1, source_target_pairs={{0,2},{1,3},{2,0},{3,1},{4,6},{5,7},{6,4},{7,5},{8,10},{9,11},{10,... | collective-permute-start | bytes 1105928 | tf_op jit(solution)/shard_map/ppermute | solution.py:23
  40.1 14.2 %collective-permute-start.6 = (bf16[144,1280]{1,0:T(8,128)(2,1)S(1)}, bf16[144,1280]{1,0:T(8,128)(2,1)S(1)}, u32[]{:S(2)}, u32[]{:S(2)}) collective-permute-start(bf16[144,1280]{1,0:T(8,128)(2,1)S(1)} %get-tuple-element.46), channel_id=1, source_target_pairs={{0,1},{1,2},{2,3},{3,0},{4,5},{5,6},{6,7},{7,4},{8,9},{9,10},{10,1... | collective-permute-start | bytes 1105928 | tf_op jit(solution)/shard_map/ppermute | solution.py:23
  40.2 18.7 %collective-permute-start.7 = (bf16[144,1280]{1,0:T(8,128)(2,1)S(1)}, bf16[144,1280]{1,0:T(8,128)(2,1)S(1)}, u32[]{:S(2)}, u32[]{:S(2)}) collective-permute-start(bf16[144,1280]{1,0:T(8,128)(2,1)S(1)} %get-tuple-element.47), channel_id=1, source_target_pairs={{0,3},{1,0},{2,1},{3,2},{4,7},{5,4},{6,5},{7,6},{8,11},{9,8},{10,9... | collective-permute-start | bytes 1105928 | tf_op jit(solution)/shard_map/ppermute | solution.py:23
  42.9 16.7 %collective-permute-start.8 = (bf16[144,1280]{1,0:T(8,128)(2,1)S(1)}, bf16[144,1280]{1,0:T(8,128)(2,1)S(1)}, u32[]{:S(2)}, u32[]{:S(2)}) collective-permute-start(bf16[144,1280]{1,0:T(8,128)(2,1)S(1)} %get-tuple-element.48), channel_id=1, source_target_pairs={{0,2},{1,3},{2,0},{3,1},{4,6},{5,7},{6,4},{7,5},{8,10},{9,11},{10,... | collective-permute-start | bytes 1105928 | tf_op jit(solution)/shard_map/ppermute | solution.py:23
  43.4 15.5 %collective-permute-start.19 = (bf16[144,768]{1,0:T(8,128)(2,1)S(1)}, bf16[144,768]{1,0:T(8,128)(2,1)S(1)}, u32[]{:S(2)}, u32[]{:S(2)}) collective-permute-start(bf16[144,768]{1,0:T(8,128)(2,1)S(1)} %stack.4), channel_id=1, source_target_pairs={{0,4},{1,5},{2,6},{3,7},{4,0},{5,1},{6,2},{7,3},{8,12},{9,13},{10,... | collective-permute-start | bytes 663560 | tf_op jit(solution)/shard_map/ppermute | solution.py:33
  54.5 14.7 %collective-permute-start.13 = (bf16[576,512]{1,0:T(8,128)(2,1)S(1)}, bf16[576,512]{1,0:T(8,128)(2,1)S(1)}, u32[]{:S(2)}, u32[]{:S(2)}) collective-permute-start(bf16[576,512]{1,0:T(8,128)(2,1)S(1)} %stack.3), channel_id=1, source_target_pairs={{0,4},{1,5},{2,6},{3,7},{4,0},{5,1},{6,2},{7,3},{8,12},{9,13},{10,... | collective-permute-start | bytes 1769480 | tf_op jit(solution)/shard_map/ppermute | solution.py:33
  66.2 10.6 %collective-permute-start.21 = (bf16[144,768]{1,0:T(8,128)(2,1)S(1)}, bf16[144,768]{1,0:T(8,128)(2,1)S(1)}, u32[]{:S(2)}, u32[]{:S(2)}) collective-permute-start(bf16[144,768]{1,0:T(8,128)(2,1)S(1)} %get-tuple-element.61), channel_id=1, source_target_pairs={{0,3},{1,0},{2,1},{3,2},{4,7},{5,4},{6,5},{7,6},{8,11},{9,8},{10,9... | collective-permute-start | bytes 663560 | tf_op jit(solution)/shard_map/ppermute | solution.py:23
  67.9 10.2 %collective-permute-start.22 = (bf16[144,768]{1,0:T(8,128)(2,1)S(1)}, bf16[144,768]{1,0:T(8,128)(2,1)S(1)}, u32[]{:S(2)}, u32[]{:S(2)}) collective-permute-start(bf16[144,768]{1,0:T(8,128)(2,1)S(1)} %get-tuple-element.62), channel_id=1, source_target_pairs={{0,1},{1,2},{2,3},{3,0},{4,5},{5,6},{6,7},{7,4},{8,9},{9,10},{10,1... | collective-permute-start | bytes 663560 | tf_op jit(solution)/shard_map/ppermute | solution.py:23
  67.9 10.2 %copy-start.5 = (f32[5120]{0:T(1024)S(1)}, f32[5120]{0:T(1024)}, u32[]{:S(2)}) copy-start(f32[5120]{0:T(1024)} %param.16) | copy-start | bytes 61444
  67.9 10.2 %collective-permute-start.23 = (bf16[144,768]{1,0:T(8,128)(2,1)S(1)}, bf16[144,768]{1,0:T(8,128)(2,1)S(1)}, u32[]{:S(2)}, u32[]{:S(2)}) collective-permute-start(bf16[144,768]{1,0:T(8,128)(2,1)S(1)} %get-tuple-element.63), channel_id=1, source_target_pairs={{0,2},{1,3},{2,0},{3,1},{4,6},{5,7},{6,4},{7,5},{8,10},{9,11},{10,... | collective-permute-start | bytes 663560 | tf_op jit(solution)/shard_map/ppermute | solution.py:23
  73.6 12.0 %collective-permute-start.14 = (bf16[144,512]{1,0:T(8,128)(2,1)S(1)}, bf16[144,512]{1,0:T(8,128)(2,1)S(1)}, u32[]{:S(2)}, u32[]{:S(2)}) collective-permute-start(bf16[144,512]{1,0:T(8,128)(2,1)S(1)} %get-tuple-element.53), channel_id=1, source_target_pairs={{0,3},{1,0},{2,1},{3,2},{4,7},{5,4},{6,5},{7,6},{8,11},{9,8},{10,9... | collective-permute-start | bytes 442376 | tf_op jit(solution)/shard_map/ppermute | solution.py:23
  76.8 8.8 %collective-permute-start.15 = (bf16[144,512]{1,0:T(8,128)(2,1)S(1)}, bf16[144,512]{1,0:T(8,128)(2,1)S(1)}, u32[]{:S(2)}, u32[]{:S(2)}) collective-permute-start(bf16[144,512]{1,0:T(8,128)(2,1)S(1)} %get-tuple-element.54), channel_id=1, source_target_pairs={{0,1},{1,2},{2,3},{3,0},{4,5},{5,6},{6,7},{7,4},{8,9},{9,10},{10,1... | collective-permute-start | bytes 442376 | tf_op jit(solution)/shard_map/ppermute | solution.py:23
  76.8 8.8 %collective-permute-start.16 = (bf16[144,512]{1,0:T(8,128)(2,1)S(1)}, bf16[144,512]{1,0:T(8,128)(2,1)S(1)}, u32[]{:S(2)}, u32[]{:S(2)}) collective-permute-start(bf16[144,512]{1,0:T(8,128)(2,1)S(1)} %get-tuple-element.55), channel_id=1, source_target_pairs={{0,2},{1,3},{2,0},{3,1},{4,6},{5,7},{6,4},{7,5},{8,10},{9,11},{10,... | collective-permute-start | bytes 442376 | tf_op jit(solution)/shard_map/ppermute | solution.py:23
  78.3 19.0 %copy-start.9 = (s32[32]{0:T(128)S(1)}, s32[32]{0:T(128)}, u32[]{:S(2)}) copy-start(s32[32]{0:T(128)} %overlaps_ref.3) | copy-start | bytes 388
  78.4 12.6 %collective-permute-start.25 = (bf16[64,3072]{1,0:T(8,128)(2,1)S(1)}, bf16[64,3072]{1,0:T(8,128)(2,1)S(1)}, u32[]{:S(2)}, u32[]{:S(2)}) collective-permute-start(bf16[64,3072]{1,0:T(8,128)(2,1)S(1)} %get-tuple-element.64.refs_0_), channel_id=1, source_target_pairs={{0,248},{8,0},{16,8},{24,16},{32,24},{40,32},{48,40},{56,48},{64,5... | collective-permute-start | bytes 1179656 | tf_op jit(solution)/shard_map/ppermute | solution.py:389
  85.3 12.0 %collective-permute-start.24 = (bf16[64,3072]{1,0:T(8,128)(2,1)S(1)}, bf16[64,3072]{1,0:T(8,128)(2,1)S(1)}, u32[]{:S(2)}, u32[]{:S(2)}) collective-permute-start(bf16[64,3072]{1,0:T(8,128)(2,1)S(1)} %get-tuple-element.66.refs_2_), channel_id=1, source_target_pairs={{0,8},{8,16},{16,24},{24,32},{32,40},{40,48},{48,56},{56,64},{64,7... | collective-permute-start | bytes 1179656 | tf_op jit(solution)/shard_map/ppermute | solution.py:389
  85.8 15.8 %collective-permute-start.18 = (bf16[64,2048]{1,0:T(8,128)(2,1)S(1)}, bf16[64,2048]{1,0:T(8,128)(2,1)S(1)}, u32[]{:S(2)}, u32[]{:S(2)}) collective-permute-start(bf16[64,2048]{1,0:T(8,128)(2,1)S(1)} %get-tuple-element.56.refs_0_), channel_id=1, source_target_pairs={{0,248},{8,0},{16,8},{24,16},{32,24},{40,32},{48,40},{56,48},{64,5... | collective-permute-start | bytes 786440 | tf_op jit(solution)/shard_map/ppermute | solution.py:389
  89.1 12.5 %collective-permute-start.17 = (bf16[64,2048]{1,0:T(8,128)(2,1)S(1)}, bf16[64,2048]{1,0:T(8,128)(2,1)S(1)}, u32[]{:S(2)}, u32[]{:S(2)}) collective-permute-start(bf16[64,2048]{1,0:T(8,128)(2,1)S(1)} %get-tuple-element.58.refs_2_), channel_id=1, source_target_pairs={{0,8},{8,16},{16,24},{24,32},{32,40},{40,48},{48,56},{56,64},{64,7... | collective-permute-start | bytes 786440 | tf_op jit(solution)/shard_map/ppermute | solution.py:389
